TPU v7x, 32 devices: a whole 2x2x4 slice. The times are simulated.
32 devices in a mesh: dp: 2 (over core), fsdp: 16 (over z, y, x).
Axes of the slice: x: 2, y: 2, z: 4, core: 2. Of those that a mesh axis runs over, the one named last changes fastest.
Arguments:
- tokens: bfloat16 [16384, 768], P(('dp', 'fsdp')), may hold values from -6 to 6
- lengths: int32 [32], P(('dp', 'fsdp')), may hold values from 128 to 512, as said below
- rel_index: int32 [1024], replicated, may hold values from 0 to 511, as said below
- w_query: bfloat16 [768, 768], P(('dp', 'fsdp')), may hold values from -0.21875 to 0.21875
- b_query: bfloat16 [768], P(('dp', 'fsdp')), may hold values from -3 to 3
- w_key: bfloat16 [768, 768], P(('dp', 'fsdp')), may hold values from -0.21875 to 0.21875
- b_key: bfloat16 [768], P(('dp', 'fsdp')), may hold values from -3 to 3
- w_value: bfloat16 [768, 768], P(('dp', 'fsdp')), may hold values from -0.21875 to 0.21875
- b_value: bfloat16 [768], P(('dp', 'fsdp')), may hold values from -3 to 3
- w_out: bfloat16 [768, 768], P(('dp', 'fsdp')), may hold values from -1.75 to 1.75
- b_out: bfloat16 [768], P(('dp', 'fsdp')), may hold values from -3 to 3
- rel_table: bfloat16 [512, 768], P(None, ('dp', 'fsdp')), may hold values from -6 to 6
- gain_one: bfloat16 [768], P(('dp', 'fsdp')), may hold values from 0.5 to 1.5
- shift_one: bfloat16 [768], P(('dp', 'fsdp')), may hold values from -2 to 2
- w_up: bfloat16 [768, 3072], P(('dp', 'fsdp')), may hold values from -0.21875 to 0.21875
- b_up: bfloat16 [3072], P(('dp', 'fsdp')), may hold values from -3 to 3
- w_down: bfloat16 [3072, 768], P(('dp', 'fsdp')), may hold values from -0.109375 to 0.109375
- b_down: bfloat16 [768], P(('dp', 'fsdp')), may hold values from -3 to 3
- gain_two: bfloat16 [768], P(('dp', 'fsdp')), may hold values from 0.5 to 1.5
- shift_two: bfloat16 [768], P(('dp', 'fsdp')), may hold values from -2 to 2
- cotangent: bfloat16 [16384, 768], P(('dp', 'fsdp')), may hold values from -6 to 6
Outputs:
- output: bfloat16 [16384, 768], P(('dp', 'fsdp'))
- grad_tokens: float32 [16384, 768], P(('dp', 'fsdp'))
- grad_w_query: float32 [768, 768], P(('dp', 'fsdp'))
- grad_b_query: float32 [768], P(('dp', 'fsdp'))
- grad_w_key: float32 [768, 768], P(('dp', 'fsdp'))
- grad_b_key: float32 [768], P(('dp', 'fsdp'))
- grad_w_value: float32 [768, 768], P(('dp', 'fsdp'))
- grad_b_value: float32 [768], P(('dp', 'fsdp'))
- grad_w_out: float32 [768, 768], P(('dp', 'fsdp'))
- grad_b_out: float32 [768], P(('dp', 'fsdp'))
- grad_rel_table: float32 [512, 768], P(None, ('dp', 'fsdp'))
- grad_gain_one: float32 [768], P(('dp', 'fsdp'))
- grad_shift_one: float32 [768], P(('dp', 'fsdp'))
- grad_w_up: float32 [768, 3072], P(('dp', 'fsdp'))
- grad_b_up: float32 [3072], P(('dp', 'fsdp'))
- grad_w_down: float32 [3072, 768], P(('dp', 'fsdp'))
- grad_b_down: float32 [768], P(('dp', 'fsdp'))
- grad_gain_two: float32 [768], P(('dp', 'fsdp'))
- grad_shift_two: float32 [768], P(('dp', 'fsdp'))
Inputs may be any that keep to these rules, and one draw needn't show every extreme that they name: `lengths`: some sequence is full in every draw. `rel_index`: entry t is the bucket of the offset t - 512; entry 0 is never read.
All inputs are finite; a program needn't handle non-finite values.
Results may differ from a plain program's by a relative error of at most 0.034.
Values may be sent and summed in bfloat16 or wider, within the bound.
A program may use at most 128 MiB of HBM per device.

v0:
```python
from functools import partial

import jax
import jax.numpy as jnp
from jax import lax
from jax.sharding import PartitionSpec as P

HEADS = 12


EPS = 1e-06


def widen(values):
    return values.astype(jnp.float32)


def multiply(left, right):
    return jnp.dot(left, right, preferred_element_type=jnp.float32)


def contract_rows(left, right):
    return lax.dot_general(
        left, right, (((0,), (0,)), ((), ())), preferred_element_type=jnp.float32
    )


def contract_cols(left, right):
    return lax.dot_general(
        left, right, (((1,), (1,)), ((), ())), preferred_element_type=jnp.float32
    )


def layer_norm(values, gain, shift):
    mean = jnp.mean(values, axis=-1, keepdims=True)
    centred = values - mean
    spread = jnp.mean(centred * centred, axis=-1, keepdims=True)
    return centred * lax.rsqrt(spread + EPS) * gain + shift


def skew(table, offset):
    count = table.shape[0]
    width = table.shape[1]
    flat = table.reshape(-1)
    piece = lax.slice_in_dim(flat, offset, offset + count * (width - 1))
    return piece.reshape(count, width - 1)[:, :count]


def skew_back(grad, offset, width):
    count = grad.shape[0]
    padded = jnp.pad(grad, ((0, 0), (0, width - 1 - count)))
    flat = jnp.pad(padded.reshape(-1), (offset, count * width - offset - count * (width - 1)))
    return flat.reshape(count, width)


def split_heads(values):
    return values.reshape(values.shape[0], HEADS, values.shape[1] // HEADS).transpose(1, 0, 2)


def merge_heads(values):
    return values.transpose(1, 0, 2).reshape(values.shape[1], values.shape[0] * values.shape[2])


def head_scores(query, key, key_pos, query_pos, live):
    count = query.shape[0]
    scale = (3.0 * query.shape[1]) ** (-0.5)
    content = contract_cols(query, key)
    to_place = skew(contract_cols(query, key_pos), count - 1)
    from_place = skew(contract_cols(key, query_pos), count).T
    scaled = scale * (content + to_place + from_place)
    return jnp.where(live[None, :], scaled, -1e30)


def head_forward(parts, live):
    query, key, value, key_pos, query_pos = parts
    scores = head_scores(query, key, key_pos, query_pos, live)
    summit = jnp.max(scores, axis=1, keepdims=True)
    weights = jnp.exp(scores - summit)
    total = jnp.sum(weights, axis=1, keepdims=True)
    probs = weights / total
    context = multiply(probs.astype(jnp.bfloat16), value)
    return (context, (summit + jnp.log(total))[:, 0])


def head_backward(parts, live):
    query, key, value, key_pos, query_pos, summit, grad_context = parts
    count = query.shape[0]
    scale = (3.0 * query.shape[1]) ** (-0.5)
    scores = head_scores(query, key, key_pos, query_pos, live)
    probs = jnp.exp(scores - summit[:, None])
    grad_probs = contract_cols(grad_context, value)
    inner = jnp.sum(probs * grad_probs, axis=1, keepdims=True)
    grad_scores = (probs * (grad_probs - inner)).astype(jnp.bfloat16)
    grad_to = skew_back(grad_scores, count - 1, 2 * count)
    grad_from = skew_back(grad_scores.T, count, 2 * count)
    grad_query = scale * (multiply(grad_scores, key) + multiply(grad_to, key_pos))
    grad_key = scale * (contract_rows(grad_scores, query) + multiply(grad_from, query_pos))
    grad_value = contract_rows(probs.astype(jnp.bfloat16), grad_context)
    grad_key_pos = scale * contract_rows(grad_to, query)
    grad_query_pos = scale * contract_rows(grad_from, key)
    return (grad_query, grad_key, grad_value, grad_key_pos, grad_query_pos)


def sequence_forward(inputs, length, pick, pick_reverse, attend, dense):
    (
        w_query,
        w_key,
        w_value,
        w_out,
        b_query,
        b_key,
        b_value,
        b_out,
        gain_one,
        shift_one,
        rel_table,
    ) = attend
    w_up, w_down, b_up, b_down, gain_two, shift_two = dense
    count = inputs.shape[0]
    live = jnp.arange(count, dtype=jnp.int32) < length
    query = (multiply(inputs, w_query) + widen(b_query)).astype(jnp.bfloat16)
    key = (multiply(inputs, w_key) + widen(b_key)).astype(jnp.bfloat16)
    value = (multiply(inputs, w_value) + widen(b_value)).astype(jnp.bfloat16)
    rel_key = (multiply(rel_table, w_key) + widen(b_key)).astype(jnp.bfloat16)
    rel_query = (multiply(rel_table, w_query) + widen(b_query)).astype(jnp.bfloat16)
    key_pos = multiply(pick_reverse, rel_key).astype(jnp.bfloat16)
    query_pos = multiply(pick, rel_query).astype(jnp.bfloat16)
    heads, summit = lax.map(
        partial(head_forward, live=live),
        (
            split_heads(query),
            split_heads(key),
            split_heads(value),
            split_heads(key_pos),
            split_heads(query_pos),
        ),
    )
    context = merge_heads(heads).astype(jnp.bfloat16)
    mixed = widen(inputs) + (multiply(context, w_out) + widen(b_out))
    normed = layer_norm(mixed, widen(gain_one), widen(shift_one))
    up = multiply(normed.astype(jnp.bfloat16), w_up) + widen(b_up)
    act = jax.nn.gelu(up, approximate=False).astype(jnp.bfloat16)
    second = normed + (multiply(act, w_down) + widen(b_down))
    result = layer_norm(second, widen(gain_two), widen(shift_two)) * live[:, None]
    saved = (query, key, value, key_pos, query_pos, summit, context, mixed, up, second)
    return (result.astype(jnp.bfloat16), saved)


def sequence_backward(inputs, length, cotan_low, pick, pick_reverse, saved, attend, dense):
    (
        w_query,
        w_key,
        w_value,
        w_out,
        b_query,
        b_key,
        b_value,
        b_out,
        gain_one,
        shift_one,
        rel_table,
    ) = attend
    w_up, w_down, b_up, b_down, gain_two, shift_two = dense
    query, key, value, key_pos, query_pos, summit, context, mixed, up, second = saved
    count = inputs.shape[0]
    live = jnp.arange(count, dtype=jnp.int32) < length
    start_grad = widen(cotan_low) * live[:, None]
    normed, norm_pull = jax.vjp(layer_norm, mixed, widen(gain_one), widen(shift_one))
    unused, final_pull = jax.vjp(layer_norm, second, widen(gain_two), widen(shift_two))
    grad_second, grad_gain_two, grad_shift_two = final_pull(start_grad)
    grad_down = grad_second.astype(jnp.bfloat16)
    act, act_pull = jax.vjp(partial(jax.nn.gelu, approximate=False), up)
    grad_w_down = contract_rows(act.astype(jnp.bfloat16), grad_down)
    grad_b_down = jnp.sum(widen(grad_down), axis=0)
    grad_up = act_pull(contract_cols(grad_down, w_down))[0].astype(jnp.bfloat16)
    grad_w_up = contract_rows(normed.astype(jnp.bfloat16), grad_up)
    grad_b_up = jnp.sum(widen(grad_up), axis=0)
    grad_normed = grad_second + contract_cols(grad_up, w_up)
    grad_mixed, grad_gain_one, grad_shift_one = norm_pull(grad_normed)
    grad_attend = grad_mixed.astype(jnp.bfloat16)
    grad_w_out = contract_rows(context, grad_attend)
    grad_b_out = jnp.sum(widen(grad_attend), axis=0)
    grad_context = contract_cols(grad_attend, w_out).astype(jnp.bfloat16)
    heads = lax.map(
        partial(head_backward, live=live),
        (
            split_heads(query),
            split_heads(key),
            split_heads(value),
            split_heads(key_pos),
            split_heads(query_pos),
            summit,
            split_heads(grad_context),
        ),
    )
    grad_query = merge_heads(heads[0]).astype(jnp.bfloat16)
    grad_key = merge_heads(heads[1]).astype(jnp.bfloat16)
    grad_value = merge_heads(heads[2]).astype(jnp.bfloat16)
    grad_key_pos = merge_heads(heads[3]).astype(jnp.bfloat16)
    grad_query_pos = merge_heads(heads[4]).astype(jnp.bfloat16)
    grad_rel_key = contract_rows(pick_reverse, grad_key_pos).astype(jnp.bfloat16)
    grad_rel_query = contract_rows(pick, grad_query_pos).astype(jnp.bfloat16)
    grad_w_query = contract_rows(inputs, grad_query) + contract_rows(rel_table, grad_rel_query)
    grad_b_query = jnp.sum(widen(grad_query), axis=0) + jnp.sum(widen(grad_rel_query), axis=0)
    grad_w_key = contract_rows(inputs, grad_key) + contract_rows(rel_table, grad_rel_key)
    grad_b_key = jnp.sum(widen(grad_key), axis=0) + jnp.sum(widen(grad_rel_key), axis=0)
    grad_w_value = contract_rows(inputs, grad_value)
    grad_b_value = jnp.sum(widen(grad_value), axis=0)
    grad_rel_table = contract_cols(grad_rel_key, w_key) + contract_cols(grad_rel_query, w_query)
    grad_inputs = (
        grad_mixed
        + contract_cols(grad_query, w_query)
        + contract_cols(grad_key, w_key)
        + contract_cols(grad_value, w_value)
    )
    grads = (
        grad_w_query,
        grad_w_key,
        grad_w_value,
        grad_w_out,
        grad_b_query,
        grad_b_key,
        grad_b_value,
        grad_b_out,
        grad_gain_one,
        grad_shift_one,
        grad_rel_table,
        grad_w_up,
        grad_w_down,
        grad_b_up,
        grad_b_down,
        grad_gain_two,
        grad_shift_two,
    )
    return (grad_inputs, grads)


def collect_attend(
    w_query, w_key, w_value, w_out, b_query, b_key, b_value, b_out, gain_one, shift_one, rel_table
):
    return (
        lax.all_gather(w_query, ("dp", "fsdp"), axis=0, tiled=True),
        lax.all_gather(w_key, ("dp", "fsdp"), axis=0, tiled=True),
        lax.all_gather(w_value, ("dp", "fsdp"), axis=0, tiled=True),
        lax.all_gather(w_out, ("dp", "fsdp"), axis=0, tiled=True),
        lax.all_gather(b_query, ("dp", "fsdp"), axis=0, tiled=True),
        lax.all_gather(b_key, ("dp", "fsdp"), axis=0, tiled=True),
        lax.all_gather(b_value, ("dp", "fsdp"), axis=0, tiled=True),
        lax.all_gather(b_out, ("dp", "fsdp"), axis=0, tiled=True),
        lax.all_gather(gain_one, ("dp", "fsdp"), axis=0, tiled=True),
        lax.all_gather(shift_one, ("dp", "fsdp"), axis=0, tiled=True),
        lax.all_gather(rel_table, ("dp", "fsdp"), axis=1, tiled=True),
    )


def collect_dense(w_up, w_down, b_up, b_down, gain_two, shift_two):
    return (
        lax.all_gather(w_up, ("dp", "fsdp"), axis=0, tiled=True),
        lax.all_gather(w_down, ("dp", "fsdp"), axis=0, tiled=True),
        lax.all_gather(b_up, ("dp", "fsdp"), axis=0, tiled=True),
        lax.all_gather(b_down, ("dp", "fsdp"), axis=0, tiled=True),
        lax.all_gather(gain_two, ("dp", "fsdp"), axis=0, tiled=True),
        lax.all_gather(shift_two, ("dp", "fsdp"), axis=0, tiled=True),
    )


def spread_attend(grads):
    (
        grad_wq,
        grad_wk,
        grad_wv,
        grad_wo,
        grad_bq,
        grad_bk,
        grad_bv,
        grad_bo,
        grad_gain,
        grad_shift,
        grad_table,
    ) = grads
    return (
        lax.psum_scatter(grad_wq, ("dp", "fsdp"), scatter_dimension=0, tiled=True),
        lax.psum_scatter(grad_wk, ("dp", "fsdp"), scatter_dimension=0, tiled=True),
        lax.psum_scatter(grad_wv, ("dp", "fsdp"), scatter_dimension=0, tiled=True),
        lax.psum_scatter(grad_wo, ("dp", "fsdp"), scatter_dimension=0, tiled=True),
        lax.psum_scatter(grad_bq, ("dp", "fsdp"), scatter_dimension=0, tiled=True),
        lax.psum_scatter(grad_bk, ("dp", "fsdp"), scatter_dimension=0, tiled=True),
        lax.psum_scatter(grad_bv, ("dp", "fsdp"), scatter_dimension=0, tiled=True),
        lax.psum_scatter(grad_bo, ("dp", "fsdp"), scatter_dimension=0, tiled=True),
        lax.psum_scatter(grad_gain, ("dp", "fsdp"), scatter_dimension=0, tiled=True),
        lax.psum_scatter(grad_shift, ("dp", "fsdp"), scatter_dimension=0, tiled=True),
        lax.psum_scatter(grad_table, ("dp", "fsdp"), scatter_dimension=1, tiled=True),
    )


def spread_dense(grads):
    grad_up, grad_down, grad_bup, grad_bdown, grad_gain, grad_shift = grads
    return (
        lax.psum_scatter(grad_up, ("dp", "fsdp"), scatter_dimension=0, tiled=True),
        lax.psum_scatter(grad_down, ("dp", "fsdp"), scatter_dimension=0, tiled=True),
        lax.psum_scatter(grad_bup, ("dp", "fsdp"), scatter_dimension=0, tiled=True),
        lax.psum_scatter(grad_bdown, ("dp", "fsdp"), scatter_dimension=0, tiled=True),
        lax.psum_scatter(grad_gain, ("dp", "fsdp"), scatter_dimension=0, tiled=True),
        lax.psum_scatter(grad_shift, ("dp", "fsdp"), scatter_dimension=0, tiled=True),
    )


def body(
    tokens,
    lengths,
    rel_index,
    w_query,
    b_query,
    w_key,
    b_key,
    w_value,
    b_value,
    w_out,
    b_out,
    rel_table,
    gain_one,
    shift_one,
    w_up,
    b_up,
    w_down,
    b_down,
    gain_two,
    shift_two,
    cotangent,
):
    attend = collect_attend(
        w_query,
        w_key,
        w_value,
        w_out,
        b_query,
        b_key,
        b_value,
        b_out,
        gain_one,
        shift_one,
        rel_table,
    )
    dense = collect_dense(w_up, w_down, b_up, b_down, gain_two, shift_two)
    number = lengths.shape[0]
    width = tokens.shape[1]
    count = tokens.shape[0] // number
    buckets = jnp.arange(attend[10].shape[0], dtype=jnp.int32)
    pick = (rel_index[:, None] == buckets[None, :]).astype(jnp.bfloat16)
    pick_reverse = pick[::-1]
    batches = tokens.reshape(number, count, width)
    cotan_rows = cotangent.reshape(number, count, width)

    def forward_one(item):
        return sequence_forward(item[0], item[1], pick, pick_reverse, attend, dense)

    results, saved_all = lax.map(forward_one, (batches, lengths))
    back_attend = collect_attend(
        w_query,
        w_key,
        w_value,
        w_out,
        b_query,
        b_key,
        b_value,
        b_out,
        gain_one,
        shift_one,
        rel_table,
    )
    back_dense = collect_dense(w_up, w_down, b_up, b_down, gain_two, shift_two)
    zeros = tuple((jnp.zeros(w.shape, jnp.float32) for w in back_attend + back_dense))

    def backward_step(total, item):
        inputs, length, cotan_low, saved = item
        grad_inputs, grads = sequence_backward(
            inputs, length, cotan_low, pick, pick_reverse, saved, back_attend, back_dense
        )
        return (tuple((a + b for a, b in zip(total, grads))), grad_inputs)

    totals, grad_inputs = lax.scan(backward_step, zeros, (batches, lengths, cotan_rows, saved_all))
    owned_attend = spread_attend(totals[:11])
    owned_dense = spread_dense(totals[11:])
    (
        grad_wq,
        grad_wk,
        grad_wv,
        grad_wo,
        grad_bq,
        grad_bk,
        grad_bv,
        grad_bo,
        grad_gain_one,
        grad_shift_one,
        grad_table,
    ) = owned_attend
    grad_up, grad_down, grad_bup, grad_bdown, grad_gain_two, grad_shift_two = owned_dense
    return (
        results.reshape(number * count, width),
        grad_inputs.reshape(number * count, width),
        grad_wq,
        grad_bq,
        grad_wk,
        grad_bk,
        grad_wv,
        grad_bv,
        grad_wo,
        grad_bo,
        grad_table,
        grad_gain_one,
        grad_shift_one,
        grad_up,
        grad_bup,
        grad_down,
        grad_bdown,
        grad_gain_two,
        grad_shift_two,
    )


def solution(mesh):
    return jax.shard_map(
        body,
        mesh=mesh,
        in_specs=(
            P(("dp", "fsdp"), None),
            P(("dp", "fsdp")),
            P(),
            P(("dp", "fsdp"), None),
            P(("dp", "fsdp")),
            P(("dp", "fsdp"), None),
            P(("dp", "fsdp")),
            P(("dp", "fsdp"), None),
            P(("dp", "fsdp")),
            P(("dp", "fsdp"), None),
            P(("dp", "fsdp")),
            P(None, ("dp", "fsdp")),
            P(("dp", "fsdp")),
            P(("dp", "fsdp")),
            P(("dp", "fsdp"), None),
            P(("dp", "fsdp")),
            P(("dp", "fsdp"), None),
            P(("dp", "fsdp")),
            P(("dp", "fsdp")),
            P(("dp", "fsdp")),
            P(("dp", "fsdp"), None),
        ),
        out_specs=(
            P(("dp", "fsdp"), None),
            P(("dp", "fsdp"), None),
            P(("dp", "fsdp"), None),
            P(("dp", "fsdp")),
            P(("dp", "fsdp"), None),
            P(("dp", "fsdp")),
            P(("dp", "fsdp"), None),
            P(("dp", "fsdp")),
            P(("dp", "fsdp"), None),
            P(("dp", "fsdp")),
            P(None, ("dp", "fsdp")),
            P(("dp", "fsdp")),
            P(("dp", "fsdp")),
            P(("dp", "fsdp"), None),
            P(("dp", "fsdp")),
            P(("dp", "fsdp"), None),
            P(("dp", "fsdp")),
            P(("dp", "fsdp")),
            P(("dp", "fsdp")),
        ),
        check_vma=False,
    )
```

profile of v0, /device:TPU:0, one launch (start us, length us, event | category | flops | bytes accessed | tf_op | source)
XLA Modules:
  0.0 1810.6 jit_solution(12654121570839998514)
XLA Ops:
  19.6 42.5 %all-reduce.25 = (bf16[768]{0:T(1024)(128)(2,1)S(1)}, bf16[768]{0:T(1024)(128)(2,1)S(1)}, bf16[768]{0:T(1024)(128)(2,1)S(1)}, bf16[768]{0:T(1024)(128)(2,1)S(1)}...) all-reduce(bf16[768]{0:T(1024)(128)(2,1)S(1)} %dynamic-update-slice, ...), channel_id=1, replica_groups=mesh['dp'=2,'fsdp'=16] {'dp','fsdp'}, use_global_device_ids=true, to_apply=%add.4 | all-reduce | flops 9984 | bytes 39936
  62.1 71.0 %all_gather.65 = bf16[512,768]{0,1:T(8,128)(2,1)S(1)} all-gather(bf16[512,24]{0,1:T(8,128)(2,1)} %param.36), channel_id=1, replica_groups=mesh['dp'=2,'fsdp'=16] {'dp','fsdp'}, dimensions={1}, use_global_device_ids=true | all-gather | bytes 811008 | tf_op jit(solution)/shard_map/all_gather | solution.py:252
  158.5 22.7 %all-gather.11.cloned.1.call-done = bf16[768,768]{1,0:T(8,128)(2,1)} async-done(((bf16[24,768]{1,0:T(8,128)(2,1)}), bf16[768,768]{1,0:T(8,128)(2,1)}) %all-gather.11.cloned.1.call-update) | async-done | bytes 1179664 | tf_op jit(solution)/shard_map/all_gather | solution.py:244
  186.1 210.1 %while.45 = (s32[]{:T(128)}, bf16[12,512,64]{1,2,0:T(8,128)(2,1)}, f32[12,512]{1,0:T(8,128)}, bf16[12,512,64]{2,1,0:T(8,128)(2,1)}, bf16[12,512,64]{2,1,0:T(8,12...) while((s32[]{:T(128)}, bf16[12,512,64]{1,2,0:T(8,128)(2,1)}, ...), condition=%wide.region_3.4_spmd.clone, body=%wide.region_0.3_spmd.clone.sunk | while | flops 203948032 | bytes 41165964 | solution.py:128
  399.6 20.0 %multiply_convert_fusion.1 = (bf16[512,3072]{1,0:T(8,128)(2,1)}, f32[512,3072]{1,0:T(8,128)}, f32[512,3072]{1,0:T(8,128)}) fusion(f32[3072]{0:T(1024)S(1)} %copy-done.31, bf16[768,3072]{1,0:T(8,128)(2,1)} %all-gather.15.cloned.1.call-done, f32[512,768]{1,0:T(8,128)S(1)} %get-tuple-element.727, f32[768]{0:T(1024)S(1)} %copy-done.34, ...), kind=kOutput, calls=%fused_computation.114 | convolution fusion | flops 2521694208 | bytes 22042624 | tf_op jit(solution)/shard_map/while/body/eval_jaxpr/dot_general | solution.py:19
  419.6 6.0 fusion.118
  430.7 8.3 convert_reduce_fusion
  450.0 548.7 %while.46 = (s32[]{:T(128)}, bf16[12,512,64]{1,2,0:T(8,128)(2,1)}, bf16[12,512,64]{1,2,0:T(8,128)(2,1)}, bf16[12,512,64]{1,2,0:T(8,128)(2,1)}, bf16[12,1024,64]{...) while((s32[]{:T(128)}, bf16[12,512,64]{1,2,0:T(8,128)(2,1)}, ...), condition=%wide.region_14.15_spmd.clone, body=%wide.region_12.14_spmd.clone.sunk | while | flops 573571072 | bytes 73528536 | solution.py:184
  523.5 3.8 reshape.369
  569.2 3.8 reshape.369
  614.9 3.8 reshape.369
  660.6 3.8 reshape.369
  797.7 3.8 reshape.369
  889.1 3.8 reshape.369
  1027.9 7.2 fusion.109
  1036.3 8.1 fusion.125
  1046.5 40.5 %all-reduce.24 = (f32[768]{0:T(1024)S(1)}, f32[768]{0:T(1024)S(1)}, f32[768]{0:T(1024)S(1)}, f32[768]{0:T(1024)S(1)}, f32[768]{0:T(1024)S(1)}, /*index=5*/f32[76...) all-reduce(f32[768]{0:T(1024)S(1)} %add.360, ...), channel_id=3, replica_groups=mesh['dp'=2,'fsdp'=16] {'dp','fsdp'}, use_global_device_ids=true, to_apply=%region_18.19.clone | all-reduce | flops 9984 | bytes 79872
  1098.5 4.5 reduce-scatter.16.cloned.1.call-done
  1102.9 104.0 %reduce-scatter.24.cloned.1.call-done = f32[24,768]{1,0:T(8,128)} async-done(((f32[768,768]{1,0:T(8,128)}), f32[24,768]{1,0:T(8,128)}) %reduce-scatter.24.cloned.1.call-update) | async-done | bytes 73744
  1207.0 104.8 %reduce-scatter.14.cloned.1.call-done = f32[24,768]{1,0:T(8,128)} async-done(((f32[768,768]{1,0:T(8,128)}), f32[24,768]{1,0:T(8,128)}) %reduce-scatter.14.cloned.1.call-update) | async-done | bytes 73744 | tf_op jit(solution)/shard_map/reduce_scatter | solution.py:285
  1311.7 103.8 %reduce-scatter.22.cloned.1.call-done = f32[24,768]{1,0:T(8,128)} async-done(((f32[768,768]{1,0:T(8,128)}), f32[24,768]{1,0:T(8,128)}) %reduce-scatter.22.cloned.1.call-update) | async-done | bytes 73744
  1415.5 104.8 %reduce-scatter.26.cloned.1.call-done = f32[24,768]{1,0:T(8,128)} async-done(((f32[768,768]{1,0:T(8,128)}), f32[24,768]{1,0:T(8,128)}) %reduce-scatter.26.cloned.1.call-update) | async-done | bytes 73744
  1520.4 141.1 %reduce-scatter.18.cloned.1.call-done = f32[24,3072]{1,0:T(8,128)} async-done(((f32[768,3072]{1,0:T(8,128)}), f32[24,3072]{1,0:T(8,128)}) %reduce-scatter.18.cloned.1.call-update) | async-done | bytes 294928 | tf_op jit(solution)/shard_map/reduce_scatter | solution.py:299
  1661.5 142.2 %reduce-scatter.20.cloned.1.call-done = f32[96,768]{1,0:T(8,128)} async-done(((f32[3072,768]{1,0:T(8,128)}), f32[96,768]{1,0:T(8,128)}) %reduce-scatter.20.cloned.1.call-update) | async-done | bytes 294928 | tf_op jit(solution)/shard_map/reduce_scatter | solution.py:300
  (839 shorter events, 838.2 us)
Async XLA Ops:
  7.2 131.9 %all-gather.9.cloned.1.call-start = ((), (), s32[]{:S(2)}) async-start(), calls=%async_computation.8 | async-start | bytes 1216512 | tf_op jit(solution)/shard_map/all_gather | solution.py:243
  7.9 137.2 %all-gather.7.cloned.1.call-start = ((), (), s32[]{:S(2)}) async-start(), calls=%async_computation.7 | async-start | bytes 1216512 | tf_op jit(solution)/shard_map/all_gather | solution.py:242
  8.7 172.5 %all-gather.11.cloned.1.call-start = ((), (), s32[]{:S(2)}) async-start(), calls=%async_computation.9 | async-start | bytes 1216512 | tf_op jit(solution)/shard_map/all_gather | solution.py:244
  9.4 386.7 %all-gather.13.cloned.1.call-start = ((), (), s32[]{:S(2)}) async-start(), calls=%async_computation.10 | async-start | bytes 1216512 | tf_op jit(solution)/shard_map/all_gather | solution.py:245
  10.0 389.2 %all-gather.15.cloned.1.call-start = ((), (), s32[]{:S(2)}) async-start(), calls=%async_computation.11 | async-start | bytes 4866048 | tf_op jit(solution)/shard_map/all_gather | solution.py:258
  10.6 409.0 %all-gather.17.cloned.1.call-start = ((), (), s32[]{:S(2)}) async-start(), calls=%async_computation.12 | async-start | bytes 4866048 | tf_op jit(solution)/shard_map/all_gather | solution.py:259
  11.1 1091.8 %reduce-scatter.16.cloned.1.call-start = ((), (), s32[]{:S(2)}) async-start(), calls=%async_computation.14 | async-start | bytes 1622016 | tf_op jit(solution)/shard_map/reduce_scatter | solution.py:292
  62.1 77.0 %copy-start.38 = (f32[768]{0:T(1024)}, f32[768]{0:T(1024)S(1)}, u32[]{:S(2)}) copy-start(f32[768]{0:T(1024)S(1)} %convert_element_type.269) | copy-start | bytes 9220
  133.1 12.0 copy-start.4
  135.3 9.8 copy-start.40
  156.9 24.3 %copy-start.37 = (f32[768]{0:T(1024)S(1)}, f32[768]{0:T(1024)}, u32[]{:S(2)}) copy-start(f32[768]{0:T(1024)} %convert_element_type.276) | copy-start | bytes 9220
  186.1 210.1 %copy-start.36 = (f32[768]{0:T(1024)S(1)}, f32[768]{0:T(1024)}, u32[]{:S(2)}) copy-start(f32[768]{0:T(1024)} %convert_element_type.281) | copy-start | bytes 9220
  398.8 43.4 %copy-start.11 = (f32[512,768]{1,0:T(8,128)}, f32[512,768]{1,0:T(8,128)S(1)}, u32[]{:S(2)}) copy-start(f32[512,768]{1,0:T(8,128)S(1)} %get-tuple-element.727) | copy-start | bytes 4718596
  399.2 20.4 %copy-start.35 = (f32[768]{0:T(1024)S(1)}, f32[768]{0:T(1024)}, u32[]{:S(2)}) copy-start(f32[768]{0:T(1024)} %convert_element_type.287) | copy-start | bytes 9220
  429.8 9.2 slice-start.2
  430.6 8.4 copy-start.26
  430.7 8.3 slice-start.3
  1006.5 200.5 %reduce-scatter.24.cloned.1.call-start = ((), (), s32[]{:S(2)}) async-start(), calls=%async_computation.18 | async-start | bytes 2433024
  1012.5 299.2 %reduce-scatter.14.cloned.1.call-start = ((), (), s32[]{:S(2)}) async-start(), calls=%async_computation.13 | async-start | bytes 2433024 | tf_op jit(solution)/shard_map/reduce_scatter | solution.py:285
  1016.1 399.4 %reduce-scatter.22.cloned.1.call-start = ((), (), s32[]{:S(2)}) async-start(), calls=%async_computation.17 | async-start | bytes 2433024
  1021.5 498.9 %reduce-scatter.26.cloned.1.call-start = ((), (), s32[]{:S(2)}) async-start(), calls=%async_computation.19 | async-start | bytes 2433024
  1026.5 634.9 %reduce-scatter.18.cloned.1.call-start = ((), (), s32[]{:S(2)}) async-start(), calls=%async_computation.15 | async-start | bytes 9732096 | tf_op jit(solution)/shard_map/reduce_scatter | solution.py:299
  1035.2 768.5 %reduce-scatter.20.cloned.1.call-start = ((), (), s32[]{:S(2)}) async-start(), calls=%async_computation.16 | async-start | bytes 9732096 | tf_op jit(solution)/shard_map/reduce_scatter | solution.py:300
  1044.5 48.4 %copy-start.22 = (bf16[768,768]{1,0:T(8,128)(2,1)S(1)}, bf16[768,768]{1,0:T(8,128)(2,1)}, u32[]{:S(2)}) copy-start(bf16[768,768]{1,0:T(8,128)(2,1)} %all-gather.7.cloned.1.call-done) | copy-start | bytes 3538948
  (73 other events, 149.0 us)
Sparse Core Ops, SparseCore 0:
  10.9 56.9 all-gather.8
  70.8 54.0 all-gather.6
  127.8 53.3 all-gather.10
  183.9 53.0 all-gather.12
  239.8 62.5 all-gather.14
  305.1 62.3 all-gather.16
  1006.6 96.2 reduce-scatter.15
  1108.8 98.1 reduce-scatter.23
  1213.7 98.0 reduce-scatter.13
  1317.4 98.0 reduce-scatter.21
  1422.3 98.0 reduce-scatter.25
  1526.7 134.7 reduce-scatter.17
  1669.0 134.6 reduce-scatter.19
where the time goes:
time: 1830 us; the launch traced here: 1810 us
  waiting for transfers between devices  732 us (40%)
  local copies, waits for them, and re-layouts  487 us (27%)
  matrix products  387 us (21%)
  blocking collectives  154 us (8%)
  other arithmetic  32.1 us (2%)
    unnamed x16, waiting for transfers between devices  316 us
    dot_general x92, matrix products, contract_cols(): lax.dot_general(left, right, (((1,), (1,)), ((), ())), preferred_element_...  148 us
    reduce_scatter x1, waiting for transfers between devices, spread_dense(): lax.psum_scatter(grad_down, ('dp', 'fsdp'), scatter_dimension=0, tiled=True)  142 us
    reduce_scatter x1, waiting for transfers between devices, spread_dense(): lax.psum_scatter(grad_up, ('dp', 'fsdp'), scatter_dimension=0, tiled=True)  141 us
    reshape x48, local copies, waits for them, and re-layouts, skew(): return piece.reshape(count, width - 1)[:, :count]  132 us
    dot_general x58, matrix products, contract_rows(): lax.dot_general(left, right, (((0,), (0,)), ((), ())), preferred_element_...  121 us
    dot_general x56, matrix products, multiply(): return jnp.dot(left, right, preferred_element_type=jnp.float32)  118 us
    reduce_scatter x1, waiting for transfers between devices, spread_attend(): lax.psum_scatter(grad_wo, ('dp', 'fsdp'), scatter_dimension=0, tiled=True)  105 us
  transfers between devices with their start and end apart: 13, of which 8 were waited for; matrix products, arithmetic and copies ran while one was open for 16% of the time, Pallas kernels for 0%

commit v1 on v0

v1 whole, which is shorter than its diff:
```python
import jax, jax.numpy as jnp
from jax import lax
from jax.sharding import PartitionSpec as P
from jax.experimental import pallas as pl
from jax.experimental.pallas import tpu as pltpu

BF = jnp.bfloat16
F32 = jnp.float32
EPS = 1e-6


def dot(left, right, dims):
    return lax.dot_general(left, right, ((dims[:1], dims[1:]), ((), ())), preferred_element_type=F32)


def nn(left, right):
    return dot(left, right, (1, 0))


def nt(left, right):
    return dot(left, right, (1, 1))


def tn(left, right):
    return dot(left, right, (0, 0))


def iota(shape, axis):
    return lax.broadcasted_iota(jnp.int32, shape, axis)


def flip_matrix(size):
    return jnp.where(iota((size, size), 0) + iota((size, size), 1) == size - 1, 1.0, 0.0).astype(BF)


def attend_head(q_ref, k_ref, v_ref, kT_ref, kprT_ref, qpsT_ref, mask_ref, flip_ref, c0, hh, scale):
    T = q_ref.shape[0]
    B = T // 2
    lanes = pl.ds(c0, 128)
    rows = pl.ds(c0, 128)
    keep = (iota((1, 128), 1) // 64 == hh)
    qh = jnp.where(keep, q_ref[:, lanes], 0)
    kh = jnp.where(keep, k_ref[:, lanes], 0)
    content = nn(qh, kT_ref[rows, :])
    to, frm = [], []
    for b in range(2):
        u0 = B * (1 - b)
        t = nn(qh[b * B:(b + 1) * B], kprT_ref[rows, u0:u0 + 3 * B])
        to.append(pltpu.roll(t, 2 * B + 1, 1, stride=1, stride_axis=0)[:, :T])
        f = nn(kh[b * B:(b + 1) * B], qpsT_ref[rows, u0:u0 + 3 * B])
        frm.append(pltpu.roll(f, 2 * B + 1, 1, stride=1, stride_axis=0)[:, :T].T)
    s = content + jnp.concatenate(to, axis=0) + jnp.concatenate(frm, axis=1) + mask_ref[0:1, :]
    m = jnp.max(s, axis=1, keepdims=True)
    e = jnp.exp2((s - m) * (scale * 1.4426950408889634))
    total = jnp.sum(e, axis=1, keepdims=True)
    return (e * (1.0 / total)).astype(BF)


def attend_forward(pair, q_ref, k_ref, v_ref, kT_ref, kprT_ref, qpsT_ref, mask_ref, flip_ref, ctx_ref, pT_ref, scale):
    T = q_ref.shape[0]
    B = T // 2
    c0 = pl.multiple_of(pair * 128, 128)
    outs = []
    for hh in range(2):
        p = attend_head(q_ref, k_ref, v_ref, kT_ref, kprT_ref, qpsT_ref, mask_ref, flip_ref, c0, hh, scale)
        outs.append(nn(p, v_ref[:, pl.ds(c0, 128)]))
        pT_ref[2 * pair + hh, 0:B, :] = nt(flip_ref[...], p[:, B:T]).astype(BF)
        pT_ref[2 * pair + hh, B:T, :] = nt(flip_ref[...], p[:, 0:B]).astype(BF)
    ctx_ref[:, pl.ds(c0, 128)] = jnp.where(iota((1, 128), 1) < 64, outs[0], outs[1]).astype(BF)


def attend_backward(pair, q_ref, kf_ref, vf_ref, qT_ref, kfT_ref, kps_ref, qps_ref, dcT_ref, pT_ref,
                    dq_ref, dkf_ref, dvf_ref, dkpsT_ref, dqpsT_ref, scale):
    T = q_ref.shape[0]
    B = T // 2
    c0 = pl.multiple_of(pair * 128, 128)
    lanes = pl.ds(c0, 128)
    low = iota((1, 128), 1) < 64
    dqs, dks, dvs = [], [], []
    for hh in range(2):
        h = 2 * pair + hh
        r0 = pl.multiple_of(c0 + 64 * hh, 64)
        keep = (iota((1, 128), 1) // 64 == hh)
        vh = jnp.where(keep, vf_ref[:, lanes], 0)
        pT = pT_ref[h]
        dpT = nn(vh, dcT_ref[lanes, :])
        pw = pT.astype(F32)
        prod = pw * dpT
        inner = jnp.sum(prod, axis=0, keepdims=True) / jnp.sum(pw, axis=0, keepdims=True)
        dsT = (prod - pw * inner).astype(BF)
        dvs.append(nt(pT, dcT_ref[lanes, :]))
        dk = nn(dsT, q_ref[:, lanes])
        ds = dsT.T
        dq = nn(ds, kf_ref[:, lanes])
        zero = jnp.zeros((B, B), BF)
        dkp, dqp, gq, gk = [], [], [], []
        for b in range(2):
            gf = pltpu.roll(jnp.concatenate([dsT[b * B:(b + 1) * B], zero], axis=1), 0, 1, stride=1, stride_axis=0)
            dkp.append(nn(gf, qps_ref[b * B:b * B + 3 * B, lanes]))
            gq.append(nn(kfT_ref[pl.ds(r0, 64), b * B:(b + 1) * B], gf))
            gt = pltpu.roll(jnp.concatenate([ds[b * B:(b + 1) * B], zero], axis=1), 0, 1, stride=1, stride_axis=0)
            dqp.append(nn(gt, kps_ref[b * B:b * B + 3 * B, lanes]))
            gk.append(nn(qT_ref[pl.ds(r0, 64), b * B:(b + 1) * B], gt))
        dks.append(dk + jnp.concatenate(dkp, axis=0))
        dqs.append(dq + jnp.concatenate(dqp, axis=0))
        for ref, g in ((dqpsT_ref, gq), (dkpsT_ref, gk)):
            ref[pl.ds(r0, 64), 0:B] = (scale * g[0][:, 0:B]).astype(BF)
            ref[pl.ds(r0, 64), B:3 * B] = (scale * (g[0][:, B:] + g[1][:, 0:2 * B])).astype(BF)
            ref[pl.ds(r0, 64), 3 * B:] = (scale * g[1][:, 2 * B:]).astype(BF)
    dq_ref[:, lanes] = (scale * jnp.where(low, dqs[0], dqs[1])).astype(BF)
    dkf_ref[:, lanes] = (scale * jnp.where(low, dks[0], dks[1])).astype(BF)
    dvf_ref[:, lanes] = jnp.where(low, dvs[0], dvs[1]).astype(BF)


def normal_cdf_pair(x):
    a = jnp.abs(x)
    e = jnp.exp2(x * x * (-0.5 * 1.4426950408889634))
    t = 1.0 / (1.0 + (0.3275911 * 0.7071067811865476) * a)
    poly = ((((1.061405429 * t - 1.453152027) * t + 1.421413741) * t - 0.284496736) * t + 0.254829592) * t
    tail = 0.5 * poly * e
    return jnp.where(x < 0, tail, 1.0 - tail), e


def row_mean(x):
    return jnp.sum(x, axis=1, keepdims=True) * (1.0 / x.shape[1])


def norm_rows(x):
    centred = x - row_mean(x)
    inv = lax.rsqrt(row_mean(centred * centred) + EPS)
    return centred * inv, inv


def norm_back(g, n, inv):
    return (g - row_mean(g) - n * row_mean(g * n)) * inv


def column_sum(x):
    return jnp.sum(x, axis=0, keepdims=True)


def dense_block(length, x_ref, ctx_ref, cot_ref, wo_ref, wup_ref, wdown_ref, rows_ref, bup_ref,
                out_ref, gmixed_ref, dcT_ref, gwo_ref, gwup_ref, gwdown_ref, small_ref, gbup_ref,
                normed_ref, nb_ref, n1_ref, inv1_ref, act_ref, gp_ref, second_ref, gd_ref, gu_ref):
    T, D = x_ref.shape
    FF = wup_ref.shape[1]
    C = 256
    row = lambda k: rows_ref[k:k + 1, :]

    def cols(n, size=C):
        return pl.ds(pl.multiple_of(n * size, size), size)

    @pl.loop(0, D // C)
    def _(n):
        second_ref[:, cols(n)] = x_ref[:, cols(n)].astype(F32) + (nn(ctx_ref[...], wo_ref[:, cols(n)]) + rows_ref[3:4, cols(n)])

    R = 128

    @pl.loop(0, T // R)
    def _(r):
        rs = pl.ds(pl.multiple_of(r * R, R), R)
        n1, inv1 = norm_rows(second_ref[rs, :])
        normed = n1 * row(4) + row(5)
        n1_ref[rs, :] = n1
        inv1_ref[rs, :] = jnp.broadcast_to(inv1, (R, 128))
        normed_ref[rs, :] = normed
        nb_ref[rs, :] = normed.astype(BF)

    @pl.loop(0, FF // C)
    def _(n):
        up = nn(nb_ref[...], wup_ref[:, cols(n)]) + bup_ref[0:1, cols(n)]
        phi, e = normal_cdf_pair(up)
        act_ref[:, cols(n)] = (up * phi).astype(BF)
        gp_ref[:, cols(n)] = (phi + up * e * 0.3989422804014327).astype(gp_ref.dtype)

    @pl.loop(0, D // C)
    def _(n):
        second_ref[:, cols(n)] = normed_ref[:, cols(n)] + (nn(act_ref[...], wdown_ref[:, cols(n)]) + rows_ref[6:7, cols(n)])

    small_ref[...] = jnp.zeros_like(small_ref)

    @pl.loop(0, T // R)
    def _(r):
        rs = pl.ds(pl.multiple_of(r * R, R), R)
        live = jnp.where(iota((R, 1), 0) + r * R < length, 1.0, 0.0)
        n2, inv2 = norm_rows(second_ref[rs, :])
        out_ref[rs, :] = ((n2 * row(7) + row(8)) * live).astype(BF)
        start = cot_ref[rs, :].astype(F32) * live
        gsec = norm_back(start * row(7), n2, inv2)
        second_ref[rs, :] = gsec
        gd = gsec.astype(BF)
        gd_ref[rs, :] = gd
        small_ref[6:7, :] += column_sum(gd.astype(F32))
        small_ref[7:8, :] += column_sum(start * n2)
        small_ref[8:9, :] += column_sum(start)

    @pl.loop(0, FF // C)
    def _(n):
        gu = nt(gd_ref[...], wdown_ref[cols(n), :]) * gp_ref[:, cols(n)].astype(F32)
        gub = gu.astype(BF)
        gu_ref[:, cols(n)] = gub
        gbup_ref[0:1, cols(n)] = column_sum(gub.astype(F32))
        gwdown_ref[cols(n), :] = tn(act_ref[:, cols(n)], gd_ref[...]).astype(gwdown_ref.dtype)
        gwup_ref[:, cols(n)] = tn(nb_ref[...], gub).astype(gwup_ref.dtype)

    @pl.loop(0, D // C)
    def _(n):
        second_ref[:, cols(n)] += nt(gu_ref[...], wup_ref[cols(n), :])

    @pl.loop(0, T // R)
    def _(r):
        rs = pl.ds(pl.multiple_of(r * R, R), R)
        gn = second_ref[rs, :]
        n1 = n1_ref[rs, :]
        gm = norm_back(gn * row(4), n1, inv1_ref[rs, 0:1])
        gmixed_ref[rs, :] = gm
        ga = gm.astype(BF)
        gd_ref[rs, :] = ga
        small_ref[3:4, :] += column_sum(ga.astype(F32))
        small_ref[4:5, :] += column_sum(gn * n1)
        small_ref[5:6, :] += column_sum(gn)

    @pl.loop(0, D // C)
    def _(n):
        gwo_ref[cols(n), :] = tn(ctx_ref[:, cols(n)], gd_ref[...]).astype(gwo_ref.dtype)
        dcT_ref[cols(n), :] = nt(wo_ref[cols(n), :], gd_ref[...]).astype(BF)


def project(x_ref, relT_ref, wq_ref, wk_ref, wv_ref, rows_ref, bcols_ref, idx_ref, flip_ref,
            q_ref, k_ref, v_ref, qT_ref, kT_ref, kf_ref, vf_ref, kfT_ref, kprT_ref, qpsT_ref, kpsT_ref,
            pickB_ref, pickA_ref):
    T, D = x_ref.shape
    NB = relT_ref.shape[1]
    C = 256
    B = T // 2

    def cols(n, size=C):
        return pl.ds(pl.multiple_of(n * size, size), size)

    pickA_ref[...] = jnp.where(iota((NB, 2 * T), 0) == idx_ref[0:1, :], 1.0, 0.0).astype(BF)
    pickB_ref[...] = jnp.where(iota((NB, 2 * T), 0) == idx_ref[1:2, :], 1.0, 0.0).astype(BF)

    @pl.loop(0, D // C)
    def _(n):
        q = (nn(x_ref[...], wq_ref[:, cols(n)]) + rows_ref[0:1, cols(n)]).astype(BF)
        q_ref[:, cols(n)] = q
        qT_ref[cols(n), :] = q.T
        k = (nn(x_ref[...], wk_ref[:, cols(n)]) + rows_ref[1:2, cols(n)]).astype(BF)
        k_ref[:, cols(n)] = k
        kT_ref[cols(n), :] = k.T
        v = (nn(x_ref[...], wv_ref[:, cols(n)]) + rows_ref[2:3, cols(n)]).astype(BF)
        v_ref[:, cols(n)] = v
        for src, dst in ((k, kf_ref), (v, vf_ref)):
            dst[0:B, cols(n)] = nn(flip_ref[...], src[B:T]).astype(BF)
            dst[B:T, cols(n)] = nn(flip_ref[...], src[0:B]).astype(BF)
        kfT_ref[cols(n), :] = kf_ref[:, cols(n)].T
        rk = (tn(wk_ref[:, cols(n)], relT_ref[...]) + bcols_ref[cols(n), 1:2].astype(F32)).astype(BF)
        rq = (tn(wq_ref[:, cols(n)], relT_ref[...]) + bcols_ref[cols(n), 0:1].astype(F32)).astype(BF)
        kprT_ref[cols(n), :] = nn(rk, pickA_ref[...]).astype(BF)
        kpsT_ref[cols(n), :] = nn(rk, pickB_ref[...]).astype(BF)
        qpsT_ref[cols(n), :] = nn(rq, pickB_ref[...]).astype(BF)


def project_back(x_ref, relT_ref, wq_ref, wk_ref, wv_ref, pickB_ref, flip_ref, gmixed_ref,
                 dq_ref, dkf_ref, dvf_ref, dkpsT_ref, dqpsT_ref,
                 gtok_ref, gwq_ref, gwk_ref, gwv_ref, grelT_ref, small_ref,
                 dk_ref, dv_ref, grk_ref, grq_ref):
    T, D = x_ref.shape
    NB = relT_ref.shape[1]
    C = 256
    B = T // 2

    def cols(n, size=C):
        return pl.ds(pl.multiple_of(n * size, size), size)

    @pl.loop(0, D // C)
    def _(n):
        for src, dst in ((dkf_ref, dk_ref), (dvf_ref, dv_ref)):
            dst[0:B, cols(n)] = nn(flip_ref[...], src[B:T, cols(n)]).astype(BF)
            dst[B:T, cols(n)] = nn(flip_ref[...], src[0:B, cols(n)]).astype(BF)
        grk_ref[cols(n), :] = nt(dkpsT_ref[cols(n), :], pickB_ref[...]).astype(BF)
        grq_ref[cols(n), :] = nt(dqpsT_ref[cols(n), :], pickB_ref[...]).astype(BF)

    ones_t = jnp.ones((8, T), BF)
    ones_b = jnp.ones((8, NB), BF)

    @pl.loop(0, D // C)
    def _(n):
        gwq_ref[cols(n), :] = (tn(x_ref[:, cols(n)], dq_ref[...]) + nt(relT_ref[cols(n), :], grq_ref[...])).astype(gwq_ref.dtype)
        gwk_ref[cols(n), :] = (tn(x_ref[:, cols(n)], dk_ref[...]) + nt(relT_ref[cols(n), :], grk_ref[...])).astype(gwk_ref.dtype)
        gwv_ref[cols(n), :] = tn(x_ref[:, cols(n)], dv_ref[...]).astype(gwv_ref.dtype)
        grelT_ref[cols(n), :] = (nn(wk_ref[cols(n), :], grk_ref[...]) + nn(wq_ref[cols(n), :], grq_ref[...])).astype(grelT_ref.dtype)
        gtok_ref[:, cols(n)] = gmixed_ref[:, cols(n)] + (
            nt(dq_ref[...], wq_ref[cols(n), :]) + nt(dk_ref[...], wk_ref[cols(n), :]) + nt(dv_ref[...], wv_ref[cols(n), :]))
        small_ref[0:1, cols(n)] = (nn(ones_t, dq_ref[:, cols(n)]) + nt(ones_b, grq_ref[cols(n), :]))[0:1]
        small_ref[1:2, cols(n)] = (nn(ones_t, dk_ref[:, cols(n)]) + nt(ones_b, grk_ref[cols(n), :]))[0:1]
        small_ref[2:3, cols(n)] = nn(ones_t, dv_ref[:, cols(n)])[0:1]


def vmem_call(kernel, outs, scratch, operands, smem=0):
    specs = [pl.BlockSpec(memory_space=pltpu.SMEM)] * smem + [pl.BlockSpec(memory_space=pltpu.VMEM)] * (len(operands) - smem)
    return pl.pallas_call(
        kernel,
        out_shape=outs,
        in_specs=specs,
        out_specs=tuple(pl.BlockSpec(memory_space=pltpu.VMEM) for _ in outs),
        scratch_shapes=scratch,
        compiler_params=pltpu.CompilerParams(vmem_limit_bytes=60 * 2**20),
    )(*operands)


def layer(x, length, rel_index, cot, wq, wk, wv, wo, relT, wup, wdown, bcols, bup, grad_type):
    T, D = x.shape
    FF = wup.shape[1]
    NB = relT.shape[1]
    heads = D // 64
    scale = 192.0 ** -0.5
    S = jax.ShapeDtypeStruct
    V = pltpu.VMEM
    rows = bcols.astype(F32).T
    bup8 = jnp.broadcast_to(bup.astype(F32)[None, :], (8, FF))
    bcols = jnp.pad(bcols, ((0, 0), (0, 128 - bcols.shape[1])))
    shifted = jnp.concatenate([rel_index[1:], jnp.full((1,), -1, jnp.int32)])
    idx = jnp.concatenate([rel_index[None, ::-1], shifted[None, :], jnp.zeros((6, 2 * T), jnp.int32)])
    flip = flip_matrix(T // 2)
    mask = jnp.broadcast_to(jnp.where(jnp.arange(T)[None, :] < length[0], 0.0, -1e30).astype(F32), (8, T))

    td, dt, d2t = S((T, D), BF), S((D, T), BF), S((D, 2 * T), BF)
    q, k, v, qT, kT, kf, vf, kfT, kprT, qpsT, kpsT, pick = vmem_call(
        project, (td, td, td, dt, dt, td, td, dt, d2t, d2t, d2t, S((NB, 2 * T), BF)),
        (V((NB, 2 * T), BF),),
        (x, relT, wq, wk, wv, rows, bcols, idx, flip))

    def forward(*refs):
        @pl.loop(0, heads // 2)
        def _(p):
            attend_forward(p, *refs, scale)

    ctx, pT = vmem_call(forward, (td, S((heads, T, T), BF)), (), (q, k, v, kT, kprT, qpsT, mask, flip))

    def dense(length_ref, *refs):
        dense_block(length_ref[0], *refs)

    out, gmixed, dcT, gwo, gwup, gwdown, small, gbup = vmem_call(
        dense,
        (td, S((T, D), F32), dt, S((D, D), grad_type), S((D, FF), grad_type), S((FF, D), grad_type), S((16, D), F32), S((8, FF), F32)),
        (V((T, D), F32), V((T, D), BF), V((T, D), F32), V((T, 128), F32), V((T, FF), BF), V((T, FF), BF), V((T, D), F32), V((T, D), BF), V((T, FF), BF)),
        (length, x, ctx, cot, wo, wup, wdown, rows, bup8), smem=1)

    def backward(*refs):
        @pl.loop(0, heads // 2)
        def _(p):
            attend_backward(p, *refs, scale)

    dq, dkf, dvf, dkpsT, dqpsT = vmem_call(
        backward, (td, td, td, d2t, d2t), (), (q, kf, vf, qT, kfT, kpsT.T, qpsT.T, dcT, pT))
    gtok, gwq, gwk, gwv, grelT, small2 = vmem_call(
        project_back,
        (S((T, D), F32), S((D, D), grad_type), S((D, D), grad_type), S((D, D), grad_type), S((D, NB), grad_type), S((16, D), F32)),
        (V((T, D), BF), V((T, D), BF), V((D, NB), BF), V((D, NB), BF)),
        (x, relT, wq, wk, wv, pick, flip, gmixed, dq, dkf, dvf, dkpsT, dqpsT))
    small = jnp.concatenate([small2[:3], small[3:9]])
    return out, gtok, gwq, gwk, gwv, gwo, grelT, gwup, gwdown, small, gbup[0]


AXES = ("dp", "fsdp")


def body(tokens, lengths, rel_index, w_query, b_query, w_key, b_key, w_value, b_value, w_out, b_out, rel_table,
         gain_one, shift_one, w_up, b_up, w_down, b_down, gain_two, shift_two, cotangent):
    rows, D = w_query.shape
    NB = rel_table.shape[0]
    FF = w_up.shape[1]
    vectors = (b_query, b_key, b_value, b_out, gain_one, shift_one, b_down, gain_two, shift_two)
    per = FF // D
    cols = jnp.concatenate([jnp.stack(vectors, axis=1), b_up.reshape(rows, per), jnp.zeros((rows, 128 - 9 - per), BF)], axis=1)
    pack = jnp.concatenate([w_query, w_key, w_value, w_out, rel_table.T, cols], axis=1)
    gathered = lax.all_gather(pack, AXES, axis=0, tiled=True)
    wup = lax.all_gather(w_up, AXES, axis=0, tiled=True)
    wdown = lax.all_gather(w_down, AXES, axis=0, tiled=True)
    wq, wk, wv, wo = (gathered[:, i * D:(i + 1) * D] for i in range(4))
    relT = gathered[:, 4 * D:4 * D + NB]
    bcols = gathered[:, 4 * D + NB:]
    bup = bcols[:, 9:9 + per].reshape(FF)
    bcols = jnp.concatenate([bcols[:, :9], jnp.zeros((D, 7), BF)], axis=1)
    out, gtok, gwq, gwk, gwv, gwo, grelT, gwup, gwdown, small, gbup = layer(
        tokens, lengths, rel_index, cotangent, wq, wk, wv, wo, relT, wup, wdown, bcols, bup, F32)
    gwup = lax.psum_scatter(gwup, AXES, scatter_dimension=0, tiled=True)
    gwdown = lax.psum_scatter(gwdown, AXES, scatter_dimension=0, tiled=True)
    gcols = jnp.concatenate([small.T, gbup.reshape(D, per), jnp.zeros((D, 128 - 9 - per), F32)], axis=1)
    gpack = jnp.concatenate([gwq, gwk, gwv, gwo, grelT, gcols], axis=1)
    gpack = lax.psum_scatter(gpack, AXES, scatter_dimension=0, tiled=True)
    gq, gk, gv, go = (gpack[:, i * D:(i + 1) * D] for i in range(4))
    grel = gpack[:, 4 * D:4 * D + NB].T
    g = gpack[:, 4 * D + NB:]
    return (out, gtok, gq, g[:, 0], gk, g[:, 1], gv, g[:, 2], go, g[:, 3], grel, g[:, 4], g[:, 5],
            gwup, g[:, 9:9 + per].reshape(rows * per), gwdown, g[:, 6], g[:, 7], g[:, 8])


def solution(mesh):
    rows, vec = P(AXES, None), P(AXES)
    return jax.shard_map(
        body,
        mesh=mesh,
        in_specs=(rows, vec, P(), rows, vec, rows, vec, rows, vec, rows, vec, P(None, AXES), vec, vec, rows, vec, rows, vec, vec, vec, rows),
        out_specs=(rows, rows, rows, vec, rows, vec, rows, vec, rows, vec, P(None, AXES), vec, vec, rows, vec, rows, vec, vec, vec),
        check_vma=False,
    )
```

time: 1830 us -> 828 us (0.45); the launches traced: 1810 us -> 827 us
  local copies, waits for them, and re-layouts: 487 us -> 45.8 us
  matrix products: 387 us -> 0 us
  blocking collectives: 154 us -> 0 us
  Pallas kernels: 0 us -> 134 us
  waiting for transfers between devices: 732 us -> 630 us
  other arithmetic: 32.1 us -> 2.55 us
    dot_general x206 -> x0, matrix products: 387 us -> none  [the longest x92 148 us: contract_cols(): lax.dot_general(left, right, (((1,), (1,)), ((), ())), preferred_element_...]
    reshape x98 -> x2, local copies, waits for them, and re-layouts: 262 us -> 1.36 us  [the longest x1 0.75 us: body(): b_up.reshape(rows, per)]
    pallas_call x0 -> x5, Pallas kernels: none -> 134 us  [vmem_call(): pl.pallas_call(kernel, out_shape=outs, in_specs=specs, out_specs=tuple((p...]
    reduce_scatter x4 -> x2, waiting for transfers between devices: 393 us -> 276 us  [the longest x1 142 us: body(): gwdown = lax.psum_scatter(gwdown, AXES, scatter_dimension=0, tiled=True)]
    all_gather x6 -> x3, waiting for transfers between devices: 22.8 us -> 134 us  [the longest x1 65.3 us: body(): wdown = lax.all_gather(w_down, AXES, axis=0, tiled=True)]
    unnamed x16 -> x7, waiting for transfers between devices: 316 us -> 220 us
    unnamed x2 -> x0, blocking collectives: 83 us -> none
    pad x48 -> x1, local copies, waits for them, and re-layouts: 76 us -> 0.72 us  [layer(): bcols = jnp.pad(bcols, ((0, 0), (0, 128 - bcols.shape[1])))]
  transfers between devices with their start and end apart: 13 -> 6, of which waited for: 8 -> 6; matrix products, arithmetic and copies ran while one was open for 16% -> 3% of each run, Pallas kernels for 0% -> 6%
where the time goes in v1:
time: 828 us; the launch traced here: 827 us
  waiting for transfers between devices  630 us (76%)
  Pallas kernels  134 us (16%)
  local copies, waits for them, and re-layouts  45.8 us (6%)
  between operations  14.9 us (2%)
    unnamed x7, waiting for transfers between devices  220 us
    reduce_scatter x1, waiting for transfers between devices, body(): gwdown = lax.psum_scatter(gwdown, AXES, scatter_dimension=0, tiled=True)  142 us
    reduce_scatter x1, waiting for transfers between devices, body(): gwup = lax.psum_scatter(gwup, AXES, scatter_dimension=0, tiled=True)  134 us
    pallas_call x5, Pallas kernels, vmem_call(): pl.pallas_call(kernel, out_shape=outs, in_specs=specs, out_specs=tuple((p...  134 us
    all_gather x1, waiting for transfers between devices, body(): wdown = lax.all_gather(w_down, AXES, axis=0, tiled=True)  65.3 us
    all_gather x1, waiting for transfers between devices, body(): gathered = lax.all_gather(pack, AXES, axis=0, tiled=True)  64.6 us
  transfers between devices with their start and end apart: 6, of which 6 were waited for; matrix products, arithmetic and copies ran while one was open for 3% of the time, Pallas kernels for 6%

profile of v1, /device:TPU:0, one launch (start us, length us, event | category | flops | bytes accessed | tf_op | source)
XLA Modules:
  0.0 827.4 jit_solution(16923076514713191572)
XLA Ops:
  14.7 1.6 concatenate.18
  21.6 64.6 %all-gather.4.cloned.1.call-done = bf16[768,3712]{1,0:T(8,128)(2,1)} async-done(((bf16[24,3712]{1,0:T(8,128)(2,1)}), bf16[768,3712]{1,0:T(8,128)(2,1)}) %all-gather.4.cloned.1.call-update) | async-done | bytes 5701648 | tf_op jit(solution)/shard_map/all_gather | solution.py:378
  86.2 0.9 slice.122
  88.7 1.0 slice_convert_fusion
  90.0 2.1 slice.118.relT_ref
  92.1 4.7 fusion.2
  96.8 13.5 %shard_map.348 = (bf16[512,768]{1,0:T(8,128)(2,1)}, bf16[512,768]{1,0:T(8,128)(2,1)}, bf16[512,768]{1,0:T(8,128)(2,1)}, bf16[768,512]{1,0:T(8,128)(2,1)}, bf16[7...) custom-call(bf16[512,768]{1,0:T(8,128)(2,1)} %x_ref.3, ...), custom_call_target="tpu_custom_call" | custom-call | tf_op jit(solution)/shard_map/pallas_call | solution.py:302
  110.3 2.7 copy.82
  113.0 1.6 copy.81
  115.2 32.0 %shard_map.349 = (bf16[512,768]{1,0:T(8,128)(2,1)}, bf16[12,512,512]{2,1,0:T(8,128)(2,1)}) custom-call(bf16[512,768]{1,0:T(8,128)(2,1)} %get-tuple-element.52.refs_0_, bf16[512,768]{1,0:T(8,128)(2,1)} %get-tuple-element.53.refs_1_, bf16[512,768]{1,0:T(8,128)(2,1)} %get-tuple-element.54.refs_2_, bf16[768,512]{1,0:T(8,128)(2,1)} %get-tuple-element.55.refs_3_, ...), custom_call_target="tpu_custom_call" | custom-call | tf_op jit(solution)/shard_map/pallas_call | solution.py:302
  147.2 4.4 all-gather.6.cloned.1.call-done.refs_4_
  151.7 65.3 %all-gather.8.cloned.1.call-done.refs_5_ = bf16[3072,768]{1,0:T(8,128)(2,1)} async-done(((bf16[96,768]{1,0:T(8,128)(2,1)}), bf16[3072,768]{1,0:T(8,128)(2,1)}) %all-gather.8.cloned.1.call-update) | async-done | bytes 4718608 | tf_op jit(solution)/shard_map/all_gather | solution.py:380
  217.6 45.3 %shard_map.350 = (bf16[512,768]{1,0:T(8,128)(2,1)}, f32[512,768]{1,0:T(8,128)}, bf16[768,512]{1,0:T(8,128)(2,1)}, f32[768,768]{1,0:T(8,128)}, f32[768,3072]{1,0:...) custom-call(s32[1]{0:T(128)} %copy.85.length_ref, bf16[512,768]{1,0:T(8,128)(2,1)} %x_ref.3, ...), custom_call_target="tpu_custom_call" | custom-call | tf_op jit(solution)/shard_map/pallas_call | solution.py:302
  262.9 25.6 %shard_map.351 = (bf16[512,768]{1,0:T(8,128)(2,1)}, bf16[512,768]{1,0:T(8,128)(2,1)}, bf16[512,768]{1,0:T(8,128)(2,1)}, bf16[768,1024]{1,0:T(8,128)(2,1)}, bf16[768,1024]{1,0:T(8,128)(2,1)}) custom-call(bf16[512,768]{1,0:T(8,128)(2,1)} %get-tuple-element.52.refs_0_, bf16[512,768]{1,0:T(8,128)(2,1)} %get-tuple-element.62.refs_1_, ...), custom_call_target="tpu_custom_call" | custom-call | tf_op jit(solution)/shard_map/pallas_call | solution.py:302
  288.5 17.2 %shard_map.352 = (f32[512,768]{1,0:T(8,128)}, f32[768,768]{1,0:T(8,128)}, f32[768,768]{1,0:T(8,128)}, f32[768,768]{1,0:T(8,128)}, f32[768,512]{1,0:T(8,128)}, /*index=5*/f32[16,768]{1,0:T(8,128)}) custom-call(bf16[512,768]{1,0:T(8,128)(2,1)} %x_ref.3, bf16[768,512]{1,0:T(8,128)(2,1)} %slice.118.relT_ref, bf16[768,768]{1,0:T(8,128)(2,1)} %get-tuple-element.101.wq_ref, ...), custom_call_target="tpu_custom_call" | custom-call | tf_op jit(solution)/shard_map/pallas_call | solution.py:302
  306.7 0.9 slice_reduce_fusion
  308.1 11.3 %concatenate.23 = f32[768,3712]{1,0:T(8,128)} concatenate(f32[768,768]{1,0:T(8,128)} %get-tuple-element.75, f32[768,768]{1,0:T(8,128)} %get-tuple-element.76, f32[768,768]{1,0:T(8,128)} %get-tuple-element.77, f32[768,768]{1,0:T(8,128)S(1)} %copy-done, f32[768,512]{1,0:T(8,128)} %get-tuple-element.79, f32[768,9]{1,0:T(8,128)S(1)} %bitcast.23, f32[768,4]{1,0:T(8,128)S(1)} %reshape_squeeze.3, ...), dimensions={1} | concatenate | bytes 22806528 | tf_op jit(solution)/shard_map/concatenate | solution.py:391
  320.5 217.2 %all-reduce.5.cloned.1.call-done = f32[768,3712]{1,0:T(8,128)} async-done(((f32[768,3712]{1,0:T(8,128)}), f32[768,3712]{1,0:T(8,128)}) %all-reduce.5.cloned.1.call-update) | async-done | bytes 11403280
  537.7 0.8 dynamic-slice.12
  539.1 1.9 dynamic-slice_reduce_fusion
  541.0 1.5 dynamic-slice_bitcast_fusion
  542.6 1.8 fusion.1
  544.4 134.0 %reduce-scatter.3.cloned.1.call-done = f32[24,3072]{1,0:T(8,128)} async-done(((f32[768,3072]{1,0:T(8,128)}), f32[24,3072]{1,0:T(8,128)}) %reduce-scatter.3.cloned.1.call-update) | async-done | bytes 294928 | tf_op jit(solution)/shard_map/reduce_scatter | solution.py:388
  678.4 142.2 %reduce-scatter.5.cloned.1.call-done = f32[96,768]{1,0:T(8,128)} async-done(((f32[3072,768]{1,0:T(8,128)}), f32[96,768]{1,0:T(8,128)}) %reduce-scatter.5.cloned.1.call-update) | async-done | bytes 294928 | tf_op jit(solution)/shard_map/reduce_scatter | solution.py:389
  (50 shorter events, 18.2 us)
Async XLA Ops:
  7.2 79.0 %all-gather.4.cloned.1.call-start = ((), (), s32[]{:S(2)}) async-start(), calls=%async_computation.2 | async-start | bytes 5879808 | tf_op jit(solution)/shard_map/all_gather | solution.py:378
  16.4 135.3 %all-gather.6.cloned.1.call-start = ((), (), s32[]{:S(2)}) async-start(), calls=%async_computation.3 | async-start | bytes 4866048 | tf_op jit(solution)/shard_map/all_gather | solution.py:379
  17.1 199.9 %all-gather.8.cloned.1.call-start = ((), (), s32[]{:S(2)}) async-start(), calls=%async_computation.4 | async-start | bytes 4866048 | tf_op jit(solution)/shard_map/all_gather | solution.py:380
  17.8 519.9 %all-reduce.5.cloned.1.call-start = ((), (), s32[]{:S(2)}) async-start(), calls=%async_computation.7 | async-start | bytes 22806528
  110.3 2.7 copy-start.1
  288.5 18.0 %copy-start.2 = (f32[16,768]{1,0:T(8,128)S(1)}, f32[16,768]{1,0:T(8,128)}, u32[]{:S(2)}) copy-start(f32[16,768]{1,0:T(8,128)} %get-tuple-element.81) | copy-start | bytes 147460
  288.5 19.5 %copy-start = (f32[768,768]{1,0:T(8,128)S(1)}, f32[768,768]{1,0:T(8,128)}, u32[]{:S(2)}) copy-start(f32[768,768]{1,0:T(8,128)} %get-tuple-element.78) | copy-start | bytes 7077892
  319.3 359.0 %reduce-scatter.3.cloned.1.call-start = ((), (), s32[]{:S(2)}) async-start(), calls=%async_computation.5 | async-start | bytes 9732096 | tf_op jit(solution)/shard_map/reduce_scatter | solution.py:388
  319.9 500.6 %reduce-scatter.5.cloned.1.call-start = ((), (), s32[]{:S(2)}) async-start(), calls=%async_computation.6 | async-start | bytes 9732096 | tf_op jit(solution)/shard_map/reduce_scatter | solution.py:389
Sparse Core Ops, SparseCore 0:
  16.5 69.7 all-gather.3
  89.1 62.5 all-gather.5
  154.6 62.3 all-gather.7
  319.5 218.2 all-reduce.4
  544.1 134.2 reduce-scatter.2
  685.7 134.8 reduce-scatter.4

commit v2 on v1

v2 whole, which is shorter than its diff:
```python
import jax
import jax.numpy as jnp
from jax import lax
from jax.experimental import pallas as pl
from jax.experimental.pallas import tpu as pltpu
from jax.sharding import PartitionSpec as P

BF = jnp.bfloat16
F32 = jnp.float32
EPS = 1e-6
HEAD = 64
AXES = ("dp", "fsdp")
MESH = pl.DeviceIdType.MESH
LOG2E = 1.4426950408889634
GRID = (2, 4, 2, 2)
BLOCKS = 32
CUT = 384
SLOTS = 3


def dot(left, right, dims):
    return lax.dot_general(left, right, ((dims[:1], dims[1:]), ((), ())), preferred_element_type=F32)


def nn(left, right):
    return dot(left, right, (1, 0))


def nt(left, right):
    return dot(left, right, (1, 1))


def tn(left, right):
    return dot(left, right, (0, 0))


def iota(shape, axis):
    return lax.broadcasted_iota(jnp.int32, shape, axis)


def column_sum(x):
    return jnp.sum(x, axis=0, keepdims=True)


def row_mean(x):
    return jnp.sum(x, axis=1, keepdims=True) * (1.0 / x.shape[1])


def norm_rows(x):
    centred = x - row_mean(x)
    inv = lax.rsqrt(row_mean(centred * centred) + EPS)
    return centred * inv, inv


def norm_back(g, n, inv):
    return (g - row_mean(g) - n * row_mean(g * n)) * inv


def normal_cdf_pair(x):
    a = jnp.abs(x)
    e = jnp.exp2(x * x * (-0.5 * LOG2E))
    t = 1.0 / (1.0 + (0.3275911 * 0.7071067811865476) * a)
    poly = ((((1.061405429 * t - 1.453152027) * t + 1.421413741) * t - 0.284496736) * t + 0.254829592) * t
    tail = 0.5 * poly * e
    return jnp.where(x < 0, tail, 1.0 - tail), e


def tile(n, size):
    return pl.ds(pl.multiple_of(n * size, size), size)


def matrix(value):
    rows = 1
    for size in value.shape[:-1]:
        rows *= size
    return value.reshape(rows, value.shape[-1])


def pair_forward(pair, q_ref, k_ref, v_ref, kprT_ref, qpsT_ref, mask_ref, flip_ref, ctx_ref, pT_ref, scale):
    T = q_ref.shape[0]
    B = T // 2
    lanes = tile(pair, 128)
    outs = []
    for hh in range(2):
        keep = iota((1, 128), 1) // HEAD == hh
        qh = jnp.where(keep, q_ref[:, lanes], 0)
        kh = jnp.where(keep, k_ref[:, lanes], 0)
        content = nt(qh, k_ref[:, lanes])
        to, frm = [], []
        for b in range(2):
            u0 = B * (1 - b)
            t = nn(qh[b * B:(b + 1) * B], kprT_ref[lanes, u0:u0 + 3 * B])
            to.append(pltpu.roll(t, 2 * B + 1, 1, stride=1, stride_axis=0)[:, :T])
            f = nn(kh[b * B:(b + 1) * B], qpsT_ref[lanes, u0:u0 + 3 * B])
            frm.append(pltpu.roll(f, 2 * B + 1, 1, stride=1, stride_axis=0)[:, :T].T)
        s = content + jnp.concatenate(to, axis=0) + jnp.concatenate(frm, axis=1) + mask_ref[0:1, :]
        top = jnp.max(s, axis=1, keepdims=True)
        e = jnp.exp2((s - top) * (scale * LOG2E))
        p = (e * (1.0 / jnp.sum(e, axis=1, keepdims=True))).astype(BF)
        outs.append(nn(p, v_ref[:, lanes]))
        pT_ref[2 * pair + hh, 0:B, :] = nt(flip_ref[...], p[:, B:T]).astype(BF)
        pT_ref[2 * pair + hh, B:T, :] = nt(flip_ref[...], p[:, 0:B]).astype(BF)
    ctx_ref[:, lanes] = jnp.where(iota((1, 128), 1) < HEAD, outs[0], outs[1]).astype(BF)


def pair_backward(pair, q_ref, kf_ref, vf_ref, kpsT_ref, qpsT_ref, dcT_ref, pT_ref, scale):
    T = q_ref.shape[0]
    B = T // 2
    lanes = tile(pair, 128)
    low = iota((1, 128), 1) < HEAD
    q, kf, dcT = q_ref[:, lanes], kf_ref[:, lanes], dcT_ref[lanes, :]
    dqs, dks, dvs, gks, gqs = [], [], [], [], []
    for hh in range(2):
        vh = jnp.where(iota((1, 128), 1) // HEAD == hh, vf_ref[:, lanes], 0)
        pT = pT_ref[2 * pair + hh]
        dpT = nn(vh, dcT)
        wide = pT.astype(F32)
        prod = wide * dpT
        inner = column_sum(prod) / column_sum(wide)
        dsT = (prod - wide * inner).astype(BF)
        ds = dsT.T
        zero = jnp.zeros((B, B), BF)
        dk, dq, gq, gk = [], [], [], []
        for b in range(2):
            rows, span = slice(b * B, (b + 1) * B), slice(b * B, b * B + 3 * B)
            gf = pltpu.roll(jnp.concatenate([dsT[rows], zero], axis=1), 0, 1, stride=1, stride_axis=0)
            dk.append(nn(dsT[rows], q) + nt(gf, qpsT_ref[lanes, span]))
            gq.append(tn(kf[rows], gf)[hh * HEAD:(hh + 1) * HEAD])
            gt = pltpu.roll(jnp.concatenate([ds[rows], zero], axis=1), 0, 1, stride=1, stride_axis=0)
            dq.append(nn(ds[rows], kf) + nt(gt, kpsT_ref[lanes, span]))
            gk.append(tn(q[rows], gt)[hh * HEAD:(hh + 1) * HEAD])
        dks.append(jnp.concatenate(dk, axis=0))
        dqs.append(jnp.concatenate(dq, axis=0))
        dvs.append(nt(pT, dcT))
        gqs.append(gq)
        gks.append(gk)
    for ref, pieces in ((qpsT_ref, gqs), (kpsT_ref, gks)):
        for hh in range(2):
            g = pieces[hh]
            rows = pl.ds(pl.multiple_of(pair * 128 + HEAD * hh, HEAD), HEAD)
            ref[rows, 0:B] = (scale * g[0][:, 0:B]).astype(BF)
            ref[rows, B:3 * B] = (scale * (g[0][:, B:] + g[1][:, 0:2 * B])).astype(BF)
            ref[rows, 3 * B:] = (scale * g[1][:, 2 * B:]).astype(BF)
    q_ref[:, lanes] = (scale * jnp.where(low, dqs[0], dqs[1])).astype(BF)
    kf_ref[:, lanes] = (scale * jnp.where(low, dks[0], dks[1])).astype(BF)
    vf_ref[:, lanes] = jnp.where(low, dvs[0], dvs[1]).astype(BF)


class Place:
    def __init__(self):
        self.nz = GRID[1]
        self.c = lax.axis_index("dp")
        f = lax.axis_index("fsdp")
        self.x = lax.rem(f, 2)
        self.y = lax.rem(lax.div(f, 2), 2)
        self.z = lax.div(f, 4)
        self.nx = 1 - self.x
        self.ny = 1 - self.y

    def at(self, c=None, z=None, y=None, x=None):
        c = self.c if c is None else c
        z = self.z if z is None else z
        y = self.y if y is None else y
        x = self.x if x is None else x
        return (c, (z * 2 + y) * 2 + x)

    def zs(self):
        return [lax.rem(self.z + d, self.nz) for d in range(1, self.nz)]

    def barrier(self):
        sem = pltpu.get_barrier_semaphore()
        peers = [self.at(z=z) for z in self.zs()] + [self.at(x=self.nx), self.at(y=self.ny), self.at(c=1 - self.c)]
        for peer in peers:
            pl.semaphore_signal(sem, inc=1, device_id=peer, device_id_type=MESH)
        pl.semaphore_wait(sem, len(peers))


def remote(src, dst, send, recv, to):
    return pltpu.make_async_remote_copy(src_ref=src, dst_ref=dst, send_sem=send, recv_sem=recv, device_id=to, device_id_type=MESH)


class Gather:
    def __init__(self, place, piece, cols, send, recv):
        self.p, self.piece, self.send, self.recv = place, piece, send, recv
        self.all, self.h1, self.h2 = pl.ds(0, cols), pl.ds(0, CUT), pl.ds(CUT, cols - CUT)

    def copies(self, k, arriving=False):
        p, g, every = self.p, self.piece, slice(None)
        x, y, c = (p.nx, p.ny, 1 - p.c) if arriving else (p.x, p.y, p.c)
        if k == 0:
            for d in range(1, p.nz):
                z = lax.rem(p.z + (p.nz - d if arriving else d), p.nz)
                yield d - 1, g(p.c, z if arriving else p.z, p.y, p.x, self.all), p.at(z=z)
        elif k == 1:
            yield 3, g(p.c, every, p.y, x, self.h1), p.at(x=p.nx)
            yield 4, g(p.c, every, y, p.x, self.h2), p.at(y=p.ny)
        elif k == 2:
            yield 5, g(p.c, every, y, every, self.h1), p.at(y=p.ny)
            yield 6, g(p.c, every, every, x, self.h2), p.at(x=p.nx)
        else:
            yield 7, g(c, every, every, every, self.all), p.at(c=1 - p.c)

    def make(self, k, arriving=False):
        return [remote(ref, ref, self.send.at[i], self.recv.at[i], to) for i, ref, to in self.copies(k, arriving)]

    def step(self, k):
        if k > 0:
            for copy in self.make(k - 1, arriving=True):
                copy.wait_recv()
        if k < 4:
            for copy in self.make(k):
                copy.start()
        else:
            for j in range(4):
                for copy in self.make(j):
                    copy.wait_send()


def add_into(ref, other):
    ref[...] = (ref[...].astype(F32) + other[...].astype(F32)).astype(BF)


class Scatter:
    def __init__(self, place, piece, cols, order, buffers, send, recv, credit, finish):
        self.p, self.piece, self.order, self.send, self.recv = place, piece, order, send, recv
        self.credit, self.finish = credit, finish
        rest = pl.ds(0, cols - CUT)
        self.all, self.h1, self.h2 = pl.ds(0, cols), pl.ds(0, CUT), pl.ds(CUT, cols - CUT)
        rd, ry, rx, rx2, ry2, rz = buffers
        self.rd = rd.at[order % SLOTS, :, :, :, :, self.all]
        self.ry, self.rx = ry.at[order], rx.at[order, :, :, :, rest]
        self.rx2, self.ry2 = rx2.at[order], ry2.at[order, :, :, rest]
        self.rz = rz.at[order, :, :, self.all]

    def make(self, k):
        p, g, every = self.p, self.piece, slice(None)
        if k == 0:
            found = [(g(1 - p.c, every, every, every, self.all), self.rd, p.at(c=1 - p.c))]
        elif k == 1:
            found = [(g(p.c, every, p.ny, every, self.h1), self.ry, p.at(y=p.ny)),
                     (g(p.c, every, every, p.nx, self.h2), self.rx, p.at(x=p.nx))]
        elif k == 2:
            found = [(g(p.c, every, p.y, p.nx, self.h1), self.rx2, p.at(x=p.nx)),
                     (g(p.c, every, p.ny, p.x, self.h2), self.ry2, p.at(y=p.ny))]
        else:
            found = [(g(p.c, z, p.y, p.x, self.all), self.rz.at[d], p.at(z=z)) for d, z in enumerate(p.zs())]
        first = (0, 1, 3, 5)[k]
        return [remote(src, dst, self.send.at[first + i], self.recv.at[first + i], to) for i, (src, dst, to) in enumerate(found)]

    def step(self, k, last):
        p, g, every = self.p, self.piece, slice(None)
        if k > 0:
            for copy in self.make(k - 1):
                copy.wait_recv()
        if k == 0 and self.order >= SLOTS:
            pl.semaphore_wait(self.credit, 1)
        if k == 1:
            @pl.loop(0, p.nz)
            def _(z):
                add_into(g(p.c, z, every, every, self.all), self.rd.at[z])
            if self.order + SLOTS < last:
                pl.semaphore_signal(self.credit, inc=1, device_id=p.at(c=1 - p.c), device_id_type=MESH)
        elif k == 2:
            @pl.loop(0, p.nz)
            def _(z):
                add_into(g(p.c, z, p.y, every, self.h1), self.ry.at[z])
                add_into(g(p.c, z, every, p.x, self.h2), self.rx.at[z])
        elif k == 3:
            add_into(g(p.c, every, p.y, p.x, self.h1), self.rx2)
            add_into(g(p.c, every, p.y, p.x, self.h2), self.ry2)
        elif k == 4:
            total = g(p.c, p.z, p.y, p.x, self.all)[...].astype(F32)
            for d in range(p.nz - 1):
                total = total + self.rz[d].astype(F32)
            self.finish(total)
        if k < 4:
            for copy in self.make(k):
                copy.start()
        else:
            for j in range(4):
                for copy in self.make(j):
                    copy.wait_send()


def layer_kernel(
    comm,
    length_ref, idx_ref, x_ref, cot_ref, r_in, q_in, k_in, v_in, o_in, up_in, down_in,
    out_ref, gtok_ref, r_out, q_out, k_out, v_out, o_out, up_out, down_out,
    GR, GA, GO, GU, GD,
    q_ref, k_ref, v_ref, kf_ref, vf_ref, kprT_ref, kpsT_ref, qpsT_ref, pick_ref, pT_ref,
    ctx_ref, dcT_ref, n1_ref, inv1_ref, nb_ref, gd_ref, act_ref, gp_ref,
    grel_ref, cols_ref, rows_ref, bup_ref, small_ref, gbup_ref, mask_ref, flip_ref, select_ref,
    *rest,
):
    T, D = x_ref.shape
    FF = act_ref.shape[1]
    NB = pick_ref.shape[0]
    B = T // 2
    C = 256
    R = 128
    CH = FF // D
    scale = (3.0 * HEAD) ** -0.5
    length = length_ref[0]
    row = lambda k: rows_ref[k:k + 1, :]
    last = 1 + D // C + 1 + 2 * CH
    nA, nO, nU, nD = 1, 1 + D // C, 2 + D // C, 2 + D // C + CH
    whole = (slice(None),) * 4

    def part(ref, *lead, trail=()):
        return lambda c, z, y, x, cols: ref.at[(*lead, c, z, y, x, *trail, slice(None), cols)]

    pieces = ([(part(GR), NB + 128)] + [(part(GA, n), D) for n in range(D // C)] + [(part(GO), D)]
              + [(part(GU, k), D) for k in range(CH)] + [(part(GD, trail=(k,)), D) for k in range(CH)])
    gathers, scatters = [], []
    if comm:
        rd, ry, rx, rx2, ry2, rz, ag_send, ag_recv, rs_send, rs_recv, credit = rest
        place = Place()
        gathers = [Gather(place, piece, cols, ag_send.at[i], ag_recv.at[i]) for i, (piece, cols) in enumerate(pieces)]
        order = [nU + k for k in range(CH)] + [nD + k for k in range(CH)] + [nO] + [nA + n for n in range(D // C)] + [0]

        def finisher(i):
            def store(total):
                if i == 0:
                    r_out[...] = total
                elif i < nO:
                    cols = pl.ds((i - nA) * C, C)
                    q_out[:, cols], k_out[:, cols], v_out[:, cols] = total[:, :C], total[:, C:2 * C], total[:, 2 * C:]
                elif i == nO:
                    o_out[...] = total
                elif i < nD:
                    up_out[:, pl.ds((i - nU) * D, D)] = total
                else:
                    down_out[i - nD] = total
            return store

        for j, i in enumerate(order):
            piece, cols = pieces[i]
            scatters.append(Scatter(place, piece, cols, j, (rd, ry, rx, rx2, ry2, rz), rs_send.at[j], rs_recv.at[j], credit, finisher(i)))

    def gather_tick(t):
        if not comm:
            return
        for k in range(4):
            i = 2 + t - (k - 1)
            if (2 < i if k == 0 else 2 <= i) and i < last:
                gathers[i].step(k)

    starts = list(range(2 * CH + 1)) + [2 * CH + 1, 2 * CH + 3, 2 * CH + 6, 2 * CH + 7]

    def scatter_tick(t):
        if not comm:
            return
        for k in range(5):
            for j in range(last):
                if starts[j] + k == t:
                    scatters[j].step(k, last)

    if comm:
        place.barrier()
        me = (place.c, place.z, place.y, place.x)
        GR[me] = r_in[...]
        GA[(0, *me)] = jnp.concatenate([q_in[:, 0:C], k_in[:, 0:C], v_in[:, 0:C]], axis=1)
        gathers[0].step(0)
        gathers[1].step(0)
        for n in range(1, D // C):
            cols = pl.ds(n * C, C)
            GA[(n, *me)] = jnp.concatenate([q_in[:, cols], k_in[:, cols], v_in[:, cols]], axis=1)
        GO[me] = o_in[...]
        for k in range(CH):
            GU[(k, *me)] = up_in[:, pl.ds(k * D, D)]
            GD[(*me, k)] = down_in[k]
    else:
        GRh, GAh, GOh, GUh, GDh = rest[:5]
        sems = rest[10]
        loads = [pltpu.make_async_copy(src, dst, sems.at[i]) for i, (src, dst) in enumerate(zip((GRh, GAh, GOh, GUh, GDh), (GR, GA, GO, GU, GD)))]
        for copy in loads:
            copy.start()
        for copy in loads:
            copy.wait()
    pickA = act_ref.at[:, 0:2 * T]
    pickA[...] = jnp.where(iota((NB, 2 * T), 0) == idx_ref[0:1, :], 1.0, 0.0).astype(BF)
    pick_ref[...] = jnp.where(iota((NB, 2 * T), 0) == idx_ref[1:2, :], 1.0, 0.0).astype(BF)
    flip_ref[...] = jnp.where(iota((B, B), 0) + iota((B, B), 1) == B - 1, 1.0, 0.0).astype(BF)
    select_ref[...] = jnp.where(iota((C // CH, C), 0) == iota((C // CH, C), 1) // CH, 1.0, 0.0).astype(BF)
    mask_ref[...] = jnp.where(iota((8, T), 1) < length, 0.0, -1e30)
    small_ref[...] = jnp.zeros_like(small_ref)
    grel_ref[...] = jnp.zeros_like(grel_ref)
    if comm:
        gathers[0].step(1)
        gathers[2].step(0)
        gathers[1].step(1)
        gathers[0].step(2)
        gathers[1].step(2)
        gathers[0].step(3)
        gathers[1].step(3)
        gathers[0].step(4)
    cols_ref[...] = matrix(GR[(*whole, slice(None), pl.ds(NB, 128))].astype(F32))
    rows_ref[...] = cols_ref[...].T[0:16]

    @pl.loop(0, FF // C)
    def _(t):
        m = C // CH
        spread = tn(cols_ref[tile(t, m), :].astype(BF), select_ref[...])
        own = iota((128, C), 0) == 9 + iota((128, C), 1) % CH
        bup_ref[0:1, tile(t, C)] = column_sum(jnp.where(own, spread, 0.0))

    if comm:
        gathers[1].step(4)

    @pl.loop(0, D // C)
    def _(n):
        for m in range(1, D // C):
            if comm:
                @pl.when(n == m)
                def _():
                    gathers[nA + m].step(4)
        cols = tile(n, C)
        weight = lambda i: matrix(GA[(n, *whole, slice(None), pl.ds(i * C, C))])
        relT = matrix(GR[(*whole, slice(None), pl.ds(0, NB))])
        wq, wk, wv = weight(0), weight(1), weight(2)
        q_ref[:, cols] = (nn(x_ref[...], wq) + rows_ref[0:1, cols]).astype(BF)
        k = (nn(x_ref[...], wk) + rows_ref[1:2, cols]).astype(BF)
        v = (nn(x_ref[...], wv) + rows_ref[2:3, cols]).astype(BF)
        k_ref[:, cols] = k
        v_ref[:, cols] = v
        for src, dst in ((k, kf_ref), (v, vf_ref)):
            dst[0:B, cols] = nn(flip_ref[...], src[B:T]).astype(BF)
            dst[B:T, cols] = nn(flip_ref[...], src[0:B]).astype(BF)
        rk = (tn(wk, relT) + cols_ref[cols, 1:2]).astype(BF)
        rq = (tn(wq, relT) + cols_ref[cols, 0:1]).astype(BF)
        kprT_ref[cols, :] = nn(rk, act_ref[:, 0:2 * T]).astype(BF)
        kpsT_ref[cols, :] = nn(rk, pick_ref[...]).astype(BF)
        qpsT_ref[cols, :] = nn(rq, pick_ref[...]).astype(BF)
        for m in range(D // C):
            if comm:
                @pl.when(n == m)
                def _():
                    gather_tick(3 * m)

        @pl.loop(0, 2)
        def _(i):
            pair_forward(2 * n + i, q_ref, k_ref, v_ref, kprT_ref, qpsT_ref, mask_ref, flip_ref, ctx_ref, pT_ref, scale)
            for m in range(2 * D // C):
                if comm:
                    @pl.when(2 * n + i == m)
                    def _():
                        gather_tick(3 * (m // 2) + 1 + m % 2)

    if comm:
        gathers[nO].step(4)
    second_ref = gtok_ref

    @pl.loop(0, D // C)
    def _(n):
        cols = tile(n, C)
        w = matrix(GO[(*whole, slice(None), cols)])
        second_ref[:, cols] = x_ref[:, cols].astype(F32) + (nn(ctx_ref[...], w) + rows_ref[3:4, cols])

    gather_tick(9)

    @pl.loop(0, T // R)
    def _(r):
        rs = tile(r, R)
        n1, inv1 = norm_rows(second_ref[rs, :])
        n1_ref[rs, :] = n1
        inv1_ref[rs, :] = jnp.broadcast_to(inv1, (R, 128))
        nb_ref[rs, :] = (n1 * row(4) + row(5)).astype(BF)

    gather_tick(10)

    @pl.loop(0, CH)
    def _(k):
        for m in range(CH):
            if comm:
                @pl.when(k == m)
                def _():
                    gathers[nU + m].step(4)
                    if m > 0:
                        gather_tick(10 + m)

        @pl.loop(0, D // C)
        def _(j):
            w = matrix(GU[(k, *whole, slice(None), tile(j, C))])
            cols = tile(k * (D // C) + j, C)
            up = nn(nb_ref[...], w) + bup_ref[0:1, cols]
            phi, e = normal_cdf_pair(up)
            act_ref[:, cols] = (up * phi).astype(BF)
            gp_ref[:, cols] = (phi + up * e * 0.3989422804014327).astype(BF)

    if comm:
        gather_tick(14)
        for k in range(CH):
            gathers[nD + k].step(4)

    @pl.loop(0, D // C)
    def _(n):
        cols = tile(n, C)
        w = matrix(GD[(*whole, slice(None), slice(None), cols)])
        normed = n1_ref[:, cols] * rows_ref[4:5, cols] + rows_ref[5:6, cols]
        second_ref[:, cols] = normed + (nn(act_ref[...], w) + rows_ref[6:7, cols])

    @pl.loop(0, T // R)
    def _(r):
        rs = tile(r, R)
        live = jnp.where(iota((R, 1), 0) + r * R < length, 1.0, 0.0)
        n2, inv2 = norm_rows(second_ref[rs, :])
        out_ref[rs, :] = ((n2 * row(7) + row(8)) * live).astype(BF)
        start = cot_ref[rs, :].astype(F32) * live
        g = norm_back(start * row(7), n2, inv2)
        second_ref[rs, :] = g
        gd = g.astype(BF)
        gd_ref[rs, :] = gd
        small_ref[6:7, :] += column_sum(gd.astype(F32))
        small_ref[7:8, :] += column_sum(start * n2)
        small_ref[8:9, :] += column_sum(start)

    half = GRID[1] // 2

    @pl.loop(0, CH)
    def _(k):
        units = tile(k, D)
        c, z0 = lax.div(k, 2), half * lax.rem(k, 2)
        w = matrix(GD[c, pl.ds(z0, half)])
        gu = (nt(gd_ref[...], w) * gp_ref[:, units].astype(F32)).astype(BF)
        gp_ref[:, units] = gu
        gbup_ref[0:1, units] = column_sum(gu.astype(F32))

        @pl.loop(0, half)
        def _(i):
            at = pl.ds(pl.multiple_of(k * D + i * (D // 2), D // 2), D // 2)
            g = tn(act_ref[:, at], gd_ref[...])
            GD[c, z0 + i] = g.reshape(*GD.shape[2:]).astype(BF)

        second_ref[...] += nt(gu, matrix(GU[k]))

        @pl.loop(0, GRID[0])
        def _(i):
            g = tn(nb_ref[:, tile(i, D // 2)], gp_ref[:, units])
            GU[k, i] = g.reshape(*GU.shape[2:]).astype(BF)

        for m in range(CH):
            if comm:
                @pl.when(k == m)
                def _():
                    scatter_tick(m)

    scatter_tick(CH)

    @pl.loop(0, T // R)
    def _(r):
        rs = tile(r, R)
        g = second_ref[rs, :]
        n1 = n1_ref[rs, :]
        gm = norm_back(g * row(4), n1, inv1_ref[rs, 0:1])
        second_ref[rs, :] = gm
        ga = gm.astype(BF)
        gd_ref[rs, :] = ga
        small_ref[3:4, :] += column_sum(ga.astype(F32))
        small_ref[4:5, :] += column_sum(g * n1)
        small_ref[5:6, :] += column_sum(g)

    @pl.loop(0, GRID[0])
    def _(i):
        at = tile(i, D // 2)
        dcT_ref[at, :] = nt(matrix(GO[i]), gd_ref[...]).astype(BF)
        g = tn(ctx_ref[:, at], gd_ref[...])
        GO[i] = g.reshape(*GO.shape[1:]).astype(BF)

    scatter_tick(CH + 1)

    grkT, grqT = kprT_ref.at[:, 0:NB], kprT_ref.at[:, NB:2 * NB]

    @pl.loop(0, D // C)
    def _(n):
        cols = tile(n, C)

        @pl.loop(0, 2)
        def _(i):
            pair_backward(2 * n + i, q_ref, kf_ref, vf_ref, kpsT_ref, qpsT_ref, dcT_ref, pT_ref, scale)
            for m in range(2 * D // C):
                if comm:
                    @pl.when(2 * n + i == m)
                    def _():
                        scatter_tick(CH + 2 + 3 * (m // 2) + m % 2)

        dq = q_ref[:, cols]
        for src, dst in ((kf_ref, k_ref), (vf_ref, v_ref)):
            dst[0:B, cols] = nn(flip_ref[...], src[B:T, cols]).astype(BF)
            dst[B:T, cols] = nn(flip_ref[...], src[0:B, cols]).astype(BF)
        dk, dv = k_ref[:, cols], v_ref[:, cols]
        grk = nt(kpsT_ref[cols, :], pick_ref[...]).astype(BF)
        grq = nt(qpsT_ref[cols, :], pick_ref[...]).astype(BF)
        weight = lambda i: matrix(GA[(n, *whole, slice(None), pl.ds(i * C, C))])
        wq, wk = weight(0), weight(1)
        gtok_ref[...] += nt(dq, wq) + nt(dk, wk) + nt(dv, weight(2))
        grel_ref[...] += nn(wk, grk) + nn(wq, grq)
        ones_t, ones_b = jnp.ones((8, T), BF), jnp.ones((8, NB), BF)
        small_ref[0:1, cols] = (nn(ones_t, dq) + nt(ones_b, grq))[0:1]
        small_ref[1:2, cols] = (nn(ones_t, dk) + nt(ones_b, grk))[0:1]
        small_ref[2:3, cols] = nn(ones_t, dv)[0:1]

        @pl.loop(0, GRID[0])
        def _(i):
            at = tile(i, D // 2)
            xt = x_ref[:, at]
            relT = matrix(GR[(i, *whole[1:], slice(None), pl.ds(0, NB))])
            for s, g in enumerate((tn(xt, dq) + nt(relT, grq), tn(xt, dk) + nt(relT, grk), tn(xt, dv))):
                GA[(n, i, *whole[1:], slice(None), pl.ds(s * C, C))] = g.reshape(*GA.shape[2:6], C).astype(BF)

        for m in range(D // C):
            if comm:
                @pl.when(n == m)
                def _():
                    scatter_tick(CH + 2 + 3 * m + 2)

    small_ref[9:16, :] = jnp.zeros((7, D), F32)
    cols_ref[...] = jnp.concatenate([small_ref[...], jnp.zeros((112, D), F32)], axis=0).T

    @pl.loop(0, FF // C)
    def _(t):
        m = C // CH
        own = iota((128, C), 0) == 9 + iota((128, C), 1) % CH
        g = jnp.where(own, gbup_ref[0:1, tile(t, C)], 0.0).astype(BF)
        cols_ref[tile(t, m), :] += nt(select_ref[...], g)

    GR[(*whole, slice(None), pl.ds(0, NB))] = grel_ref[...].reshape(*GR.shape[:5], NB).astype(BF)
    GR[(*whole, slice(None), pl.ds(NB, 128))] = cols_ref[...].reshape(*GR.shape[:5], 128).astype(BF)
    if comm:
        for t in range(starts[-1], starts[-1] + 5):
            scatter_tick(t)
    else:
        GRh, GAh, GOh, GUh, GDh = rest[5:10]
        stores = [pltpu.make_async_copy(src, dst, sems.at[i]) for i, (dst, src) in enumerate(zip((GRh, GAh, GOh, GUh, GDh), (GR, GA, GO, GU, GD)))]
        for copy in stores:
            copy.start()
        for copy in stores:
            copy.wait()


def layer_scratch(T, D, FF, NB, heads):
    V = pltpu.VMEM
    n, ch = D // 256, FF // D
    rows = D // BLOCKS
    td = V((T, D), BF)
    return [
        V((*GRID, rows, NB + 128), BF), V((n, *GRID, rows, D), BF), V((*GRID, rows, D), BF), V((ch, *GRID, rows, D), BF), V((*GRID, ch, rows, D), BF),
        td, td, td, td, td, V((D, 2 * T), BF), V((D, 2 * T), BF), V((D, 2 * T), BF), V((NB, 2 * T), BF), V((heads, T, T), BF),
        td, V((D, T), BF), V((T, D), F32), V((T, 128), F32), td, td, V((T, FF), BF), V((T, FF), BF),
        V((D, NB), F32), V((D, 128), F32), V((16, D), F32), V((8, FF), F32), V((16, D), F32), V((8, FF), F32), V((8, T), F32),
        V((T // 2, T // 2), BF), V((256 // ch, 256), BF),
    ]


def call_layer(comm, length, idx, x, cot, parts):
    T, D = x.shape
    S = jax.ShapeDtypeStruct
    VM, HBM = pl.BlockSpec(memory_space=pltpu.VMEM), pl.BlockSpec(memory_space=pl.ANY)
    heads = D // HEAD
    if comm:
        rshard, wq, wk, wv, wo, wup, wdown = parts
        rows, FF = wup.shape
        NB = rshard.shape[1] - 128
        outs = [S((T, D), BF), S((T, D), F32), S(rshard.shape, F32)] + [S((rows, D), F32)] * 4 + [S(wup.shape, F32), S(wdown.shape, F32)]
        in_specs = [pl.BlockSpec(memory_space=pltpu.SMEM)] + [VM] * (3 + len(parts))
        out_specs = [VM] * len(outs)
        nz, last = GRID[1], 2 + D // 256 + 2 * (FF // D)
        V = pltpu.VMEM
        sems = [pltpu.SemaphoreType.DMA((last, 8))] * 4 + [pltpu.SemaphoreType.REGULAR]
        extra = [V((SLOTS, nz, 2, 2, rows, D), BF), V((last, nz, 2, rows, CUT), BF), V((last, nz, 2, rows, D - CUT), BF),
                 V((last, nz, rows, CUT), BF), V((last, nz, rows, D - CUT), BF), V((last, nz - 1, rows, D), BF)] + sems

        def kernel(*refs):
            layer_kernel(True, *refs)
    else:
        gr, ga, go, gu, gd = parts
        FF, NB = gu.shape[0] * D, gr.shape[-1] - 128
        outs = [S((T, D), BF), S((T, D), F32)] + [S(p.shape, p.dtype) for p in parts]
        in_specs = [pl.BlockSpec(memory_space=pltpu.SMEM)] + [VM] * 3 + [HBM] * 5
        out_specs = [VM] * 2 + [HBM] * 5
        extra = [pltpu.SemaphoreType.DMA((5,))]

        def kernel(*refs):
            ins, given, results, stored, scratch = refs[:4], refs[4:9], refs[9:11], refs[11:16], refs[16:]
            none = [None] * 7
            layer_kernel(False, *ins, *none, *results, *none, *scratch[:-1], *given, *stored, scratch[-1])

    return pl.pallas_call(
        kernel,
        out_shape=outs,
        in_specs=in_specs,
        out_specs=out_specs,
        scratch_shapes=layer_scratch(T, D, FF, NB, heads) + extra,
        compiler_params=pltpu.CompilerParams(
            vmem_limit_bytes=VMEM_LIMIT,
            **(dict(collective_id=0, has_side_effects=True) if comm else {}),
        ),
    )(length, idx, x, cot, *parts)


VMEM_LIMIT = 63 * 2**20


def body(comm, tokens, lengths, rel_index, w_query, b_query, w_key, b_key, w_value, b_value, w_out, b_out, rel_table,
         gain_one, shift_one, w_up, b_up, w_down, b_down, gain_two, shift_two, cotangent):
    rows, D = w_query.shape
    T = tokens.shape[0]
    NB = rel_table.shape[0]
    FF = w_up.shape[1]
    ch, n = FF // D, D // 256
    vectors = (b_query, b_key, b_value, b_out, gain_one, shift_one, b_down, gain_two, shift_two)
    pack = jnp.concatenate([rel_table.T, jnp.stack(vectors, axis=1), b_up.reshape(rows, ch), jnp.zeros((rows, 128 - 9 - ch), BF)], axis=1)
    shifted = jnp.concatenate([rel_index[1:], jnp.full((1,), -1, jnp.int32)])
    idx = jnp.concatenate([rel_index[None, ::-1], shifted[None, :], jnp.zeros((6, 2 * T), jnp.int32)])
    if comm:
        out, gtok, gr, gq, gk, gv, go, gup, gdown = call_layer(
            True, lengths, idx, tokens, cotangent, (pack, w_query, w_key, w_value, w_out, w_up, w_down.reshape(ch, rows, D)))
        gdown = gdown.reshape(w_down.shape)
    else:
        gather = lambda w: lax.all_gather(w, AXES, axis=0, tiled=True)
        r = D // BLOCKS
        attend = gather(jnp.concatenate([pack, w_out, w_query, w_key, w_value], axis=1))
        gr, go = attend[:, :NB + 128].reshape(*GRID, r, NB + 128), attend[:, NB + 128:NB + 128 + D].reshape(*GRID, r, D)
        qkv = attend[:, NB + 128 + D:].reshape(*GRID, r, 3, n, 256)
        ga = qkv.transpose(6, 0, 1, 2, 3, 4, 5, 7).reshape(n, *GRID, r, D)
        gu = gather(w_up).reshape(*GRID, r, ch, D).transpose(5, 0, 1, 2, 3, 4, 6)
        gd = gather(w_down).reshape(*GRID, ch, r, D)
        out, gtok, gr, ga, go, gu, gd = call_layer(False, lengths, idx, tokens, cotangent, (gr, ga, go, gu, gd))
        scatter = lambda g: lax.psum_scatter(g.astype(F32), AXES, scatter_dimension=0, tiled=True)
        ga = ga.reshape(n, *GRID, r, 3, 256).transpose(1, 2, 3, 4, 5, 6, 0, 7).reshape(D, 3 * D)
        gup = scatter(gu.transpose(1, 2, 3, 4, 5, 0, 6).reshape(D, FF))
        gdown = scatter(gd.reshape(FF, D))
        attend = scatter(jnp.concatenate([gr.reshape(D, NB + 128), go.reshape(D, D), ga], axis=1))
        gr = attend[:, :NB + 128]
        go, gq, gk, gv = (attend[:, NB + 128 + i * D:NB + 128 + (i + 1) * D] for i in range(4))
    grel = gr[:, :NB].T
    vec = lambda i: gr[:, NB + i]
    return (out, gtok, gq, vec(0), gk, vec(1), gv, vec(2), go, vec(3), grel, vec(4), vec(5),
            gup, gr[:, NB + 9:NB + 9 + ch].reshape(rows * ch), gdown, vec(6), vec(7), vec(8))


def solution(mesh):
    rows, vec = P(AXES, None), P(AXES)
    comm = mesh.shape["dp"] == GRID[0] and mesh.shape["fsdp"] == GRID[1] * GRID[2] * GRID[3]

    def step(*args):
        return body(comm, *args)

    return jax.shard_map(
        step,
        mesh=mesh,
        in_specs=(rows, vec, P(), rows, vec, rows, vec, rows, vec, rows, vec, P(None, AXES), vec, vec, rows, vec, rows, vec, vec, vec, rows),
        out_specs=(rows, rows, rows, vec, rows, vec, rows, vec, rows, vec, P(None, AXES), vec, vec, rows, vec, rows, vec, vec, vec),
        check_vma=False,
    )
```

time: 828 us -> 220 us (0.27)
  waiting for transfers between devices: 630 us -> 0 us
  Pallas kernels: 134 us -> 195 us
  local copies, waits for them, and re-layouts: 45.8 us -> 22.6 us
  between operations: 14.9 us -> 1.38 us
    reduce_scatter x2 -> x0, waiting for transfers between devices: 276 us -> none  [the longest x1 142 us: body(): gwdown = lax.psum_scatter(gwdown, AXES, scatter_dimension=0, tiled=True)]
    unnamed x7 -> x0, waiting for transfers between devices: 220 us -> none
    all_gather x3 -> x0, waiting for transfers between devices: 134 us -> none  [the longest x1 65.3 us: body(): wdown = lax.all_gather(w_down, AXES, axis=0, tiled=True)]
    pallas_call x5 -> x1, Pallas kernels: 134 us -> 195 us  [call_layer(): pl.pallas_call(kernel, out_shape=outs, in_specs=in_specs, out_specs=out_s...]
    concatenate x4 -> x2, local copies, waits for them, and re-layouts: 13.1 us -> 1.52 us  [the longest x1 1.45 us: body(): jnp.concatenate([rel_table.T, jnp.stack(vectors, axis=1), b_up.reshape(ro...]
    slice x10 -> x3, local copies, waits for them, and re-layouts: 14.7 us -> 3.65 us  [the longest x1 2.12 us: body(): vec = lambda i: gr[:, NB + i]]
  transfers between devices with their start and end apart: 6 -> 0, of which waited for: 6 -> 0; matrix products, arithmetic and copies ran while one was open for 3% -> 0% of each run, Pallas kernels for 6% -> 0%
where the time goes in v2:
time: 220 us
  Pallas kernels  195 us (89%)
  local copies, waits for them, and re-layouts  22.6 us (10%)
    pallas_call x1, Pallas kernels, call_layer(): pl.pallas_call(kernel, out_shape=outs, in_specs=in_specs, out_specs=out_s...  195 us
    unnamed x22, local copies, waits for them, and re-layouts  7.19 us
    another operation x9, local copies, waits for them, and re-layouts, body(): jnp.stack(vectors, axis=1)  6.73 us

profile of v2, /device:TPU:0, one launch (start us, length us, event | category | flops | bytes accessed | tf_op | source)
XLA Modules:
  0.0 219.9 jit_solution(8226161208791207845)
XLA Ops:
  1.4 0.8 slice.36
  2.2 0.8 rev.3
  3.0 0.7 copy.49
  3.7 0.7 copy.50
  4.5 0.7 copy.51
  5.2 0.7 copy.52
  6.0 0.7 copy.53
  6.7 0.7 copy.54
  7.5 0.7 reshape.50
  8.2 0.8 copy.55
  9.0 0.7 copy.56
  9.7 0.7 copy.57
  10.5 1.4 concatenate.11.refs_4_
  11.9 0.7 add_add_fusion.refs_1_
  12.6 195.1 %shard_map.348 = (bf16[512,768]{1,0:T(8,128)(2,1)}, f32[512,768]{1,0:T(8,128)}, f32[24,640]{1,0:T(8,128)}, f32[24,768]{1,0:T(8,128)}, f32[24,768]{1,0:T(8,128)},...) custom-call(s32[1]{0:T(128)S(6)} %copy.66.refs_0_, ...), custom_call_target="tpu_custom_call" | custom-call | tf_op jit(solution)/shard_map/pallas_call | solution.py:687
  207.7 2.1 slice_reduce_fusion
  209.9 0.8 slice.44
  210.6 1.4 slice_bitcast_fusion
  212.7 2.1 copy.67
  214.8 1.1 copy.68
  215.9 0.6 copy.69
  217.2 0.6 copy.71
  218.5 0.7 copy.73
  219.2 0.7 copy.74
  (21 shorter events, 2.1 us)
Async XLA Ops:
  207.7 7.0 %copy-start = (f32[512,768]{1,0:T(8,128)S(1)}, f32[512,768]{1,0:T(8,128)}, u32[]{:S(2)}) copy-start(f32[512,768]{1,0:T(8,128)} %get-tuple-element.66) | copy-start | bytes 4718596
  214.7 1.2 copy-start.6
  214.7 1.8 copy-start.5
  214.7 2.5 %copy-start.4 = (f32[24,768]{1,0:T(8,128)S(1)}, f32[24,768]{1,0:T(8,128)}, u32[]{:S(2)}) copy-start(f32[24,768]{1,0:T(8,128)} %get-tuple-element.71) | copy-start | bytes 221188
  214.7 3.1 %copy-start.3 = (f32[24,768]{1,0:T(8,128)S(1)}, f32[24,768]{1,0:T(8,128)}, u32[]{:S(2)}) copy-start(f32[24,768]{1,0:T(8,128)} %get-tuple-element.73) | copy-start | bytes 221188
  214.7 3.7 %copy-start.2 = (f32[24,3072]{1,0:T(8,128)S(1)}, f32[24,3072]{1,0:T(8,128)}, u32[]{:S(2)}) copy-start(f32[24,3072]{1,0:T(8,128)} %get-tuple-element.78) | copy-start | bytes 884740
  214.8 4.4 %copy-start.1 = (f32[4,24,768]{2,1,0:T(8,128)S(1)}, f32[4,24,768]{2,1,0:T(8,128)}, u32[]{:S(2)}) copy-start(f32[4,24,768]{2,1,0:T(8,128)} %get-tuple-element.36) | copy-start | bytes 884740

commit v3 on v2

v3 whole, which is shorter than its diff:
```python
import jax
import jax.numpy as jnp
from jax import lax
from jax.experimental import pallas as pl
from jax.experimental.pallas import tpu as pltpu
from jax.sharding import PartitionSpec as P

BF = jnp.bfloat16
F32 = jnp.float32
EPS = 1e-6
HEAD = 64
AXES = ("dp", "fsdp")
MESH = pl.DeviceIdType.MESH
LOG2E = 1.4426950408889634
GRID = (2, 4, 2, 2)
BLOCKS = 32
SLOTS = 3


def dot(left, right, dims):
    return lax.dot_general(left, right, ((dims[:1], dims[1:]), ((), ())), preferred_element_type=F32)


def nn(left, right):
    return dot(left, right, (1, 0))


def nt(left, right):
    return dot(left, right, (1, 1))


def tn(left, right):
    return dot(left, right, (0, 0))


def iota(shape, axis):
    return lax.broadcasted_iota(jnp.int32, shape, axis)


def column_sum(x):
    return jnp.sum(x, axis=0, keepdims=True)


def row_mean(x):
    return jnp.sum(x, axis=1, keepdims=True) * (1.0 / x.shape[1])


def norm_rows(x):
    centred = x - row_mean(x)
    inv = lax.rsqrt(row_mean(centred * centred) + EPS)
    return centred * inv, inv


def norm_back(g, n, inv):
    return (g - row_mean(g) - n * row_mean(g * n)) * inv


def normal_cdf_pair(x):
    a = jnp.abs(x)
    e = jnp.exp2(x * x * (-0.5 * LOG2E))
    t = 1.0 / (1.0 + (0.3275911 * 0.7071067811865476) * a)
    poly = ((((1.061405429 * t - 1.453152027) * t + 1.421413741) * t - 0.284496736) * t + 0.254829592) * t
    tail = 0.5 * poly * e
    return jnp.where(x < 0, tail, 1.0 - tail), e


def tile(n, size):
    return pl.ds(pl.multiple_of(n * size, size), size)


def matrix(value):
    rows = 1
    for size in value.shape[:-1]:
        rows *= size
    return value.reshape(rows, value.shape[-1])


def pair_forward(pair, q_ref, k_ref, v_ref, kprT_ref, qpsT_ref, mask_ref, flip_ref, ctx_ref, pT_ref, scale):
    T = q_ref.shape[0]
    B = T // 2
    lanes = tile(pair, 128)
    outs = []
    for hh in range(2):
        keep = iota((1, 128), 1) // HEAD == hh
        qh = jnp.where(keep, q_ref[:, lanes], 0)
        kh = jnp.where(keep, k_ref[:, lanes], 0)
        content = nt(qh, k_ref[:, lanes])
        to, frm = [], []
        for b in range(2):
            u0 = B * (1 - b)
            t = nn(qh[b * B:(b + 1) * B], kprT_ref[lanes, u0:u0 + 3 * B])
            to.append(pltpu.roll(t, 2 * B + 1, 1, stride=1, stride_axis=0)[:, :T])
            f = nn(kh[b * B:(b + 1) * B], qpsT_ref[lanes, u0:u0 + 3 * B])
            frm.append(pltpu.roll(f, 2 * B + 1, 1, stride=1, stride_axis=0)[:, :T].T)
        s = content + jnp.concatenate(to, axis=0) + jnp.concatenate(frm, axis=1) + mask_ref[0:1, :]
        top = jnp.max(s, axis=1, keepdims=True)
        e = jnp.exp2((s - top) * (scale * LOG2E))
        p = (e * (1.0 / jnp.sum(e, axis=1, keepdims=True))).astype(BF)
        outs.append(nn(p, v_ref[:, lanes]))
        pT_ref[2 * pair + hh, 0:B, :] = nt(flip_ref[...], p[:, B:T]).astype(BF)
        pT_ref[2 * pair + hh, B:T, :] = nt(flip_ref[...], p[:, 0:B]).astype(BF)
    ctx_ref[:, lanes] = jnp.where(iota((1, 128), 1) < HEAD, outs[0], outs[1]).astype(BF)


def pair_backward(pair, q_ref, kf_ref, vf_ref, kpsT_ref, qpsT_ref, dcT_ref, pT_ref, scale):
    T = q_ref.shape[0]
    B = T // 2
    lanes = tile(pair, 128)
    low = iota((1, 128), 1) < HEAD
    q, kf, dcT = q_ref[:, lanes], kf_ref[:, lanes], dcT_ref[lanes, :]
    dqs, dks, dvs, gks, gqs = [], [], [], [], []
    for hh in range(2):
        vh = jnp.where(iota((1, 128), 1) // HEAD == hh, vf_ref[:, lanes], 0)
        pT = pT_ref[2 * pair + hh]
        dpT = nn(vh, dcT)
        wide = pT.astype(F32)
        prod = wide * dpT
        inner = column_sum(prod) / column_sum(wide)
        dsT = (prod - wide * inner).astype(BF)
        ds = dsT.T
        zero = jnp.zeros((B, B), BF)
        dk, dq, gq, gk = [], [], [], []
        for b in range(2):
            rows, span = slice(b * B, (b + 1) * B), slice(b * B, b * B + 3 * B)
            gf = pltpu.roll(jnp.concatenate([dsT[rows], zero], axis=1), 0, 1, stride=1, stride_axis=0)
            dk.append(nn(dsT[rows], q) + nt(gf, qpsT_ref[lanes, span]))
            gq.append(tn(kf[rows], gf)[hh * HEAD:(hh + 1) * HEAD])
            gt = pltpu.roll(jnp.concatenate([ds[rows], zero], axis=1), 0, 1, stride=1, stride_axis=0)
            dq.append(nn(ds[rows], kf) + nt(gt, kpsT_ref[lanes, span]))
            gk.append(tn(q[rows], gt)[hh * HEAD:(hh + 1) * HEAD])
        dks.append(jnp.concatenate(dk, axis=0))
        dqs.append(jnp.concatenate(dq, axis=0))
        dvs.append(nt(pT, dcT))
        gqs.append(gq)
        gks.append(gk)
    for ref, pieces in ((qpsT_ref, gqs), (kpsT_ref, gks)):
        for hh in range(2):
            g = pieces[hh]
            rows = pl.ds(pl.multiple_of(pair * 128 + HEAD * hh, HEAD), HEAD)
            ref[rows, 0:B] = (scale * g[0][:, 0:B]).astype(BF)
            ref[rows, B:3 * B] = (scale * (g[0][:, B:] + g[1][:, 0:2 * B])).astype(BF)
            ref[rows, 3 * B:] = (scale * g[1][:, 2 * B:]).astype(BF)
    q_ref[:, lanes] = (scale * jnp.where(low, dqs[0], dqs[1])).astype(BF)
    kf_ref[:, lanes] = (scale * jnp.where(low, dks[0], dks[1])).astype(BF)
    vf_ref[:, lanes] = jnp.where(low, dvs[0], dvs[1]).astype(BF)


class Place:
    def __init__(self):
        self.nz = GRID[1]
        self.c = lax.axis_index("dp")
        f = lax.axis_index("fsdp")
        self.x = lax.rem(f, 2)
        self.y = lax.rem(lax.div(f, 2), 2)
        self.z = lax.div(f, 4)
        self.nx = 1 - self.x
        self.ny = 1 - self.y

    def at(self, c=None, z=None, y=None, x=None):
        c = self.c if c is None else c
        z = self.z if z is None else z
        y = self.y if y is None else y
        x = self.x if x is None else x
        return (c, (z * 2 + y) * 2 + x)

    def zs(self):
        return [lax.rem(self.z + d, self.nz) for d in range(1, self.nz)]

    def barrier(self):
        sem = pltpu.get_barrier_semaphore()
        peers = [self.at(z=z) for z in self.zs()] + [self.at(x=self.nx), self.at(y=self.ny), self.at(c=1 - self.c)]
        for peer in peers:
            pl.semaphore_signal(sem, inc=1, device_id=peer, device_id_type=MESH)
        pl.semaphore_wait(sem, len(peers))


def remote(src, dst, send, recv, to):
    return pltpu.make_async_remote_copy(src_ref=src, dst_ref=dst, send_sem=send, recv_sem=recv, device_id=to, device_id_type=MESH)


class Part:
    def __init__(self, place, piece, lo, cols):
        cut = cols // 256 * 128
        self.p, self.piece, self.lo, self.cols, self.cut = place, piece, lo, cols, cut
        self.all, self.h1, self.h2 = pl.ds(lo, cols), pl.ds(lo, cut), pl.ds(lo + cut, cols - cut)


class Gather(Part):
    def __init__(self, place, piece, lo, cols, early, send, recv):
        super().__init__(place, piece, lo, cols)
        self.early, self.send, self.recv = early, send, recv

    def copies(self, k):
        p, g, every = self.p, self.piece, slice(None)
        if k == 0 and self.early:
            return [(g(p.c, p.z, p.y, p.x, self.h1), p.at(x=p.nx)), (g(p.c, p.z, p.y, p.x, self.h2), p.at(y=p.ny))]
        if k == 1 and self.early:
            return ([(g(p.c, p.z, p.y, every, self.h1), p.at(z=z)) for z in p.zs()]
                    + [(g(p.c, p.z, every, p.x, self.h2), p.at(z=z)) for z in p.zs()])
        if k == 0:
            return [(g(p.c, p.z, p.y, p.x, self.all), p.at(z=z)) for z in p.zs()]
        if k == 1:
            return [(g(p.c, every, p.y, p.x, self.h1), p.at(x=p.nx)), (g(p.c, every, p.y, p.x, self.h2), p.at(y=p.ny))]
        if k == 2:
            return [(g(p.c, every, p.y, every, self.h1), p.at(y=p.ny)), (g(p.c, every, every, p.x, self.h2), p.at(x=p.nx))]
        return [(g(p.c, every, every, every, self.all), p.at(c=1 - p.c))]

    def settle(self, k):
        p, g, every = self.p, self.piece, slice(None)
        three = pl.ds(0, p.nz - 1)
        if k == 0:
            ref = g(p.c, p.z, p.y, p.x, self.all) if self.early else g(p.c, three, p.y, p.x, self.all)
        elif k == 1:
            ref = g(p.c, three, p.y, every, self.all) if self.early else g(p.c, every, p.y, p.x, self.all)
        elif k == 2:
            ref = g(p.c, every, p.y, every, self.all)
        else:
            ref = g(p.c, every, every, every, self.all)
        copy = remote(ref, ref, self.send.at[0], self.recv.at[k], p.at(c=1 - p.c))
        copy.wait_recv()
        copy.wait_send()

    def step(self, k):
        if k > 0:
            self.settle(k - 1)
        if k < 4:
            for ref, to in self.copies(k):
                remote(ref, ref, self.send.at[0], self.recv.at[k], to).start()


def add_into(ref, *others):
    total = ref[...].astype(F32)
    for other in others:
        total = total + other[...].astype(F32)
    ref[...] = total.astype(BF)


class Scatter(Part):
    def __init__(self, place, piece, lo, cols, late, order, last, slots, buffers, send, recv, credit, finish):
        super().__init__(place, piece, lo, cols)
        self.late, self.order, self.last, self.send, self.recv, self.credit, self.finish = late, order, last, send, recv, credit, finish
        self.rd = slots.at[order % SLOTS, :, :, :, :, pl.ds(0, cols)]
        self.ry, self.rx, self.third, self.fourth = buffers[0], buffers[1], buffers[2:4], buffers[4:]

    def make(self, k):
        p, g, every = self.p, self.piece, slice(None)
        if k == 0:
            found = [(g(1 - p.c, every, every, every, self.all), self.rd, p.at(c=1 - p.c))]
        elif k == 1:
            found = [(g(p.c, every, p.ny, every, self.h1), self.ry, p.at(y=p.ny)),
                     (g(p.c, every, every, p.nx, self.h2), self.rx, p.at(x=p.nx))]
        elif self.late and k == 2:
            found = []
            for d, z in enumerate(p.zs()):
                found += [(g(p.c, z, p.y, every, self.h1), self.third[0].at[d], p.at(z=z)),
                          (g(p.c, z, every, p.x, self.h2), self.third[1].at[d], p.at(z=z))]
        elif self.late:
            found = [(g(p.c, p.z, p.y, p.nx, self.h1), self.fourth[0], p.at(x=p.nx)),
                     (g(p.c, p.z, p.ny, p.x, self.h2), self.fourth[1], p.at(y=p.ny))]
        elif k == 2:
            found = [(g(p.c, every, p.y, p.nx, self.h1), self.third[0], p.at(x=p.nx)),
                     (g(p.c, every, p.ny, p.x, self.h2), self.third[1], p.at(y=p.ny))]
        else:
            found = [(g(p.c, z, p.y, p.x, self.all), self.fourth[0].at[d], p.at(z=z)) for d, z in enumerate(p.zs())]
        return [remote(src, dst, self.send.at[0], self.recv.at[k], to) for src, dst, to in found]

    def settle(self, k):
        p, g, every = self.p, self.piece, slice(None)
        if k == 0:
            ref = self.rd
        elif k == 1:
            ref = g(p.c, every, p.y, every, self.all)
        elif k == 2:
            ref = g(p.c, pl.ds(0, p.nz - 1), p.y, every, self.all) if self.late else g(p.c, every, p.y, p.x, self.all)
        else:
            ref = g(p.c, p.z, p.y, p.x, self.all) if self.late else self.fourth[0]
        copy = remote(ref, ref, self.send.at[0], self.recv.at[k], p.at(c=1 - p.c))
        copy.wait_recv()
        copy.wait_send()

    def step(self, k):
        p, g, every = self.p, self.piece, slice(None)
        if k > 0:
            self.settle(k - 1)
        if k == 0 and self.order >= SLOTS:
            pl.semaphore_wait(self.credit, 1)
        if k == 1:
            @pl.loop(0, p.nz)
            def _(z):
                add_into(g(p.c, z, every, every, self.all), self.rd.at[z])
            if self.order + SLOTS < self.last:
                pl.semaphore_signal(self.credit, inc=1, device_id=p.at(c=1 - p.c), device_id_type=MESH)
        elif k == 2:
            @pl.loop(0, p.nz)
            def _(z):
                add_into(g(p.c, z, p.y, every, self.h1), self.ry.at[z])
                add_into(g(p.c, z, every, p.x, self.h2), self.rx.at[z])
        elif k == 3 and self.late:
            add_into(g(p.c, p.z, p.y, every, self.h1), *[self.third[0].at[d] for d in range(p.nz - 1)])
            add_into(g(p.c, p.z, every, p.x, self.h2), *[self.third[1].at[d] for d in range(p.nz - 1)])
        elif k == 3:
            add_into(g(p.c, every, p.y, p.x, self.h1), self.third[0])
            add_into(g(p.c, every, p.y, p.x, self.h2), self.third[1])
        elif k == 4 and self.late:
            self.finish(self.lo, g(p.c, p.z, p.y, p.x, self.h1)[...].astype(F32) + self.fourth[0][...].astype(F32))
            self.finish(self.lo + self.cut, g(p.c, p.z, p.y, p.x, self.h2)[...].astype(F32) + self.fourth[1][...].astype(F32))
        elif k == 4:
            total = g(p.c, p.z, p.y, p.x, self.all)[...].astype(F32)
            for d in range(p.nz - 1):
                total = total + self.fourth[0][d].astype(F32)
            self.finish(self.lo, total)
        if k < 4:
            for copy in self.make(k):
                copy.start()


def scatter_buffers(rows, cols, late):
    nz = GRID[1]
    h1 = cols // 256 * 128
    h2 = cols - h1
    shapes = [(nz, 2, rows, h1), (nz, 2, rows, h2)]
    shapes += [(nz - 1, 2, rows, h1), (nz - 1, 2, rows, h2), (rows, h1), (rows, h2)] if late else [(nz, rows, h1), (nz, rows, h2), (nz - 1, rows, cols)]
    return [pltpu.VMEM(shape, BF) for shape in shapes]


GATHERS = (
    (0, 0, 256, 0),
    (0, 256, 384, 0),
    (1, 0, 256, 0),
    (1, 256, 256, 0),
    (1, 512, 256, 0),
    (2, 0, 768, 0),
    (3, 0, 768, 0),
    (4, 0, 768, 0),
    (5, 0, 768, 1),
    (6, 0, 768, 0),
    (7, 0, 768, 0),
    (8, 0, 768, 1),
    (9, 0, 768, 0),
    (10, 0, 768, 0),
    (11, 0, 768, 1),
    (12, 0, 768, 1),
)
SCATTERS = (
    (5, 0, 768, 0),
    (6, 0, 768, 1),
    (7, 0, 768, 0),
    (8, 0, 768, 0),
    (9, 0, 768, 1),
    (10, 0, 768, 1),
    (11, 0, 768, 0),
    (12, 0, 768, 0),
    (4, 0, 768, 0),
    (1, 0, 768, 0),
    (2, 0, 768, 0),
    (0, 0, 256, 0),
    (0, 256, 384, 1),
    (3, 512, 256, 0),
    (3, 256, 256, 0),
    (3, 0, 256, 0),
)
TICKS = {
    "pre": ((0, 0, 0), (0, 1, 0), (0, 2, 0), (0, 3, 0), (0, 4, 0), (0, 5, 0), (0, 6, 0),),
    "before P0": ((0, 0, 1), (0, 1, 1), (0, 2, 1), (0, 7, 0), (0, 0, 2), (0, 1, 2), (0, 3, 1), (0, 2, 2), (0, 4, 1), (0, 0, 3), (0, 0, 4), (0, 1, 3), (0, 3, 2), (0, 2, 3), (0, 1, 4), (0, 4, 2), (0, 5, 1), (0, 8, 0), (0, 2, 4), (0, 3, 3), (0, 4, 3), (0, 6, 1), (0, 9, 0), (0, 3, 4), (0, 4, 4),),
    "P0": ((0, 5, 2), (0, 6, 2), (0, 7, 1), (0, 8, 1), (0, 10, 0), (0, 11, 0),),
    "F0": ((0, 5, 3), (0, 9, 1), (0, 12, 0),),
    "F1": ((0, 6, 3), (0, 7, 2), (0, 8, 2), (0, 11, 1), (0, 13, 0),),
    "before P1": ((0, 5, 4),),
    "P1": ((0, 9, 2), (0, 10, 1), (0, 14, 0),),
    "F2": ((0, 7, 3), (0, 12, 1), (0, 8, 3), (0, 15, 0),),
    "F3": ((0, 9, 3), (0, 11, 2),),
    "before P2": ((0, 6, 4),),
    "P2": ((0, 10, 2), (0, 12, 2), (0, 13, 1), (0, 14, 1), (0, 15, 1),),
    "F4": ((0, 11, 3),),
    "F5": ((0, 10, 3), (0, 14, 2),),
    "before wo": ((0, 7, 4),),
    "wo": ((0, 12, 3),),
    "before U0": ((0, 8, 4),),
    "U0": ((0, 13, 2),),
    "before U1": ((0, 9, 4),),
    "U1": ((0, 14, 3), (0, 15, 2),),
    "before U2": ((0, 10, 4),),
    "before U3": ((0, 11, 4),),
    "U3": ((0, 13, 3),),
    "before down": ((0, 12, 4), (0, 14, 4), (0, 15, 3), (0, 13, 4), (0, 15, 4),),
    "b0": ((1, 0, 0),),
    "b1": ((1, 0, 1), (1, 1, 0),),
    "b2": ((1, 1, 1), (1, 0, 2), (1, 2, 0),),
    "b3": ((1, 1, 2), (1, 2, 1), (1, 3, 0), (1, 4, 0), (1, 5, 0),),
    "ln1b": ((1, 0, 3),),
    "wob": ((1, 3, 1), (1, 6, 0),),
    "B0": ((1, 2, 2), (1, 1, 3), (1, 3, 2), (1, 4, 1), (1, 5, 1), (1, 6, 1), (1, 7, 0), (1, 8, 0),),
    "B1": ((1, 0, 4), (1, 1, 4), (1, 2, 3), (1, 3, 3), (1, 7, 1), (1, 8, 1), (1, 4, 2),),
    "gw0": ((1, 2, 4), (1, 5, 2), (1, 9, 0),),
    "B2": ((1, 3, 4), (1, 6, 2), (1, 9, 1),),
    "B3": ((1, 7, 2), (1, 4, 3), (1, 8, 2),),
    "gw1": ((1, 6, 3), (1, 10, 0),),
    "B4": ((1, 4, 4), (1, 5, 3), (1, 7, 3), (1, 8, 3), (1, 9, 2), (1, 6, 4), (1, 5, 4), (1, 10, 1),),
    "B5": ((1, 7, 4), (1, 9, 3),),
    "rel2": ((1, 10, 2), (1, 11, 0), (1, 12, 0),),
    "gv2": ((1, 8, 4), (1, 13, 0),),
    "gk2": ((1, 11, 1), (1, 12, 1), (1, 10, 3), (1, 13, 1), (1, 14, 0),),
    "gq2": ((1, 9, 4), (1, 11, 2), (1, 14, 1), (1, 15, 0),),
    "end": ((1, 12, 2), (1, 15, 1), (1, 13, 2), (1, 10, 4), (1, 11, 3), (1, 14, 2), (1, 15, 2), (1, 13, 3), (1, 12, 3), (1, 14, 3), (1, 11, 4), (1, 15, 3), (1, 12, 4), (1, 13, 4), (1, 14, 4), (1, 15, 4),),
}


def layer_kernel(
    comm,
    length_ref, index_ref, x_ref, cot_ref, vec_in, rel_in, q_in, k_in, v_in, o_in, up_in, down_in,
    out_ref, gtok_ref, r_out, q_out, k_out, v_out, o_out, up_out, down_out,
    GR, GA, GO, GU, GD,
    q_ref, k_ref, v_ref, kf_ref, vf_ref, kprT_ref, kpsT_ref, qpsT_ref, pick_ref, pT_ref,
    ctx_ref, dcT_ref, n1_ref, inv1_ref, nb_ref, gd_ref, act_ref, gp_ref,
    grel_ref, cols_ref, rows_ref, bup_ref, small_ref, gbup_ref, mask_ref, flip_ref, select_ref,
    *rest,
):
    T, D = x_ref.shape
    FF = act_ref.shape[1]
    NB = pick_ref.shape[0]
    B = T // 2
    C = 256
    R = 128
    CH = FF // D
    scale = (3.0 * HEAD) ** -0.5
    length = length_ref[0]
    row = lambda k: rows_ref[k:k + 1, :]
    whole = (slice(None),) * 4
    per = D // BLOCKS

    def part(ref, *lead, trail=()):
        return lambda c, z, y, x, cols: ref.at[(*lead, c, z, y, x, *trail, slice(None), cols)]

    pieces = [part(GR)] + [part(GA, n) for n in range(D // C)] + [part(GO)]
    pieces += [part(GU, k) for k in range(CH)] + [part(GD, trail=(k,)) for k in range(CH)]
    if comm:
        slots, buffers, (ag_send, ag_recv, rs_send, rs_recv, credit) = rest[0], list(rest[1:-5]), rest[-5:]
        place = Place()
        gathers = [Gather(place, pieces[i], lo, cols, early, ag_send.at[j], ag_recv.at[j]) for j, (i, lo, cols, early) in enumerate(GATHERS)]
        nA, nO, nU, nD = 1, 1 + D // C, 2 + D // C, 2 + D // C + CH

        def finisher(i):
            def store(lo, total):
                cols = pl.ds(lo, total.shape[1])
                if i == 0:
                    r_out[:, cols] = total
                elif i < nO:
                    for b in range(0, total.shape[1], 128):
                        ref = (q_out, k_out, v_out)[(lo + b) // C]
                        ref[:, pl.ds((i - nA) * C + (lo + b) % C, 128)] = total[:, b:b + 128]
                elif i == nO:
                    o_out[:, cols] = total
                elif i < nD:
                    up_out[:, pl.ds((i - nU) * D + lo, total.shape[1])] = total
                else:
                    down_out[pl.ds((i - nD) * per, per), cols] = total
            return store

        scatters = []
        for j, (i, lo, cols, late) in enumerate(SCATTERS):
            number = 6 if late else 5
            scatters.append(Scatter(place, pieces[i], lo, cols, late, j, len(SCATTERS), slots, buffers[:number],
                                    rs_send.at[j], rs_recv.at[j], credit, finisher(i)))
            buffers = buffers[number:]

    def run(name):
        if comm:
            for kind, j, k in TICKS.get(name, ()):
                (scatters if kind else gathers)[j].step(k)

    def due(name, index, values):
        if comm:
            for m in values:
                label = f"{name}{m}"
                if label in TICKS:
                    @pl.when(index == m)
                    def _():
                        run(label)

    if comm:
        me = (place.c, place.z, place.y, place.x)
        rows_ref[...] = jnp.zeros_like(rows_ref)
        for k, ref in enumerate(vec_in[:-1]):
            rows_ref[k:k + 1, 0:per] = ref[...].astype(F32).reshape(1, per)
        last = vec_in[-1][...].astype(F32).reshape(1, CH * per)
        for k in range(CH):
            rows_ref[9 + k:10 + k, 0:per] = last[:, k * per:(k + 1) * per]
        own = jnp.concatenate([rows_ref[:, 0:128], jnp.zeros((112, 128), F32)], axis=0).T
        GR[(*me, slice(None), pl.ds(0, NB))] = rel_in[...]
        GR[(*me, slice(None), pl.ds(NB, 128))] = own[0:per].astype(BF)
        for n in range(D // C):
            cols = pl.ds(n * C, C)
            for i, ref in enumerate((q_in, k_in, v_in)):
                GA[(n, *me, slice(None), pl.ds(i * C, C))] = ref[:, cols]
        GO[me] = o_in[...]
        for k in range(CH):
            GU[(k, *me)] = up_in[:, pl.ds(k * D, D)]
            GD[(*me, k)] = down_in[k]
        place.barrier()
        run("pre")
    else:
        GRh, GAh, GOh, GUh, GDh = rest[:5]
        sems = rest[10]
        loads = [pltpu.make_async_copy(src, dst, sems.at[i]) for i, (src, dst) in enumerate(zip((GRh, GAh, GOh, GUh, GDh), (GR, GA, GO, GU, GD)))]
        for copy in loads:
            copy.start()
        for copy in loads:
            copy.wait()
    flip_ref[...] = jnp.where(iota((B, B), 0) + iota((B, B), 1) == B - 1, 1.0, 0.0).astype(BF)
    index = jnp.broadcast_to(index_ref[...].reshape(1, 2 * T), (8, 2 * T))
    high = lax.shift_right_logical(index, 4)
    parts = [v.astype(F32).astype(BF) for v in (high, index - 16 * high)]
    back = [jnp.concatenate([nn(v[:, b * B:(b + 1) * B], flip_ref[...]) for b in range(2 * T // B - 1, -1, -1)], axis=1) for v in parts]
    reverse = (back[0] * 16.0 + back[1]).astype(jnp.int32)
    shifted = jnp.where(iota((8, 2 * T), 1) == 2 * T - 1, -1, pltpu.roll(index, 2 * T - 1, 1))
    act_ref[:, 0:2 * T] = jnp.where(iota((NB, 2 * T), 0) == reverse[0:1], 1.0, 0.0).astype(BF)
    pick_ref[...] = jnp.where(iota((NB, 2 * T), 0) == shifted[0:1], 1.0, 0.0).astype(BF)
    W = 4 * per
    block = sum(jnp.where(iota((W, CH * W), 0) >= per * i, 1, 0) for i in range(1, 4))
    ublock = sum(jnp.where(iota((1, CH * W), 1) >= per * CH * i, 1, 0) for i in range(1, 4))
    uslice = sum(jnp.where(iota((1, CH * W), 1) >= per * i, 1, 0) for i in range(1, 4 * CH))
    place_in = iota((1, CH * W), 1) - per * uslice
    select_ref[...] = jnp.where((block == ublock) & (iota((W, CH * W), 0) - per * block == place_in), 1.0, 0.0).astype(BF)
    own_column = iota((128, CH * W), 0) == 9 + uslice - CH * ublock
    mask_ref[...] = jnp.where(iota((8, T), 1) < length, 0.0, -1e30)
    small_ref[...] = jnp.zeros_like(small_ref)
    grel_ref[...] = jnp.zeros_like(grel_ref)
    run("before P0")
    cols_ref[...] = matrix(GR[(*whole, slice(None), pl.ds(NB, 128))].astype(F32))
    rows_ref[...] = cols_ref[...].T[0:16]

    @pl.loop(0, D // W)
    def _(t):
        spread = tn(cols_ref[tile(t, W), :].astype(BF), select_ref[...])
        bup_ref[0:1, tile(t, CH * W)] = column_sum(jnp.where(own_column, spread, 0.0))

    @pl.loop(0, D // C)
    def _(n):
        due("before P", n, range(1, D // C))
        cols = tile(n, C)
        weight = lambda i: matrix(GA[(n, *whole, slice(None), pl.ds(i * C, C))])
        relT = matrix(GR[(*whole, slice(None), pl.ds(0, NB))])
        wq, wk, wv = weight(0), weight(1), weight(2)
        q_ref[:, cols] = (nn(x_ref[...], wq) + rows_ref[0:1, cols]).astype(BF)
        k = (nn(x_ref[...], wk) + rows_ref[1:2, cols]).astype(BF)
        v = (nn(x_ref[...], wv) + rows_ref[2:3, cols]).astype(BF)
        k_ref[:, cols] = k
        v_ref[:, cols] = v
        for src, dst in ((k, kf_ref), (v, vf_ref)):
            dst[0:B, cols] = nn(flip_ref[...], src[B:T]).astype(BF)
            dst[B:T, cols] = nn(flip_ref[...], src[0:B]).astype(BF)
        rk = (tn(wk, relT) + cols_ref[cols, 1:2]).astype(BF)
        rq = (tn(wq, relT) + cols_ref[cols, 0:1]).astype(BF)
        kprT_ref[cols, :] = nn(rk, act_ref[:, 0:2 * T]).astype(BF)
        kpsT_ref[cols, :] = nn(rk, pick_ref[...]).astype(BF)
        qpsT_ref[cols, :] = nn(rq, pick_ref[...]).astype(BF)
        due("P", n, range(D // C))

        @pl.loop(0, 2)
        def _(i):
            pair_forward(2 * n + i, q_ref, k_ref, v_ref, kprT_ref, qpsT_ref, mask_ref, flip_ref, ctx_ref, pT_ref, scale)
            due("F", 2 * n + i, range(2 * D // C))

    run("before wo")
    second_ref = gtok_ref

    @pl.loop(0, D // C)
    def _(n):
        cols = tile(n, C)
        w = matrix(GO[(*whole, slice(None), cols)])
        second_ref[:, cols] = x_ref[:, cols].astype(F32) + (nn(ctx_ref[...], w) + rows_ref[3:4, cols])

    run("wo")

    @pl.loop(0, T // R)
    def _(r):
        rs = tile(r, R)
        n1, inv1 = norm_rows(second_ref[rs, :])
        n1_ref[rs, :] = n1
        inv1_ref[rs, :] = jnp.broadcast_to(inv1, (R, 128))
        nb_ref[rs, :] = (n1 * row(4) + row(5)).astype(BF)

    run("ln1")

    @pl.loop(0, CH)
    def _(k):
        due("before U", k, range(CH))

        @pl.loop(0, D // C)
        def _(j):
            w = matrix(GU[(k, *whole, slice(None), tile(j, C))])
            cols = tile(k * (D // C) + j, C)
            up = nn(nb_ref[...], w) + bup_ref[0:1, cols]
            phi, e = normal_cdf_pair(up)
            act_ref[:, cols] = (up * phi).astype(BF)
            gp_ref[:, cols] = (phi + up * e * 0.3989422804014327).astype(BF)

        due("U", k, range(CH))

    run("before down")

    @pl.loop(0, D // C)
    def _(n):
        cols = tile(n, C)
        w = matrix(GD[(*whole, slice(None), slice(None), cols)])
        normed = n1_ref[:, cols] * rows_ref[4:5, cols] + rows_ref[5:6, cols]
        second_ref[:, cols] = normed + (nn(act_ref[...], w) + rows_ref[6:7, cols])

    run("down")

    @pl.loop(0, T // R)
    def _(r):
        rs = tile(r, R)
        live = jnp.where(iota((R, 1), 0) + r * R < length, 1.0, 0.0)
        n2, inv2 = norm_rows(second_ref[rs, :])
        out_ref[rs, :] = ((n2 * row(7) + row(8)) * live).astype(BF)
        start = cot_ref[rs, :].astype(F32) * live
        g = norm_back(start * row(7), n2, inv2)
        second_ref[rs, :] = g
        gd = g.astype(BF)
        gd_ref[rs, :] = gd
        small_ref[6:7, :] += column_sum(gd.astype(F32))
        small_ref[7:8, :] += column_sum(start * n2)
        small_ref[8:9, :] += column_sum(start)

    run("ln2")
    half = GRID[1] // 2

    @pl.loop(0, CH)
    def _(k):
        units = tile(k, D)
        c, z0 = lax.div(k, 2), half * lax.rem(k, 2)
        w = matrix(GD[c, pl.ds(z0, half)])
        gu = (nt(gd_ref[...], w) * gp_ref[:, units].astype(F32)).astype(BF)
        gp_ref[:, units] = gu
        gbup_ref[0:1, units] = column_sum(gu.astype(F32))

        @pl.loop(0, half)
        def _(i):
            at = pl.ds(pl.multiple_of(k * D + i * (D // 2), D // 2), D // 2)
            g = tn(act_ref[:, at], gd_ref[...])
            GD[c, z0 + i] = g.reshape(*GD.shape[2:]).astype(BF)

        second_ref[...] += nt(gu, matrix(GU[k]))

        @pl.loop(0, GRID[0])
        def _(i):
            g = tn(nb_ref[:, tile(i, D // 2)], gp_ref[:, units])
            GU[k, i] = g.reshape(*GU.shape[2:]).astype(BF)

        due("b", k, range(CH))

    @pl.loop(0, T // R)
    def _(r):
        rs = tile(r, R)
        g = second_ref[rs, :]
        n1 = n1_ref[rs, :]
        gm = norm_back(g * row(4), n1, inv1_ref[rs, 0:1])
        second_ref[rs, :] = gm
        ga = gm.astype(BF)
        gd_ref[rs, :] = ga
        small_ref[3:4, :] += column_sum(ga.astype(F32))
        small_ref[4:5, :] += column_sum(g * n1)
        small_ref[5:6, :] += column_sum(g)

    run("ln1b")

    @pl.loop(0, GRID[0])
    def _(i):
        at = tile(i, D // 2)
        dcT_ref[at, :] = nt(matrix(GO[i]), gd_ref[...]).astype(BF)
        g = tn(ctx_ref[:, at], gd_ref[...])
        GO[i] = g.reshape(*GO.shape[1:]).astype(BF)

    run("wob")

    kprT_ref[:, 0:NB] = matrix(GR[(*whole, slice(None), pl.ds(0, NB))])

    @pl.loop(0, D // C)
    def _(n):
        cols = tile(n, C)
        final = (D // C - 1,)

        @pl.loop(0, 2)
        def _(i):
            pair_backward(2 * n + i, q_ref, kf_ref, vf_ref, kpsT_ref, qpsT_ref, dcT_ref, pT_ref, scale)
            due("B", 2 * n + i, range(2 * D // C))

        dq = q_ref[:, cols]
        for src, dst in ((kf_ref, k_ref), (vf_ref, v_ref)):
            dst[0:B, cols] = nn(flip_ref[...], src[B:T, cols]).astype(BF)
            dst[B:T, cols] = nn(flip_ref[...], src[0:B, cols]).astype(BF)
        dk, dv = k_ref[:, cols], v_ref[:, cols]
        grk = nt(kpsT_ref[cols, :], pick_ref[...]).astype(BF)
        grq = nt(qpsT_ref[cols, :], pick_ref[...]).astype(BF)
        weight = lambda i: matrix(GA[(n, *whole, slice(None), pl.ds(i * C, C))])
        grel_ref[...] += nn(weight(1), grk) + nn(weight(0), grq)
        ones_t, ones_b = jnp.ones((8, T), BF), jnp.ones((8, NB), BF)
        small_ref[0:1, cols] = (nn(ones_t, dq) + nt(ones_b, grq))[0:1]
        small_ref[1:2, cols] = (nn(ones_t, dk) + nt(ones_b, grk))[0:1]
        small_ref[2:3, cols] = nn(ones_t, dv)[0:1]

        @pl.when(n == final[0])
        def _():
            small_ref[9:16, :] = jnp.zeros((7, D), F32)
            cols_ref[...] = jnp.concatenate([small_ref[...], jnp.zeros((112, D), F32)], axis=0).T

            @pl.loop(0, D // W)
            def _(t):
                g = jnp.where(own_column, gbup_ref[0:1, tile(t, CH * W)], 0.0).astype(BF)
                cols_ref[tile(t, W), :] += nt(select_ref[...], g)

            GR[(*whole, slice(None), pl.ds(0, NB))] = grel_ref[...].reshape(*GR.shape[:5], NB).astype(BF)
            GR[(*whole, slice(None), pl.ds(NB, 128))] = cols_ref[...].reshape(*GR.shape[:5], 128).astype(BF)

        due("rel", n, final)
        for i, name, d, gr in ((2, "gv", dv, None), (1, "gk", dk, grk), (0, "gq", dq, grq)):
            gtok_ref[...] += nt(d, weight(i))
            for half in range(GRID[0]):
                g = tn(x_ref[:, half * (D // 2):(half + 1) * (D // 2)], d)
                if gr is not None:
                    g = g + nt(kprT_ref[half * (D // 2):(half + 1) * (D // 2), 0:NB], gr)
                GA[(n, half, *whole[1:], slice(None), pl.ds(i * C, C))] = g.reshape(*GA.shape[2:6], C).astype(BF)
            due(name, n, final)
        due("gw", n, range(D // C))

    if comm:
        run("end")
    else:
        GRh, GAh, GOh, GUh, GDh = rest[5:10]
        stores = [pltpu.make_async_copy(src, dst, sems.at[i]) for i, (dst, src) in enumerate(zip((GRh, GAh, GOh, GUh, GDh), (GR, GA, GO, GU, GD)))]
        for copy in stores:
            copy.start()
        for copy in stores:
            copy.wait()


def finish_kernel(r_ref, *refs):
    n = (len(refs) - 11) // 2
    for i in range(n):
        refs[n + i][...] = refs[i][...]
    rel_out, vectors, wide = refs[2 * n], refs[2 * n + 1:2 * n + 10], refs[2 * n + 10]
    rows, NB = rel_out.shape
    rel_out[...] = r_ref[:, 0:NB]
    flat = jnp.concatenate([r_ref[:, NB:], jnp.zeros((128 - rows, 128), F32)], axis=0).T
    for k, ref in enumerate(vectors):
        ref[...] = flat[k:k + 1, 0:rows].reshape(rows)
    wide[...] = jnp.concatenate([flat[9 + k:10 + k, 0:rows] for k in range(wide.shape[0] // rows)], axis=1).reshape(wide.shape[0])


def layer_scratch(T, D, FF, NB, heads):
    V = pltpu.VMEM
    n, ch = D // 256, FF // D
    rows = D // BLOCKS
    td, r = V((T, D), BF), V((*GRID, rows, NB + 128), BF)
    return [
        r, V((n, *GRID, rows, D), BF), V((*GRID, rows, D), BF), V((ch, *GRID, rows, D), BF), V((*GRID, ch, rows, D), BF),
        td, td, td, td, td, V((D, 2 * T), BF), V((D, 2 * T), BF), V((D, 2 * T), BF), V((NB, 2 * T), BF), V((heads, T, T), BF),
        td, V((D, T), BF), V((T, D), F32), V((T, 128), F32), td, td, V((T, FF), BF), V((T, FF), BF),
        V((D, NB), F32), V((D, 128), F32), V((16, D), F32), V((8, FF), F32), V((16, D), F32), V((8, FF), F32), V((8, T), F32),
        V((T // 2, T // 2), BF), V((4 * rows, 4 * rows * ch), BF),
    ]


def call_layer(comm, length, index, x, cot, parts):
    T, D = x.shape
    S = jax.ShapeDtypeStruct
    VM, HBM, SM = (pl.BlockSpec(memory_space=space) for space in (pltpu.VMEM, pl.ANY, pltpu.SMEM))
    heads = D // HEAD
    if comm:
        vectors, rel, wq, wk, wv, wo, wup, wdown = parts
        operands = (*vectors, rel, wq, wk, wv, wo, wup, wdown)
        rows, FF = wup.shape
        NB = rel.shape[1]
        outs = [S((T, D), BF), S((T, D), F32), S((rows, NB + 128), F32)] + [S((rows, D), F32)] * 4 + [S(wup.shape, F32), S((FF // D * rows, D), F32)]
        out_specs = [VM] * len(outs)
        in_specs = [SM] + [VM] * (3 + len(operands))
        sems = [pltpu.SemaphoreType.DMA((len(parts), k)) for parts in (GATHERS, SCATTERS) for k in (1, 4)] + [pltpu.SemaphoreType.REGULAR]
        extra = [pltpu.VMEM((SLOTS, *GRID[1:], rows, D), BF)]
        for _, _, cols, late in SCATTERS:
            extra += scatter_buffers(rows, cols, late)
        extra += sems

        def kernel(*refs):
            given = 4 + len(vectors)
            layer_kernel(True, *refs[:4], refs[4:given], *refs[given:])
    else:
        gr, ga, go, gu, gd = operands = parts
        FF, NB = gu.shape[0] * D, gr.shape[-1] - 128
        outs = [S((T, D), BF), S((T, D), F32)] + [S(p.shape, p.dtype) for p in parts]
        in_specs = [SM] + [VM] * 3 + [HBM] * 5
        out_specs = [VM] * 2 + [HBM] * 5
        extra = [pltpu.SemaphoreType.DMA((5,))]

        def kernel(*refs):
            ins, given, results, stored, scratch = refs[:4], refs[4:9], refs[9:11], refs[11:16], refs[16:]
            layer_kernel(False, *ins, *[None] * 8, *results, *[None] * 7, *scratch[:-1], *given, *stored, scratch[-1])

    return pl.pallas_call(
        kernel,
        out_shape=outs,
        in_specs=in_specs,
        out_specs=out_specs,
        scratch_shapes=layer_scratch(T, D, FF, NB, heads) + extra,
        compiler_params=pltpu.CompilerParams(
            vmem_limit_bytes=VMEM_LIMIT,
            **(dict(collective_id=0, has_side_effects=True) if comm else {}),
        ),
    )(length, index, x, cot, *operands)


VMEM_LIMIT = 63 * 2**20


def body(comm, tokens, lengths, rel_index, w_query, b_query, w_key, b_key, w_value, b_value, w_out, b_out, rel_table,
         gain_one, shift_one, w_up, b_up, w_down, b_down, gain_two, shift_two, cotangent):
    rows, D = w_query.shape
    NB = rel_table.shape[0]
    FF = w_up.shape[1]
    ch, n = FF // D, D // 256
    vectors = (b_query, b_key, b_value, b_out, gain_one, shift_one, b_down, gain_two, shift_two)
    if comm:
        results = call_layer(True, lengths, rel_index, tokens, cotangent,
                             ((*vectors, b_up), rel_table.T, w_query, w_key, w_value, w_out, w_up, w_down.reshape(ch, rows, D)))
        out, gtok, gr, gq, gk, gv, go, gup, gdown = results
        S = jax.ShapeDtypeStruct
        VM = pl.BlockSpec(memory_space=pltpu.VMEM)
        moved = (out, gtok, gq, gk, gv, go, gup, gdown)
        *moved, rel, bq, bk, bv, bo, g1, s1, bd, g2, s2, bu = pl.pallas_call(
            finish_kernel,
            out_shape=[S(a.shape, a.dtype) for a in moved] + [S((rows, NB), F32)] + [S((rows,), F32)] * 9 + [S(b_up.shape, F32)],
            in_specs=[VM] * 9,
            out_specs=[VM] * 19,
            compiler_params=pltpu.CompilerParams(vmem_limit_bytes=VMEM_LIMIT),
        )(gr, *moved)
        out, gtok, gq, gk, gv, go, gup, gdown = moved
        return (out, gtok, gq, bq, gk, bk, gv, bv, go, bo, rel.T, g1, s1, gup, bu, gdown, bd, g2, s2)
    gather = lambda w: lax.all_gather(w, AXES, axis=0, tiled=True)
    scatter = lambda g: lax.psum_scatter(g.astype(F32), AXES, scatter_dimension=0, tiled=True)
    r = D // BLOCKS
    pad = jnp.zeros((rows, 128 - 9), BF)
    attend = gather(jnp.concatenate([w_out, w_query, w_key, w_value, rel_table.T, jnp.stack(vectors, axis=1), pad], axis=1))
    wide = gather(b_up).reshape(BLOCKS, ch, r).transpose(0, 2, 1).reshape(D, ch)
    gr = jnp.concatenate([attend[:, 4 * D:4 * D + NB + 9], wide, pad[0] * jnp.ones((D, 1), BF)], axis=1)[:, :NB + 128].reshape(*GRID, r, NB + 128)
    go = attend[:, :D].reshape(*GRID, r, D)
    ga = attend[:, D:4 * D].reshape(*GRID, r, 3, n, 256).transpose(6, 0, 1, 2, 3, 4, 5, 7).reshape(n, *GRID, r, D)
    gu = gather(w_up).reshape(*GRID, r, ch, D).transpose(5, 0, 1, 2, 3, 4, 6)
    gd = gather(w_down).reshape(*GRID, ch, r, D)
    out, gtok, gr, ga, go, gu, gd = call_layer(False, lengths, rel_index, tokens, cotangent, (gr, ga, go, gu, gd))
    gr = gr.reshape(D, NB + 128)
    ga = ga.reshape(n, *GRID, r, 3, 256).transpose(1, 2, 3, 4, 5, 6, 0, 7).reshape(D, 3 * D)
    wide = scatter(gr[:, NB + 9:NB + 9 + ch].reshape(BLOCKS, r, ch).transpose(0, 2, 1).reshape(FF))
    gup = scatter(gu.transpose(1, 2, 3, 4, 5, 0, 6).reshape(D, FF))
    gdown = scatter(gd.reshape(FF, D))
    attend = scatter(jnp.concatenate([go.reshape(D, D), ga, gr], axis=1))
    go, gq, gk, gv = (attend[:, i * D:(i + 1) * D] for i in range(4))
    vec = lambda i: attend[:, 4 * D + NB + i]
    return (out, gtok, gq, vec(0), gk, vec(1), gv, vec(2), go, vec(3), attend[:, 4 * D:4 * D + NB].T, vec(4), vec(5),
            gup, wide, gdown, vec(6), vec(7), vec(8))


def solution(mesh):
    rows, vec = P(AXES, None), P(AXES)
    comm = mesh.shape["dp"] == GRID[0] and mesh.shape["fsdp"] == GRID[1] * GRID[2] * GRID[3]

    def step(*args):
        return body(comm, *args)

    return jax.shard_map(
        step,
        mesh=mesh,
        in_specs=(rows, vec, P(), rows, vec, rows, vec, rows, vec, rows, vec, P(None, AXES), vec, vec, rows, vec, rows, vec, vec, vec, rows),
        out_specs=(rows, rows, rows, vec, rows, vec, rows, vec, rows, vec, P(None, AXES), vec, vec, rows, vec, rows, vec, vec, vec),
        check_vma=False,
    )
```

time: 220 us -> 179 us (0.81)
  local copies, waits for them, and re-layouts: 22.6 us -> 0 us
  Pallas kernels: 195 us -> 178 us
    pallas_call x1, Pallas kernels: 195 us -> 174 us  [call_layer(): pl.pallas_call(kernel, out_shape=outs, in_specs=in_specs, out_specs=out_s...]
    unnamed x22 -> x0, local copies, waits for them, and re-layouts: 7.19 us -> none
    another operation x9 -> x0, local copies, waits for them, and re-layouts: 6.73 us -> none  [body(): jnp.stack(vectors, axis=1)]
    pallas_call x0 -> x1, Pallas kernels: none -> 3.7 us  [body(): pl.pallas_call(finish_kernel, out_shape=[S(a.shape, a.dtype) for a in mov...]
    slice x3 -> x0, local copies, waits for them, and re-layouts: 3.65 us -> none  [the longest x1 2.12 us: body(): vec = lambda i: gr[:, NB + i]]
where the time goes in v3:
time: 179 us
  Pallas kernels  178 us (99%)
    pallas_call x1, Pallas kernels, call_layer(): pl.pallas_call(kernel, out_shape=outs, in_specs=in_specs, out_specs=out_s...  174 us
    pallas_call x1, Pallas kernels, body(): pl.pallas_call(finish_kernel, out_shape=[S(a.shape, a.dtype) for a in mov...  3.7 us

profile of v3, /device:TPU:0, one launch (start us, length us, event | category | flops | bytes accessed | tf_op | source)
XLA Modules:
  0.0 179.2 jit_solution(8234492074915562242)
XLA Ops:
  1.3 174.0 %shard_map.348 = (bf16[512,768]{1,0:T(8,128)(2,1)}, f32[512,768]{1,0:T(8,128)}, f32[24,640]{1,0:T(8,128)}, f32[24,768]{1,0:T(8,128)}, f32[24,768]{1,0:T(8,128)},...) custom-call(s32[1]{0:T(128)S(6)} %copy.40.refs_0_, s32[1024]{0:T(1024)} %refs_1_.1, ...), custom_call_target="tpu_custom_call" | custom-call | tf_op jit(solution)/shard_map/pallas_call | solution.py:799
  175.3 3.7 %shard_map.349 = (bf16[512,768]{1,0:T(8,128)(2,1)}, f32[512,768]{1,0:T(8,128)}, f32[24,768]{1,0:T(8,128)}, f32[24,768]{1,0:T(8,128)}, f32[24,768]{1,0:T(8,128)},...) custom-call(f32[24,640]{1,0:T(8,128)} %get-tuple-element.47.r_ref, ...), custom_call_target="tpu_custom_call" | custom-call | tf_op jit(solution)/shard_map/pallas_call | solution.py:829

commit v4 on v3

--- a/solution.py
+++ b/solution.py
@@ -12,7 +12,7 @@
 AXES = ("dp", "fsdp")
 MESH = pl.DeviceIdType.MESH
 LOG2E = 1.4426950408889634
-GRID = (2, 4, 2, 2)
+GRID = (2, 2, 2, 2, 2)
 BLOCKS = 32
 SLOTS = 3
 
@@ -147,262 +147,199 @@
 
 class Place:
     def __init__(self):
-        self.nz = GRID[1]
-        self.c = lax.axis_index("dp")
         f = lax.axis_index("fsdp")
-        self.x = lax.rem(f, 2)
-        self.y = lax.rem(lax.div(f, 2), 2)
-        self.z = lax.div(f, 4)
-        self.nx = 1 - self.x
-        self.ny = 1 - self.y
-
-    def at(self, c=None, z=None, y=None, x=None):
-        c = self.c if c is None else c
-        z = self.z if z is None else z
-        y = self.y if y is None else y
-        x = self.x if x is None else x
-        return (c, (z * 2 + y) * 2 + x)
-
-    def zs(self):
-        return [lax.rem(self.z + d, self.nz) for d in range(1, self.nz)]
+        self.here = dict(c=lax.axis_index("dp"), v=lax.div(f, 8), w=lax.rem(lax.div(f, 4), 2), y=lax.rem(lax.div(f, 2), 2), x=lax.rem(f, 2))
+
+    def across(self, axis):
+        to = {**self.here, axis: 1 - self.here[axis]}
+        return (to["c"], ((to["v"] * 2 + to["w"]) * 2 + to["y"]) * 2 + to["x"])
+
+    def index(self, whole="", other=""):
+        return tuple(slice(None) if a in whole else 1 - i if a in other else i for a, i in self.here.items())
 
     def barrier(self):
         sem = pltpu.get_barrier_semaphore()
-        peers = [self.at(z=z) for z in self.zs()] + [self.at(x=self.nx), self.at(y=self.ny), self.at(c=1 - self.c)]
-        for peer in peers:
-            pl.semaphore_signal(sem, inc=1, device_id=peer, device_id_type=MESH)
-        pl.semaphore_wait(sem, len(peers))
+        for axis in self.here:
+            pl.semaphore_signal(sem, inc=1, device_id=self.across(axis), device_id_type=MESH)
+        pl.semaphore_wait(sem, len(self.here))
 
 
 def remote(src, dst, send, recv, to):
     return pltpu.make_async_remote_copy(src_ref=src, dst_ref=dst, send_sem=send, recv_sem=recv, device_id=to, device_id_type=MESH)
+
+
+GATHERS = (
+    (0, 384, 256),
+    (1, 0, 256),
+    (1, 256, 256),
+    (1, 512, 256),
+    (0, 0, 384),
+    (2, 0, 768),
+    (3, 0, 768),
+    (4, 0, 768),
+    (5, 0, 768),
+    (6, 0, 768),
+    (7, 0, 768),
+    (8, 0, 768),
+    (9, 0, 768),
+    (10, 0, 768),
+    (11, 0, 768),
+    (12, 0, 768),
+)
+SCATTERS = (
+    (5, 0, 768),
+    (6, 0, 768),
+    (7, 0, 768),
+    (8, 0, 768),
+    (9, 0, 768),
+    (10, 0, 768),
+    (11, 0, 768),
+    (12, 0, 768),
+    (4, 0, 768),
+    (1, 0, 768),
+    (2, 0, 768),
+    (0, 0, 384),
+    (0, 384, 256),
+    (3, 512, 256),
+    (3, 256, 256),
+    (3, 0, 256),
+)
+TICKS = {
+    "pre": ((0, 0, 0), (0, 1, 0), (0, 2, 0), (0, 3, 0), (0, 4, 0), (0, 5, 0), (0, 6, 0),),
+    "before Q0": ((0, 0, 1), (0, 1, 1), (0, 2, 1), (0, 7, 0), (0, 3, 1), (0, 4, 1), (0, 0, 2), (0, 1, 2), (0, 2, 2), (0, 5, 1), (0, 8, 0), (0, 3, 2), (0, 4, 2), (0, 6, 1), (0, 9, 0), (0, 0, 3), (0, 7, 1), (0, 5, 2), (0, 1, 3), (0, 10, 0), (0, 2, 3), (0, 6, 2), (0, 8, 1), (0, 11, 0), (0, 0, 4), (0, 3, 3), (0, 7, 2), (0, 1, 4), (0, 4, 3), (0, 9, 1), (0, 12, 0), (0, 2, 4), (0, 0, 5), (0, 8, 2), (0, 1, 5), (0, 3, 4), (0, 2, 5), (0, 5, 3), (0, 4, 4), (0, 10, 1), (0, 13, 0), (0, 9, 2), (0, 3, 5),),
+    "before P0": ((0, 4, 5),),
+    "P0": ((0, 6, 3),),
+    "F0": ((0, 5, 4), (0, 7, 3), (0, 10, 2), (0, 11, 1), (0, 14, 0),),
+    "F1": ((0, 6, 4), (0, 8, 3), (0, 12, 1), (0, 15, 0),),
+    "before Q1": ((0, 5, 5),),
+    "Q1": ((0, 13, 1), (0, 7, 4),),
+    "P1": ((0, 11, 2),),
+    "F2": ((0, 8, 4), (0, 9, 3), (0, 12, 2), (0, 10, 3),),
+    "F3": ((0, 13, 2), (0, 14, 1), (0, 15, 1),),
+    "before Q2": ((0, 6, 5),),
+    "Q2": ((0, 11, 3),),
+    "P2": ((0, 9, 4),),
+    "F4": ((0, 10, 4), (0, 12, 3), (0, 14, 2), (0, 15, 2),),
+    "F5": ((0, 11, 4), (0, 13, 3),),
+    "before wo": ((0, 7, 5),),
+    "before U0": ((0, 8, 5),),
+    "U0": ((0, 12, 4), (0, 14, 3),),
+    "before U1": ((0, 9, 5),),
+    "U1": ((0, 15, 3),),
+    "before U2": ((0, 10, 5),),
+    "U2": ((0, 13, 4),),
+    "before U3": ((0, 11, 5),),
+    "before down": ((0, 12, 5), (0, 14, 4), (0, 13, 5), (0, 15, 4), (0, 14, 5), (0, 15, 5),),
+    "b0": ((1, 0, 0),),
+    "b1": ((1, 1, 0),),
+    "b2": ((1, 0, 1), (1, 2, 0),),
+    "b3": ((1, 1, 1), (1, 3, 0),),
+    "d0": ((1, 2, 1),),
+    "d2": ((1, 0, 2),),
+    "d3": ((1, 3, 1), (1, 4, 0), (1, 5, 0), (1, 6, 0),),
+    "wob": ((1, 1, 2),),
+    "B0": ((1, 0, 3), (1, 2, 2), (1, 4, 1), (1, 5, 1), (1, 6, 1), (1, 7, 0), (1, 8, 0),),
+    "B1": ((1, 0, 4), (1, 1, 3), (1, 3, 2), (1, 7, 1),),
+    "gw0": ((1, 2, 3), (1, 4, 2), (1, 8, 1), (1, 9, 0),),
+    "B2": ((1, 0, 5), (1, 3, 3), (1, 5, 2), (1, 9, 1),),
+    "B3": ((1, 1, 4), (1, 4, 3), (1, 6, 2),),
+    "gw1": ((1, 2, 4), (1, 5, 3), (1, 7, 2), (1, 10, 0),),
+    "B4": ((1, 1, 5), (1, 3, 4), (1, 2, 5), (1, 6, 3), (1, 8, 2), (1, 10, 1),),
+    "B5": ((1, 3, 5), (1, 4, 4), (1, 5, 4), (1, 6, 4), (1, 7, 3), (1, 9, 2),),
+    "rel2": ((1, 11, 0), (1, 12, 0),),
+    "gv2": ((1, 13, 0),),
+    "gk2": ((1, 8, 3),),
+    "gq2": ((1, 10, 2), (1, 4, 5), (1, 7, 4), (1, 11, 1), (1, 14, 0), (1, 12, 1), (1, 15, 0), (1, 13, 1),),
+    "end": ((1, 5, 5), (1, 8, 4), (1, 6, 5), (1, 14, 1), (1, 15, 1), (1, 9, 3), (1, 11, 2), (1, 12, 2), (1, 13, 2), (1, 10, 3), (1, 14, 2), (1, 7, 5), (1, 15, 2), (1, 8, 5), (1, 9, 4), (1, 11, 3), (1, 10, 4), (1, 12, 3), (1, 13, 3), (1, 11, 4), (1, 14, 3), (1, 12, 4), (1, 15, 3), (1, 13, 4), (1, 9, 5), (1, 10, 5), (1, 14, 4), (1, 11, 5), (1, 12, 5), (1, 15, 4), (1, 13, 5), (1, 14, 5), (1, 15, 5),),
+}
+STEPS = ((("v", ""),), (("x", "v"), ("y", "v")), (("w", "vx"), ("w", "vy")), (("y", "vxw"), ("x", "vyw")))
 
 
 class Part:
     def __init__(self, place, piece, lo, cols):
         cut = cols // 256 * 128
-        self.p, self.piece, self.lo, self.cols, self.cut = place, piece, lo, cols, cut
-        self.all, self.h1, self.h2 = pl.ds(lo, cols), pl.ds(lo, cut), pl.ds(lo + cut, cols - cut)
-
-
-class Gather(Part):
-    def __init__(self, place, piece, lo, cols, early, send, recv):
-        super().__init__(place, piece, lo, cols)
-        self.early, self.send, self.recv = early, send, recv
-
-    def copies(self, k):
-        p, g, every = self.p, self.piece, slice(None)
-        if k == 0 and self.early:
-            return [(g(p.c, p.z, p.y, p.x, self.h1), p.at(x=p.nx)), (g(p.c, p.z, p.y, p.x, self.h2), p.at(y=p.ny))]
-        if k == 1 and self.early:
-            return ([(g(p.c, p.z, p.y, every, self.h1), p.at(z=z)) for z in p.zs()]
-                    + [(g(p.c, p.z, every, p.x, self.h2), p.at(z=z)) for z in p.zs()])
-        if k == 0:
-            return [(g(p.c, p.z, p.y, p.x, self.all), p.at(z=z)) for z in p.zs()]
-        if k == 1:
-            return [(g(p.c, every, p.y, p.x, self.h1), p.at(x=p.nx)), (g(p.c, every, p.y, p.x, self.h2), p.at(y=p.ny))]
-        if k == 2:
-            return [(g(p.c, every, p.y, every, self.h1), p.at(y=p.ny)), (g(p.c, every, every, p.x, self.h2), p.at(x=p.nx))]
-        return [(g(p.c, every, every, every, self.all), p.at(c=1 - p.c))]
-
-    def settle(self, k):
-        p, g, every = self.p, self.piece, slice(None)
-        three = pl.ds(0, p.nz - 1)
-        if k == 0:
-            ref = g(p.c, p.z, p.y, p.x, self.all) if self.early else g(p.c, three, p.y, p.x, self.all)
-        elif k == 1:
-            ref = g(p.c, three, p.y, every, self.all) if self.early else g(p.c, every, p.y, p.x, self.all)
-        elif k == 2:
-            ref = g(p.c, every, p.y, every, self.all)
-        else:
-            ref = g(p.c, every, every, every, self.all)
-        copy = remote(ref, ref, self.send.at[0], self.recv.at[k], p.at(c=1 - p.c))
+        self.p, self.piece, self.lo, self.cols = place, piece, lo, cols
+        self.all = pl.ds(lo, cols)
+        self.halves = (pl.ds(lo, cut), pl.ds(lo + cut, cols - cut))
+
+    def spans(self, k):
+        return (self.all,) if len(STEPS[k]) == 1 else self.halves
+
+    def settle(self, ref, send, recv):
+        copy = remote(ref, ref, send, recv, self.p.across("c"))
         copy.wait_recv()
         copy.wait_send()
 
+
+class Gather(Part):
+    def __init__(self, place, piece, lo, cols, send, recv):
+        super().__init__(place, piece, lo, cols)
+        self.send, self.recv = send, recv
+
     def step(self, k):
+        n = len(STEPS)
         if k > 0:
-            self.settle(k - 1)
-        if k < 4:
-            for ref, to in self.copies(k):
-                remote(ref, ref, self.send.at[0], self.recv.at[k], to).start()
-
-
-def add_into(ref, *others):
-    total = ref[...].astype(F32)
-    for other in others:
-        total = total + other[...].astype(F32)
-    ref[...] = total.astype(BF)
+            done = "vwyx" if k - 1 == n else STEPS[k - 1][0][1]
+            self.settle(self.piece(self.p.index(done), self.all), self.send.at[0], self.recv.at[k - 1])
+        if k < n:
+            for (axis, done), span in zip(STEPS[k], self.spans(k)):
+                ref = self.piece(self.p.index(done), span)
+                remote(ref, ref, self.send.at[0], self.recv.at[k], self.p.across(axis)).start()
+        elif k == n:
+            ref = self.piece(self.p.index("vwyx"), self.all)
+            remote(ref, ref, self.send.at[0], self.recv.at[k], self.p.across("c")).start()
+
+
+def add_into(ref, other):
+    ref[...] = (ref[...].astype(F32) + other[...].astype(F32)).astype(BF)
 
 
 class Scatter(Part):
-    def __init__(self, place, piece, lo, cols, late, order, last, slots, buffers, send, recv, credit, finish):
+    def __init__(self, place, piece, lo, cols, order, last, slots, buffers, send, recv, credit, finish):
         super().__init__(place, piece, lo, cols)
-        self.late, self.order, self.last, self.send, self.recv, self.credit, self.finish = late, order, last, send, recv, credit, finish
-        self.rd = slots.at[order % SLOTS, :, :, :, :, pl.ds(0, cols)]
-        self.ry, self.rx, self.third, self.fourth = buffers[0], buffers[1], buffers[2:4], buffers[4:]
-
-    def make(self, k):
-        p, g, every = self.p, self.piece, slice(None)
+        self.order, self.last, self.send, self.recv, self.credit, self.finish = order, last, send, recv, credit, finish
+        self.slot = slots.at[order % SLOTS, :, :, :, :, :, pl.ds(0, cols)]
+        self.buffers = buffers
+
+    def step(self, k):
+        p, g, n = self.p, self.piece, len(STEPS)
+        if k == 1:
+            self.settle(self.slot, self.send.at[0], self.recv.at[0])
+
+            @pl.loop(0, 2)
+            def _(v):
+                at = p.index("vwyx")
+                add_into(g((at[0], v, *at[2:]), self.all), self.slot.at[v])
+
+            if self.order + SLOTS < self.last:
+                pl.semaphore_signal(self.credit, inc=1, device_id=p.across("c"), device_id_type=MESH)
+        elif k > 1:
+            j = n + 1 - k
+            self.settle(g(p.index(STEPS[j][0][1]), self.all), self.send.at[0], self.recv.at[k - 1])
+            if k <= n:
+                for (_, done), span, buffer in zip(STEPS[j], self.spans(j), self.buffers[j]):
+                    add_into(g(p.index(done), span), buffer)
+            else:
+                self.finish(self.lo, g(p.index(), self.all)[...].astype(F32) + self.buffers[0][0][...].astype(F32))
         if k == 0:
-            found = [(g(1 - p.c, every, every, every, self.all), self.rd, p.at(c=1 - p.c))]
-        elif k == 1:
-            found = [(g(p.c, every, p.ny, every, self.h1), self.ry, p.at(y=p.ny)),
-                     (g(p.c, every, every, p.nx, self.h2), self.rx, p.at(x=p.nx))]
-        elif self.late and k == 2:
-            found = []
-            for d, z in enumerate(p.zs()):
-                found += [(g(p.c, z, p.y, every, self.h1), self.third[0].at[d], p.at(z=z)),
-                          (g(p.c, z, every, p.x, self.h2), self.third[1].at[d], p.at(z=z))]
-        elif self.late:
-            found = [(g(p.c, p.z, p.y, p.nx, self.h1), self.fourth[0], p.at(x=p.nx)),
-                     (g(p.c, p.z, p.ny, p.x, self.h2), self.fourth[1], p.at(y=p.ny))]
-        elif k == 2:
-            found = [(g(p.c, every, p.y, p.nx, self.h1), self.third[0], p.at(x=p.nx)),
-                     (g(p.c, every, p.ny, p.x, self.h2), self.third[1], p.at(y=p.ny))]
-        else:
-            found = [(g(p.c, z, p.y, p.x, self.all), self.fourth[0].at[d], p.at(z=z)) for d, z in enumerate(p.zs())]
-        return [remote(src, dst, self.send.at[0], self.recv.at[k], to) for src, dst, to in found]
-
-    def settle(self, k):
-        p, g, every = self.p, self.piece, slice(None)
-        if k == 0:
-            ref = self.rd
-        elif k == 1:
-            ref = g(p.c, every, p.y, every, self.all)
-        elif k == 2:
-            ref = g(p.c, pl.ds(0, p.nz - 1), p.y, every, self.all) if self.late else g(p.c, every, p.y, p.x, self.all)
-        else:
-            ref = g(p.c, p.z, p.y, p.x, self.all) if self.late else self.fourth[0]
-        copy = remote(ref, ref, self.send.at[0], self.recv.at[k], p.at(c=1 - p.c))
-        copy.wait_recv()
-        copy.wait_send()
-
-    def step(self, k):
-        p, g, every = self.p, self.piece, slice(None)
-        if k > 0:
-            self.settle(k - 1)
-        if k == 0 and self.order >= SLOTS:
-            pl.semaphore_wait(self.credit, 1)
-        if k == 1:
-            @pl.loop(0, p.nz)
-            def _(z):
-                add_into(g(p.c, z, every, every, self.all), self.rd.at[z])
-            if self.order + SLOTS < self.last:
-                pl.semaphore_signal(self.credit, inc=1, device_id=p.at(c=1 - p.c), device_id_type=MESH)
-        elif k == 2:
-            @pl.loop(0, p.nz)
-            def _(z):
-                add_into(g(p.c, z, p.y, every, self.h1), self.ry.at[z])
-                add_into(g(p.c, z, every, p.x, self.h2), self.rx.at[z])
-        elif k == 3 and self.late:
-            add_into(g(p.c, p.z, p.y, every, self.h1), *[self.third[0].at[d] for d in range(p.nz - 1)])
-            add_into(g(p.c, p.z, every, p.x, self.h2), *[self.third[1].at[d] for d in range(p.nz - 1)])
-        elif k == 3:
-            add_into(g(p.c, every, p.y, p.x, self.h1), self.third[0])
-            add_into(g(p.c, every, p.y, p.x, self.h2), self.third[1])
-        elif k == 4 and self.late:
-            self.finish(self.lo, g(p.c, p.z, p.y, p.x, self.h1)[...].astype(F32) + self.fourth[0][...].astype(F32))
-            self.finish(self.lo + self.cut, g(p.c, p.z, p.y, p.x, self.h2)[...].astype(F32) + self.fourth[1][...].astype(F32))
-        elif k == 4:
-            total = g(p.c, p.z, p.y, p.x, self.all)[...].astype(F32)
-            for d in range(p.nz - 1):
-                total = total + self.fourth[0][d].astype(F32)
-            self.finish(self.lo, total)
-        if k < 4:
-            for copy in self.make(k):
-                copy.start()
-
-
-def scatter_buffers(rows, cols, late):
-    nz = GRID[1]
-    h1 = cols // 256 * 128
-    h2 = cols - h1
-    shapes = [(nz, 2, rows, h1), (nz, 2, rows, h2)]
-    shapes += [(nz - 1, 2, rows, h1), (nz - 1, 2, rows, h2), (rows, h1), (rows, h2)] if late else [(nz, rows, h1), (nz, rows, h2), (nz - 1, rows, cols)]
-    return [pltpu.VMEM(shape, BF) for shape in shapes]
-
-
-GATHERS = (
-    (0, 0, 256, 0),
-    (0, 256, 384, 0),
-    (1, 0, 256, 0),
-    (1, 256, 256, 0),
-    (1, 512, 256, 0),
-    (2, 0, 768, 0),
-    (3, 0, 768, 0),
-    (4, 0, 768, 0),
-    (5, 0, 768, 1),
-    (6, 0, 768, 0),
-    (7, 0, 768, 0),
-    (8, 0, 768, 1),
-    (9, 0, 768, 0),
-    (10, 0, 768, 0),
-    (11, 0, 768, 1),
-    (12, 0, 768, 1),
-)
-SCATTERS = (
-    (5, 0, 768, 0),
-    (6, 0, 768, 1),
-    (7, 0, 768, 0),
-    (8, 0, 768, 0),
-    (9, 0, 768, 1),
-    (10, 0, 768, 1),
-    (11, 0, 768, 0),
-    (12, 0, 768, 0),
-    (4, 0, 768, 0),
-    (1, 0, 768, 0),
-    (2, 0, 768, 0),
-    (0, 0, 256, 0),
-    (0, 256, 384, 1),
-    (3, 512, 256, 0),
-    (3, 256, 256, 0),
-    (3, 0, 256, 0),
-)
-TICKS = {
-    "pre": ((0, 0, 0), (0, 1, 0), (0, 2, 0), (0, 3, 0), (0, 4, 0), (0, 5, 0), (0, 6, 0),),
-    "before P0": ((0, 0, 1), (0, 1, 1), (0, 2, 1), (0, 7, 0), (0, 0, 2), (0, 1, 2), (0, 3, 1), (0, 2, 2), (0, 4, 1), (0, 0, 3), (0, 0, 4), (0, 1, 3), (0, 3, 2), (0, 2, 3), (0, 1, 4), (0, 4, 2), (0, 5, 1), (0, 8, 0), (0, 2, 4), (0, 3, 3), (0, 4, 3), (0, 6, 1), (0, 9, 0), (0, 3, 4), (0, 4, 4),),
-    "P0": ((0, 5, 2), (0, 6, 2), (0, 7, 1), (0, 8, 1), (0, 10, 0), (0, 11, 0),),
-    "F0": ((0, 5, 3), (0, 9, 1), (0, 12, 0),),
-    "F1": ((0, 6, 3), (0, 7, 2), (0, 8, 2), (0, 11, 1), (0, 13, 0),),
-    "before P1": ((0, 5, 4),),
-    "P1": ((0, 9, 2), (0, 10, 1), (0, 14, 0),),
-    "F2": ((0, 7, 3), (0, 12, 1), (0, 8, 3), (0, 15, 0),),
-    "F3": ((0, 9, 3), (0, 11, 2),),
-    "before P2": ((0, 6, 4),),
-    "P2": ((0, 10, 2), (0, 12, 2), (0, 13, 1), (0, 14, 1), (0, 15, 1),),
-    "F4": ((0, 11, 3),),
-    "F5": ((0, 10, 3), (0, 14, 2),),
-    "before wo": ((0, 7, 4),),
-    "wo": ((0, 12, 3),),
-    "before U0": ((0, 8, 4),),
-    "U0": ((0, 13, 2),),
-    "before U1": ((0, 9, 4),),
-    "U1": ((0, 14, 3), (0, 15, 2),),
-    "before U2": ((0, 10, 4),),
-    "before U3": ((0, 11, 4),),
-    "U3": ((0, 13, 3),),
-    "before down": ((0, 12, 4), (0, 14, 4), (0, 15, 3), (0, 13, 4), (0, 15, 4),),
-    "b0": ((1, 0, 0),),
-    "b1": ((1, 0, 1), (1, 1, 0),),
-    "b2": ((1, 1, 1), (1, 0, 2), (1, 2, 0),),
-    "b3": ((1, 1, 2), (1, 2, 1), (1, 3, 0), (1, 4, 0), (1, 5, 0),),
-    "ln1b": ((1, 0, 3),),
-    "wob": ((1, 3, 1), (1, 6, 0),),
-    "B0": ((1, 2, 2), (1, 1, 3), (1, 3, 2), (1, 4, 1), (1, 5, 1), (1, 6, 1), (1, 7, 0), (1, 8, 0),),
-    "B1": ((1, 0, 4), (1, 1, 4), (1, 2, 3), (1, 3, 3), (1, 7, 1), (1, 8, 1), (1, 4, 2),),
-    "gw0": ((1, 2, 4), (1, 5, 2), (1, 9, 0),),
-    "B2": ((1, 3, 4), (1, 6, 2), (1, 9, 1),),
-    "B3": ((1, 7, 2), (1, 4, 3), (1, 8, 2),),
-    "gw1": ((1, 6, 3), (1, 10, 0),),
-    "B4": ((1, 4, 4), (1, 5, 3), (1, 7, 3), (1, 8, 3), (1, 9, 2), (1, 6, 4), (1, 5, 4), (1, 10, 1),),
-    "B5": ((1, 7, 4), (1, 9, 3),),
-    "rel2": ((1, 10, 2), (1, 11, 0), (1, 12, 0),),
-    "gv2": ((1, 8, 4), (1, 13, 0),),
-    "gk2": ((1, 11, 1), (1, 12, 1), (1, 10, 3), (1, 13, 1), (1, 14, 0),),
-    "gq2": ((1, 9, 4), (1, 11, 2), (1, 14, 1), (1, 15, 0),),
-    "end": ((1, 12, 2), (1, 15, 1), (1, 13, 2), (1, 10, 4), (1, 11, 3), (1, 14, 2), (1, 15, 2), (1, 13, 3), (1, 12, 3), (1, 14, 3), (1, 11, 4), (1, 15, 3), (1, 12, 4), (1, 13, 4), (1, 14, 4), (1, 15, 4),),
-}
+            if self.order >= SLOTS:
+                pl.semaphore_wait(self.credit, 1)
+            ref = g(p.index("vwyx", "c"), self.all)
+            remote(ref, self.slot, self.send.at[0], self.recv.at[0], p.across("c")).start()
+        elif k <= n:
+            j = n - k
+            for (axis, done), span, buffer in zip(STEPS[j], self.spans(j), self.buffers[j]):
+                ref = g(p.index(done, axis), span)
+                remote(ref, buffer, self.send.at[0], self.recv.at[k], p.across(axis)).start()
+
+
+def scatter_buffers(rows, cols):
+    cut = cols // 256 * 128
+    found = []
+    for step in STEPS:
+        widths = (cols,) if len(step) == 1 else (cut, cols - cut)
+        found.append([pltpu.VMEM((*(2,) * len(done), rows, width), BF) for (_, done), width in zip(step, widths)])
+    return found
 
 
 def layer_kernel(
@@ -425,18 +362,18 @@
     scale = (3.0 * HEAD) ** -0.5
     length = length_ref[0]
     row = lambda k: rows_ref[k:k + 1, :]
-    whole = (slice(None),) * 4
+    whole = (slice(None),) * len(GRID)
     per = D // BLOCKS
 
     def part(ref, *lead, trail=()):
-        return lambda c, z, y, x, cols: ref.at[(*lead, c, z, y, x, *trail, slice(None), cols)]
+        return lambda blocks, cols: ref.at[(*lead, *blocks, *trail, slice(None), cols)]
 
     pieces = [part(GR)] + [part(GA, n) for n in range(D // C)] + [part(GO)]
     pieces += [part(GU, k) for k in range(CH)] + [part(GD, trail=(k,)) for k in range(CH)]
     if comm:
-        slots, buffers, (ag_send, ag_recv, rs_send, rs_recv, credit) = rest[0], list(rest[1:-5]), rest[-5:]
+        slots, buffers, (ag_send, ag_recv, rs_send, rs_recv, credit) = rest[0], rest[1:-5], rest[-5:]
         place = Place()
-        gathers = [Gather(place, pieces[i], lo, cols, early, ag_send.at[j], ag_recv.at[j]) for j, (i, lo, cols, early) in enumerate(GATHERS)]
+        gathers = [Gather(place, pieces[i], lo, cols, ag_send.at[j], ag_recv.at[j]) for j, (i, lo, cols) in enumerate(GATHERS)]
         nA, nO, nU, nD = 1, 1 + D // C, 2 + D // C, 2 + D // C + CH
 
         def finisher(i):
@@ -457,11 +394,8 @@
             return store
 
         scatters = []
-        for j, (i, lo, cols, late) in enumerate(SCATTERS):
-            number = 6 if late else 5
-            scatters.append(Scatter(place, pieces[i], lo, cols, late, j, len(SCATTERS), slots, buffers[:number],
-                                    rs_send.at[j], rs_recv.at[j], credit, finisher(i)))
-            buffers = buffers[number:]
+        for j, (i, lo, cols) in enumerate(SCATTERS):
+            scatters.append(Scatter(place, pieces[i], lo, cols, j, len(SCATTERS), slots, buffers[j], rs_send.at[j], rs_recv.at[j], credit, finisher(i)))
 
     def run(name):
         if comm:
@@ -478,7 +412,7 @@
                         run(label)
 
     if comm:
-        me = (place.c, place.z, place.y, place.x)
+        me = place.index()
         rows_ref[...] = jnp.zeros_like(rows_ref)
         for k, ref in enumerate(vec_in[:-1]):
             rows_ref[k:k + 1, 0:per] = ref[...].astype(F32).reshape(1, per)
@@ -525,7 +459,7 @@
     mask_ref[...] = jnp.where(iota((8, T), 1) < length, 0.0, -1e30)
     small_ref[...] = jnp.zeros_like(small_ref)
     grel_ref[...] = jnp.zeros_like(grel_ref)
-    run("before P0")
+    run("before Q0")
     cols_ref[...] = matrix(GR[(*whole, slice(None), pl.ds(NB, 128))].astype(F32))
     rows_ref[...] = cols_ref[...].T[0:16]
 
@@ -536,21 +470,22 @@
 
     @pl.loop(0, D // C)
     def _(n):
-        due("before P", n, range(1, D // C))
+        due("before Q", n, range(1, D // C))
         cols = tile(n, C)
         weight = lambda i: matrix(GA[(n, *whole, slice(None), pl.ds(i * C, C))])
-        relT = matrix(GR[(*whole, slice(None), pl.ds(0, NB))])
-        wq, wk, wv = weight(0), weight(1), weight(2)
-        q_ref[:, cols] = (nn(x_ref[...], wq) + rows_ref[0:1, cols]).astype(BF)
-        k = (nn(x_ref[...], wk) + rows_ref[1:2, cols]).astype(BF)
-        v = (nn(x_ref[...], wv) + rows_ref[2:3, cols]).astype(BF)
+        q_ref[:, cols] = (nn(x_ref[...], weight(0)) + rows_ref[0:1, cols]).astype(BF)
+        k = (nn(x_ref[...], weight(1)) + rows_ref[1:2, cols]).astype(BF)
+        v = (nn(x_ref[...], weight(2)) + rows_ref[2:3, cols]).astype(BF)
         k_ref[:, cols] = k
         v_ref[:, cols] = v
         for src, dst in ((k, kf_ref), (v, vf_ref)):
             dst[0:B, cols] = nn(flip_ref[...], src[B:T]).astype(BF)
             dst[B:T, cols] = nn(flip_ref[...], src[0:B]).astype(BF)
-        rk = (tn(wk, relT) + cols_ref[cols, 1:2]).astype(BF)
-        rq = (tn(wq, relT) + cols_ref[cols, 0:1]).astype(BF)
+        due("Q", n, range(D // C))
+        due("before P", n, (0,))
+        relT = matrix(GR[(*whole, slice(None), pl.ds(0, NB))])
+        rk = (tn(weight(1), relT) + cols_ref[cols, 1:2]).astype(BF)
+        rq = (tn(weight(0), relT) + cols_ref[cols, 0:1]).astype(BF)
         kprT_ref[cols, :] = nn(rk, act_ref[:, 0:2 * T]).astype(BF)
         kpsT_ref[cols, :] = nn(rk, pick_ref[...]).astype(BF)
         qpsT_ref[cols, :] = nn(rq, pick_ref[...]).astype(BF)
@@ -624,31 +559,32 @@
         small_ref[8:9, :] += column_sum(start)
 
     run("ln2")
-    half = GRID[1] // 2
 
     @pl.loop(0, CH)
     def _(k):
         units = tile(k, D)
-        c, z0 = lax.div(k, 2), half * lax.rem(k, 2)
-        w = matrix(GD[c, pl.ds(z0, half)])
+        w = matrix(GD[lax.div(k, 2), lax.rem(k, 2)])
         gu = (nt(gd_ref[...], w) * gp_ref[:, units].astype(F32)).astype(BF)
         gp_ref[:, units] = gu
         gbup_ref[0:1, units] = column_sum(gu.astype(F32))
-
-        @pl.loop(0, half)
+        second_ref[...] += nt(gu, matrix(GU[k]))
+
+        @pl.loop(0, 2)
+        def _(i):
+            g = tn(nb_ref[:, tile(i, D // 2)], gp_ref[:, units])
+            GU[k, i] = g.reshape(*GU.shape[2:]).astype(BF)
+
+        due("b", k, range(CH))
+
+    @pl.loop(0, CH)
+    def _(k):
+        @pl.loop(0, 2)
         def _(i):
             at = pl.ds(pl.multiple_of(k * D + i * (D // 2), D // 2), D // 2)
             g = tn(act_ref[:, at], gd_ref[...])
-            GD[c, z0 + i] = g.reshape(*GD.shape[2:]).astype(BF)
-
-        second_ref[...] += nt(gu, matrix(GU[k]))
-
-        @pl.loop(0, GRID[0])
-        def _(i):
-            g = tn(nb_ref[:, tile(i, D // 2)], gp_ref[:, units])
-            GU[k, i] = g.reshape(*GU.shape[2:]).astype(BF)
-
-        due("b", k, range(CH))
+            GD[lax.div(k, 2), lax.rem(k, 2), i] = g.reshape(*GD.shape[3:]).astype(BF)
+
+        due("d", k, range(CH))
 
     @pl.loop(0, T // R)
     def _(r):
@@ -710,8 +646,8 @@
                 g = jnp.where(own_column, gbup_ref[0:1, tile(t, CH * W)], 0.0).astype(BF)
                 cols_ref[tile(t, W), :] += nt(select_ref[...], g)
 
-            GR[(*whole, slice(None), pl.ds(0, NB))] = grel_ref[...].reshape(*GR.shape[:5], NB).astype(BF)
-            GR[(*whole, slice(None), pl.ds(NB, 128))] = cols_ref[...].reshape(*GR.shape[:5], 128).astype(BF)
+            GR[(*whole, slice(None), pl.ds(0, NB))] = grel_ref[...].reshape(*GR.shape[:6], NB).astype(BF)
+            GR[(*whole, slice(None), pl.ds(NB, 128))] = cols_ref[...].reshape(*GR.shape[:6], 128).astype(BF)
 
         due("rel", n, final)
         for i, name, d, gr in ((2, "gv", dv, None), (1, "gk", dk, grk), (0, "gq", dq, grq)):
@@ -720,7 +656,7 @@
                 g = tn(x_ref[:, half * (D // 2):(half + 1) * (D // 2)], d)
                 if gr is not None:
                     g = g + nt(kprT_ref[half * (D // 2):(half + 1) * (D // 2), 0:NB], gr)
-                GA[(n, half, *whole[1:], slice(None), pl.ds(i * C, C))] = g.reshape(*GA.shape[2:6], C).astype(BF)
+                GA[(n, half, *whole[1:], slice(None), pl.ds(i * C, C))] = g.reshape(*GA.shape[2:7], C).astype(BF)
             due(name, n, final)
         due("gw", n, range(D // C))
 
@@ -775,11 +711,9 @@
         outs = [S((T, D), BF), S((T, D), F32), S((rows, NB + 128), F32)] + [S((rows, D), F32)] * 4 + [S(wup.shape, F32), S((FF // D * rows, D), F32)]
         out_specs = [VM] * len(outs)
         in_specs = [SM] + [VM] * (3 + len(operands))
-        sems = [pltpu.SemaphoreType.DMA((len(parts), k)) for parts in (GATHERS, SCATTERS) for k in (1, 4)] + [pltpu.SemaphoreType.REGULAR]
+        sems = [pltpu.SemaphoreType.DMA((len(parts), k)) for parts in (GATHERS, SCATTERS) for k in (1, 5)] + [pltpu.SemaphoreType.REGULAR]
         extra = [pltpu.VMEM((SLOTS, *GRID[1:], rows, D), BF)]
-        for _, _, cols, late in SCATTERS:
-            extra += scatter_buffers(rows, cols, late)
-        extra += sems
+        extra += [scatter_buffers(rows, cols) for _, _, cols in SCATTERS] + sems
 
         def kernel(*refs):
             given = 4 + len(vectors)
@@ -843,14 +777,14 @@
     wide = gather(b_up).reshape(BLOCKS, ch, r).transpose(0, 2, 1).reshape(D, ch)
     gr = jnp.concatenate([attend[:, 4 * D:4 * D + NB + 9], wide, pad[0] * jnp.ones((D, 1), BF)], axis=1)[:, :NB + 128].reshape(*GRID, r, NB + 128)
     go = attend[:, :D].reshape(*GRID, r, D)
-    ga = attend[:, D:4 * D].reshape(*GRID, r, 3, n, 256).transpose(6, 0, 1, 2, 3, 4, 5, 7).reshape(n, *GRID, r, D)
-    gu = gather(w_up).reshape(*GRID, r, ch, D).transpose(5, 0, 1, 2, 3, 4, 6)
+    ga = attend[:, D:4 * D].reshape(*GRID, r, 3, n, 256).transpose(7, 0, 1, 2, 3, 4, 5, 6, 8).reshape(n, *GRID, r, D)
+    gu = gather(w_up).reshape(*GRID, r, ch, D).transpose(6, 0, 1, 2, 3, 4, 5, 7)
     gd = gather(w_down).reshape(*GRID, ch, r, D)
     out, gtok, gr, ga, go, gu, gd = call_layer(False, lengths, rel_index, tokens, cotangent, (gr, ga, go, gu, gd))
     gr = gr.reshape(D, NB + 128)
-    ga = ga.reshape(n, *GRID, r, 3, 256).transpose(1, 2, 3, 4, 5, 6, 0, 7).reshape(D, 3 * D)
+    ga = ga.reshape(n, *GRID, r, 3, 256).transpose(1, 2, 3, 4, 5, 6, 7, 0, 8).reshape(D, 3 * D)
     wide = scatter(gr[:, NB + 9:NB + 9 + ch].reshape(BLOCKS, r, ch).transpose(0, 2, 1).reshape(FF))
-    gup = scatter(gu.transpose(1, 2, 3, 4, 5, 0, 6).reshape(D, FF))
+    gup = scatter(gu.transpose(1, 2, 3, 4, 5, 6, 0, 7).reshape(D, FF))
     gdown = scatter(gd.reshape(FF, D))
     attend = scatter(jnp.concatenate([go.reshape(D, D), ga, gr], axis=1))
     go, gq, gk, gv = (attend[:, i * D:(i + 1) * D] for i in range(4))
@@ -861,7 +795,7 @@
 
 def solution(mesh):
     rows, vec = P(AXES, None), P(AXES)
-    comm = mesh.shape["dp"] == GRID[0] and mesh.shape["fsdp"] == GRID[1] * GRID[2] * GRID[3]
+    comm = mesh.shape["dp"] == GRID[0] and mesh.shape["fsdp"] == BLOCKS // GRID[0]
 
     def step(*args):
         return body(comm, *args)

time: 179 us -> 171 us (0.955)
  Pallas kernels: 178 us -> 169 us
    pallas_call x1, Pallas kernels: 174 us -> 165 us  [call_layer(): pl.pallas_call(kernel, out_shape=outs, in_specs=in_specs, out_specs=out_s...]
where the time goes in v4:
time: 171 us
  Pallas kernels  169 us (99%)
    pallas_call x1, Pallas kernels, call_layer(): pl.pallas_call(kernel, out_shape=outs, in_specs=in_specs, out_specs=out_s...  165 us
    pallas_call x1, Pallas kernels, body(): pl.pallas_call(finish_kernel, out_shape=[S(a.shape, a.dtype) for a in mov...  3.7 us

profile of v4, /device:TPU:0, one launch (start us, length us, event | category | flops | bytes accessed | tf_op | source)
XLA Modules:
  0.0 170.6 jit_solution(7690484342729955077)
XLA Ops:
  1.3 165.4 %shard_map.348 = (bf16[512,768]{1,0:T(8,128)(2,1)}, f32[512,768]{1,0:T(8,128)}, f32[24,640]{1,0:T(8,128)}, f32[24,768]{1,0:T(8,128)}, f32[24,768]{1,0:T(8,128)},...) custom-call(s32[1]{0:T(128)S(6)} %copy.40.refs_0_, s32[1024]{0:T(1024)} %refs_1_.1, ...), custom_call_target="tpu_custom_call" | custom-call | tf_op jit(solution)/shard_map/pallas_call | solution.py:733
  166.7 3.7 %shard_map.349 = (bf16[512,768]{1,0:T(8,128)(2,1)}, f32[512,768]{1,0:T(8,128)}, f32[24,768]{1,0:T(8,128)}, f32[24,768]{1,0:T(8,128)}, f32[24,768]{1,0:T(8,128)},...) custom-call(f32[24,640]{1,0:T(8,128)} %get-tuple-element.47.r_ref, ...), custom_call_target="tpu_custom_call" | custom-call | tf_op jit(solution)/shard_map/pallas_call | solution.py:763

commit v5 on v4

--- a/solution.py
+++ b/solution.py
@@ -205,31 +205,29 @@
     (3, 0, 256),
 )
 TICKS = {
-    "pre": ((0, 0, 0), (0, 1, 0), (0, 2, 0), (0, 3, 0), (0, 4, 0), (0, 5, 0), (0, 6, 0),),
-    "before Q0": ((0, 0, 1), (0, 1, 1), (0, 2, 1), (0, 7, 0), (0, 3, 1), (0, 4, 1), (0, 0, 2), (0, 1, 2), (0, 2, 2), (0, 5, 1), (0, 8, 0), (0, 3, 2), (0, 4, 2), (0, 6, 1), (0, 9, 0), (0, 0, 3), (0, 7, 1), (0, 5, 2), (0, 1, 3), (0, 10, 0), (0, 2, 3), (0, 6, 2), (0, 8, 1), (0, 11, 0), (0, 0, 4), (0, 3, 3), (0, 7, 2), (0, 1, 4), (0, 4, 3), (0, 9, 1), (0, 12, 0), (0, 2, 4), (0, 0, 5), (0, 8, 2), (0, 1, 5), (0, 3, 4), (0, 2, 5), (0, 5, 3), (0, 4, 4), (0, 10, 1), (0, 13, 0), (0, 9, 2), (0, 3, 5),),
+    "pre": ((0, 0, 0), (0, 1, 0), (0, 2, 0), (0, 3, 0), (0, 4, 0), (0, 5, 0),),
+    "before Q0": ((0, 0, 1), (0, 1, 1), (0, 2, 1), (0, 6, 0), (0, 3, 1), (0, 4, 1), (0, 7, 0), (0, 0, 2), (0, 1, 2), (0, 2, 2), (0, 3, 2), (0, 4, 2), (0, 5, 1), (0, 8, 0), (0, 0, 3), (0, 6, 1), (0, 9, 0), (0, 5, 2), (0, 1, 3), (0, 7, 1), (0, 10, 0), (0, 2, 3), (0, 0, 4), (0, 6, 2), (0, 3, 3), (0, 0, 5), (0, 1, 4), (0, 4, 3), (0, 7, 2), (0, 1, 5), (0, 8, 1), (0, 11, 0), (0, 2, 4), (0, 9, 1), (0, 12, 0), (0, 3, 4), (0, 2, 5), (0, 3, 5),),
+    "Q0": ((0, 4, 4), (0, 5, 3), (0, 8, 2), (0, 9, 2), (0, 10, 1), (0, 13, 0),),
     "before P0": ((0, 4, 5),),
-    "P0": ((0, 6, 3),),
-    "F0": ((0, 5, 4), (0, 7, 3), (0, 10, 2), (0, 11, 1), (0, 14, 0),),
+    "F0": ((0, 5, 4), (0, 6, 3), (0, 7, 3), (0, 10, 2), (0, 11, 1), (0, 14, 0),),
     "F1": ((0, 6, 4), (0, 8, 3), (0, 12, 1), (0, 15, 0),),
     "before Q1": ((0, 5, 5),),
-    "Q1": ((0, 13, 1), (0, 7, 4),),
-    "P1": ((0, 11, 2),),
-    "F2": ((0, 8, 4), (0, 9, 3), (0, 12, 2), (0, 10, 3),),
-    "F3": ((0, 13, 2), (0, 14, 1), (0, 15, 1),),
+    "P1": ((0, 7, 4), (0, 9, 3), (0, 13, 1), (0, 11, 2),),
+    "F2": ((0, 8, 4), (0, 10, 3), (0, 12, 2), (0, 14, 1), (0, 15, 1),),
+    "F3": ((0, 9, 4), (0, 11, 3), (0, 13, 2),),
     "before Q2": ((0, 6, 5),),
-    "Q2": ((0, 11, 3),),
-    "P2": ((0, 9, 4),),
-    "F4": ((0, 10, 4), (0, 12, 3), (0, 14, 2), (0, 15, 2),),
-    "F5": ((0, 11, 4), (0, 13, 3),),
+    "P2": ((0, 10, 4), (0, 12, 3), (0, 14, 2),),
+    "F4": ((0, 11, 4), (0, 13, 3), (0, 15, 2),),
+    "F5": ((0, 12, 4), (0, 14, 3), (0, 15, 3),),
     "before wo": ((0, 7, 5),),
+    "ln1": ((0, 13, 4),),
     "before U0": ((0, 8, 5),),
-    "U0": ((0, 12, 4), (0, 14, 3),),
     "before U1": ((0, 9, 5),),
-    "U1": ((0, 15, 3),),
+    "U1": ((0, 14, 4),),
     "before U2": ((0, 10, 5),),
-    "U2": ((0, 13, 4),),
+    "U2": ((0, 15, 4),),
     "before U3": ((0, 11, 5),),
-    "before down": ((0, 12, 5), (0, 14, 4), (0, 13, 5), (0, 15, 4), (0, 14, 5), (0, 15, 5),),
+    "before down": ((0, 12, 5), (0, 13, 5), (0, 14, 5), (0, 15, 5),),
     "b0": ((1, 0, 0),),
     "b1": ((1, 1, 0),),
     "b2": ((1, 0, 1), (1, 2, 0),),

time: 171 us -> 169 us (0.988)
  Pallas kernels: 169 us -> 167 us
    pallas_call x1, Pallas kernels: 165 us -> 164 us  [call_layer(): pl.pallas_call(kernel, out_shape=outs, in_specs=in_specs, out_specs=out_s...]
where the time goes in v5:
time: 169 us
  Pallas kernels  167 us (99%)
    pallas_call x1, Pallas kernels, call_layer(): pl.pallas_call(kernel, out_shape=outs, in_specs=in_specs, out_specs=out_s...  164 us
    pallas_call x1, Pallas kernels, body(): pl.pallas_call(finish_kernel, out_shape=[S(a.shape, a.dtype) for a in mov...  3.7 us

profile of v5, /device:TPU:0, one launch (start us, length us, event | category | flops | bytes accessed | tf_op | source)
XLA Modules:
  0.0 168.8 jit_solution(14353392764738060)
XLA Ops:
  1.3 163.6 %shard_map.348 = (bf16[512,768]{1,0:T(8,128)(2,1)}, f32[512,768]{1,0:T(8,128)}, f32[24,640]{1,0:T(8,128)}, f32[24,768]{1,0:T(8,128)}, f32[24,768]{1,0:T(8,128)},...) custom-call(s32[1]{0:T(128)S(6)} %copy.40.refs_0_, s32[1024]{0:T(1024)} %refs_1_.1, ...), custom_call_target="tpu_custom_call" | custom-call | tf_op jit(solution)/shard_map/pallas_call | solution.py:731
  164.9 3.7 %shard_map.349 = (bf16[512,768]{1,0:T(8,128)(2,1)}, f32[512,768]{1,0:T(8,128)}, f32[24,768]{1,0:T(8,128)}, f32[24,768]{1,0:T(8,128)}, f32[24,768]{1,0:T(8,128)},...) custom-call(f32[24,640]{1,0:T(8,128)} %get-tuple-element.47.r_ref, ...), custom_call_target="tpu_custom_call" | custom-call | tf_op jit(solution)/shard_map/pallas_call | solution.py:761

commit v6 on v5

--- a/solution.py
+++ b/solution.py
@@ -157,11 +157,13 @@
     def index(self, whole="", other=""):
         return tuple(slice(None) if a in whole else 1 - i if a in other else i for a, i in self.here.items())
 
-    def barrier(self):
+    def greet(self):
         sem = pltpu.get_barrier_semaphore()
         for axis in self.here:
             pl.semaphore_signal(sem, inc=1, device_id=self.across(axis), device_id_type=MESH)
-        pl.semaphore_wait(sem, len(self.here))
+
+    def meet(self):
+        pl.semaphore_wait(pltpu.get_barrier_semaphore(), len(self.here))
 
 
 def remote(src, dst, send, recv, to):
@@ -410,6 +412,7 @@
                         run(label)
 
     if comm:
+        place.greet()
         me = place.index()
         rows_ref[...] = jnp.zeros_like(rows_ref)
         for k, ref in enumerate(vec_in[:-1]):
@@ -428,7 +431,7 @@
         for k in range(CH):
             GU[(k, *me)] = up_in[:, pl.ds(k * D, D)]
             GD[(*me, k)] = down_in[k]
-        place.barrier()
+        place.meet()
         run("pre")
     else:
         GRh, GAh, GOh, GUh, GDh = rest[:5]

time: 169 us -> 169 us (level)
  no operation moved by 1% of the time
where the time goes in v6:
time: 169 us
  Pallas kernels  167 us (99%)
    pallas_call x1, Pallas kernels, call_layer(): pl.pallas_call(kernel, out_shape=outs, in_specs=in_specs, out_specs=out_s...  163 us
    pallas_call x1, Pallas kernels, body(): pl.pallas_call(finish_kernel, out_shape=[S(a.shape, a.dtype) for a in mov...  3.7 us

profile of v6, /device:TPU:0, one launch (start us, length us, event | category | flops | bytes accessed | tf_op | source)
XLA Modules:
  0.0 168.6 jit_solution(17760516098267981462)
XLA Ops:
  1.3 163.4 %shard_map.348 = (bf16[512,768]{1,0:T(8,128)(2,1)}, f32[512,768]{1,0:T(8,128)}, f32[24,640]{1,0:T(8,128)}, f32[24,768]{1,0:T(8,128)}, f32[24,768]{1,0:T(8,128)},...) custom-call(s32[1]{0:T(128)S(6)} %copy.40.refs_0_, s32[1024]{0:T(1024)} %refs_1_.1, ...), custom_call_target="tpu_custom_call" | custom-call | tf_op jit(solution)/shard_map/pallas_call | solution.py:734
  164.8 3.7 %shard_map.349 = (bf16[512,768]{1,0:T(8,128)(2,1)}, f32[512,768]{1,0:T(8,128)}, f32[24,768]{1,0:T(8,128)}, f32[24,768]{1,0:T(8,128)}, f32[24,768]{1,0:T(8,128)},...) custom-call(f32[24,640]{1,0:T(8,128)} %get-tuple-element.47.r_ref, ...), custom_call_target="tpu_custom_call" | custom-call | tf_op jit(solution)/shard_map/pallas_call | solution.py:764
